TPU v7x, 256 devices: a whole 4x4x8 slice. The times are simulated.
256 devices in a mesh: span: 64 (over y, z_lo, x), depth: 4 (over z_hi, core).
Axes of the slice: x: 4, y: 4, z: 8 (z_hi: 2, z_lo: 4; z = z_hi * 4 + z_lo), core: 2. Of those that a mesh axis runs over, the one named last changes fastest.
Arguments:
- shell_temp: float32 [64, 1024, 256], P('span', 'depth'), may hold values from -6 to 6
- contact_gain: float32 [64, 1024, 256], P('span', 'depth'), may hold values from 0.2 to 2
- die_temp: float32 [48, 2048, 1024], P(None, 'span', 'depth'), may hold values from -4 to 4
- diffusivity: float32 [48, 2048, 1024], P(None, 'span', 'depth'), may hold values from 0.02 to 0.12
- routes: int32 [64, 1024, 1], P('span', 'depth'), may hold values from 0 to 63; in each aligned block of 256 rows (0 to 255, 256 to 511, ..., all dimensions but the last counted through in order) at most 8 rows name the same one
- tile_rows: int32 [64, 1024], P('span', 'depth'), may hold values from 0 to 31
- closed: int32 [64, 1024], P('span', 'depth'), may hold values 0 or 1
Outputs:
- shell_next: float32 [64, 1024, 256], P('span', 'depth')
- die_next: float32 [48, 2048, 1024], P(None, 'span', 'depth')
Inputs may be any that keep to these rules, and one draw needn't show every extreme that they name: `routes`: among the 256 block rows of one device, at most 8 name the same span index, and in some device's rows one span index is named exactly 8 times.
All inputs are finite; a program needn't handle non-finite values. No bound on the sum of `closed` on one device may be relied on, other than what follows from the above.
Results may differ from a plain program's by a relative error of at most 0.00025.
Values sent between devices are 32-bit elements; how exact they have to be, the bound alone decides.
No kernel may reach another device: no remote copies, remote signals or barrier semaphores. Data moves between devices by JAX's collectives and lax.ppermute only.
A program may use at most 128 MiB of HBM per device.

v0:
```python
import jax
import jax.numpy as jnp
from jax import lax
from jax.sharding import PartitionSpec as P

STENCIL_WEIGHT = (0.0, 1.0, 0.5, 0.25)
SHELL_RATE = 0.15
SHELL_SINK = 0.5
FACE_GAIN = 0.5


def padded_2(array, sides, width):
    for axis, dim in sides:
        size, length = (lax.axis_size(axis), array.shape[dim])
        up = [(i, (i + 1) % size) for i in range(size - 1)]
        down = [(j, i) for i, j in up]
        last = lax.slice_in_dim(array, length - width, length, axis=dim)
        initial = lax.slice_in_dim(array, 0, width, axis=dim)
        before = lax.ppermute(last, axis, up)
        after = lax.ppermute(initial, axis, down)
        array = jnp.concatenate([before, array, after], axis=dim)
    return array


def stencil_apply(padded):
    depth_count = padded.shape[0]
    rows_inner = padded.shape[1] - 2
    cols_inner = padded.shape[2] - 2
    framed = jnp.pad(padded, ((1, 1), (0, 0), (0, 0)))
    summed = -14.0 * padded[:, 1:-1, 1:-1]
    for step_z in range(3):
        for step_x in range(3):
            for step_y in range(3):
                reach_count = abs(step_z - 1) + abs(step_x - 1) + abs(step_y - 1)
                if reach_count > 0:
                    summed = (
                        summed
                        + STENCIL_WEIGHT[reach_count]
                        * framed[
                            step_z : step_z + depth_count,
                            step_x : step_x + rows_inner,
                            step_y : step_y + cols_inner,
                        ]
                    )
    return summed


def deposit(tile_codes, flux_rows, row_count):
    select = (jnp.arange(row_count, dtype=jnp.int32)[:, None] == tile_codes[None, :]).astype(
        jnp.float32
    )
    return jnp.dot(
        select, flux_rows, precision=lax.Precision.HIGHEST, preferred_element_type=jnp.float32
    )


def local(shell_temp, contact_gain, die_temp, diffusivity, routes, tile_rows, closed):
    shells = shell_temp[0]
    shell_gain = contact_gain[0]
    block_count, block_width = shells.shape
    span_count = lax.axis_size("span")
    capacity = 2 * block_count // span_count
    slot_count = span_count * capacity
    rimmed = padded_2(shells, (("depth", 0),), 1)
    framed = jnp.pad(rimmed, ((0, 0), (1, 1)))
    laplace = (
        framed[2:, 1:-1] + framed[:-2, 1:-1] + framed[1:-1, 2:] + framed[1:-1, :-2] - 4.0 * shells
    )
    target = routes[0, :, 0]
    span_ids = jnp.arange(span_count, dtype=jnp.int32)
    member = (target[:, None] == span_ids[None, :]).astype(jnp.int32)
    earlier = jnp.cumsum(member, axis=0) - member
    slot_index = jnp.sum(earlier * member, axis=1)
    position = target * capacity + slot_index
    tile_code = jnp.where(closed[0] > 0, tile_rows[0], -1)
    face_rows = die_temp[0]
    row_count = face_rows.shape[0]
    empty_slots = jnp.zeros((slot_count, block_width), jnp.float32)
    send_temp = empty_slots.at[position].set(shells)
    send_gain = empty_slots.at[position].set(shell_gain)
    send_code = (
        jnp.full((slot_count,), -1.0, jnp.float32).at[position].set(tile_code.astype(jnp.float32))
    )
    got_temp, got_gain, got_code = (
        lax.all_to_all(send_temp, "span", split_axis=0, concat_axis=0, tiled=True),
        lax.all_to_all(send_gain, "span", split_axis=0, concat_axis=0, tiled=True),
        lax.all_to_all(send_code, "span", split_axis=0, concat_axis=0, tiled=True),
    )
    got_tile = got_code.astype(jnp.int32)
    slot_live = (got_tile >= 0).astype(jnp.float32)
    face_values = face_rows[jnp.maximum(got_tile, 0)]
    flux_slots = got_gain * (got_temp - face_values) * slot_live[:, None]
    heat_in = deposit(got_tile, flux_slots, row_count)
    flux_back = lax.all_to_all(flux_slots, "span", split_axis=0, concat_axis=0, tiled=True)
    flux_mine = flux_back[position]
    shell_next = shells + SHELL_RATE * laplace - SHELL_SINK * flux_mine
    heated_face = face_rows + FACE_GAIN * heat_in
    heated = jnp.concatenate([heated_face[None], die_temp[1:]], axis=0)
    field = heated
    for sweep_index in range(2):
        padded = padded_2(field, (("span", 1), ("depth", 2)), 1)
        field = field + diffusivity * stencil_apply(padded)
    return (shell_next[None], field)


def solution(mesh):
    placed = (
        P("span", "depth", None),
        P("span", "depth", None),
        P(None, "span", "depth"),
        P(None, "span", "depth"),
        P("span", "depth", None),
        P("span", "depth"),
        P("span", "depth"),
    )
    return jax.shard_map(
        local,
        mesh=mesh,
        in_specs=placed,
        out_specs=(P("span", "depth", None), P(None, "span", "depth")),
        check_vma=False,
    )
```

profile of v0, /device:TPU:1, one launch (start us, length us, event | category | flops | bytes accessed | tf_op | source)
XLA Modules:
  0.0 189.0 jit_solution(3382772459011469190)
XLA Ops:
  0.6 0.7 fusion.84
  2.2 0.8 fusion.83
  4.4 1.4 scatter_custom_fusion.2
  6.5 12.6 %all-to-all-start.2 = ((f32[64,8,1]{1,2,0:T(1,128)}), f32[64,8,1]{1,2,0:T(1,128)S(1)}, u32[]{:S(2)}, u32[]{:S(2)}) async-start(f32[64,8,1]{1,2,0:T(1,128)} %bitcast.14), calls=%async_computation.2 | async-start | bytes 65536 | tf_op jit(solution)/shard_map/all_to_all | solution.py:87
  19.0 2.6 %scatter_custom_fusion.1 = f32[512,256]{1,0:T(8,128)} fusion(s32[256]{0:T(256)S(1)} %bitcast.79, f32[]{:T(128)} %constant.11.clone.1, f32[1,256,256]{2,1,0:T(8,128)} %param.7), kind=kCustom, calls=%fused_computation.161 | custom fusion | bytes 786436 | tf_op jit(solution)/shard_map/scatter | solution.py:79
  21.7 6.2 %all-to-all-done.2 = f32[64,8,1]{1,2,0:T(1,128)S(1)} async-done(((f32[64,8,1]{1,2,0:T(1,128)}), f32[64,8,1]{1,2,0:T(1,128)S(1)}, u32[]{:S(2)}, u32[]{:S(2)}) %all-to-all-start.2) | async-done | bytes 2080 | tf_op jit(solution)/shard_map/all_to_all | solution.py:87
  27.9 4.6 %all-to-all-start.1 = ((f32[64,8,256]{2,1,0:T(8,128)}), f32[64,8,256]{2,1,0:T(8,128)S(1)}, u32[]{:S(2)}, u32[]{:S(2)}) async-start(f32[64,8,256]{2,1,0:T(8,128)} %bitcast.11), calls=%async_computation.1 | async-start | bytes 1048576 | tf_op jit(solution)/shard_map/all_to_all | solution.py:85
  32.5 2.2 %scatter_custom_fusion = f32[512,256]{1,0:T(8,128)} fusion(s32[256]{0:T(256)S(1)} %bitcast.80, f32[1,256,256]{2,1,0:T(8,128)S(1)} %copy-done, f32[]{:T(128)} %constant.11.clone.1), kind=kCustom, calls=%fused_computation.158 | custom fusion | bytes 786436 | tf_op jit(solution)/shard_map/scatter | solution.py:80
  34.7 14.7 %all-to-all-done.1 = f32[64,8,256]{2,1,0:T(8,128)S(1)} async-done(((f32[64,8,256]{2,1,0:T(8,128)}), f32[64,8,256]{2,1,0:T(8,128)S(1)}, u32[]{:S(2)}, u32[]{:S(2)}) %all-to-all-start.1) | async-done | bytes 524320 | tf_op jit(solution)/shard_map/all_to_all | solution.py:85
  49.4 5.8 %all-to-all-start = ((f32[64,8,256]{2,1,0:T(8,128)}), f32[64,8,256]{2,1,0:T(8,128)}, u32[]{:S(2)}, u32[]{:S(2)}) async-start(f32[64,8,256]{2,1,0:T(8,128)} %bitcast.10), calls=%async_computation | async-start | bytes 1048576 | tf_op jit(solution)/shard_map/all_to_all | solution.py:86
  55.2 0.7 slice_bitcast_fusion.1
  55.9 8.0 %collective-permute-start.1 = (f32[1,256]{1,0:T(1,128)S(1)}, f32[1,256]{1,0:T(1,128)S(1)}, u32[]{:S(2)}, u32[]{:S(2)}) collective-permute-start(f32[1,256]{1,0:T(1,128)S(1)} %get-tuple-element.20), channel_id=1, source_target_pairs={{0,1},{1,2},{2,3},{4,5},{5,6},{6,7},{8,9},{9,10},{10,11},{12,13},{... | collective-permute-start | bytes 3080 | tf_op jit(solution)/shard_map/ppermute | solution.py:19
  64.0 1.9 %collective-permute-start = (f32[1,256]{1,0:T(1,128)S(1)}, f32[1,256]{1,0:T(1,128)S(1)}, u32[]{:S(2)}, u32[]{:S(2)}) collective-permute-start(f32[1,256]{1,0:T(1,128)S(1)} %get-tuple-element.21), channel_id=1, source_target_pairs={{1,0},{2,1},{3,2},{5,4},{6,5},{7,6},{9,8},{10,9},{11,10},{13,12},{... | collective-permute-start | bytes 3080 | tf_op jit(solution)/shard_map/ppermute | solution.py:20
  65.9 1.5 slice.267
  67.4 0.8 slice_bitcast_fusion
  68.6 1.6 gather_fusion
  70.2 1.8 all-to-all-done
  71.9 1.4 fusion.61
  73.6 0.9 copy.59
  74.5 1.1 copy-done.7
  75.6 2.2 %collective-permute-start.2 = (f32[48,1,256]{2,0,1:T(8,128)S(1)}, f32[48,1,256]{2,0,1:T(8,128)S(1)}, u32[]{:S(2)}, u32[]{:S(2)}) collective-permute-start(f32[48,1,256]{2,0,1:T(8,128)S(1)} %get-tuple-element.18), channel_id=1, source_target_pairs={{0,4},{4,8},{8,12},{12,16},{16,20},{20,24},{24,28},{28,32},{32,36}... | collective-permute-start | bytes 147464 | tf_op jit(solution)/shard_map/ppermute | solution.py:19
  77.8 1.3 collective-permute-start.3
  79.1 4.4 %copy.47 = f32[48,32,256]{0,1,2:T(8,128)} copy(f32[48,32,256]{2,1,0:T(8,128)S(1)} %pad_maximum_fusion.9) | data formatting | bytes 3145728 | tf_op jit(solution)/shard_map/concatenate | solution.py:98
  83.8 3.2 %pad_maximum_fusion = f32[48,34,256]{0,1,2:T(8,128)S(1)} fusion(f32[48,1,256]{0,1,2:T(1,128)S(1)} %copy.48, f32[48,32,256]{0,1,2:T(8,128)} %copy.47, f32[48,1,256]{0,1,2:T(1,128)S(1)} %copy.46), kind=kLoop, calls=%fused_computation.5 | loop fusion | flops 835584 | bytes 3342336 | tf_op jit(solution)/shard_map/concatenate | solution.py:21
  87.0 2.3 %copy-done.3 = f32[48,34,256]{0,1,2:T(8,128)} copy-done((f32[48,34,256]{0,1,2:T(8,128)}, f32[48,34,256]{0,1,2:T(8,128)S(1)}, u32[]{:S(2)}) %copy-start.3) | copy-done | bytes 1671192
  89.3 8.9 %collective-permute-start.4 = (f32[48,34,1]{0,1,2:T(8,128)S(1)}, f32[48,34,1]{0,1,2:T(8,128)S(1)}, u32[]{:S(2)}, u32[]{:S(2)}) collective-permute-start(f32[48,34,1]{0,1,2:T(8,128)S(1)} %get-tuple-element.10), channel_id=1, source_target_pairs={{0,1},{1,2},{2,3},{4,5},{5,6},{6,7},{8,9},{9,10},{10,11},{12,13},{... | collective-permute-start | bytes 19592 | tf_op jit(solution)/shard_map/ppermute | solution.py:19
  98.2 2.1 %collective-permute-start.5 = (f32[48,34,1]{0,1,2:T(8,128)S(1)}, f32[48,34,1]{0,1,2:T(8,128)S(1)}, u32[]{:S(2)}, u32[]{:S(2)}) collective-permute-start(f32[48,34,1]{0,1,2:T(8,128)S(1)} %get-tuple-element.11), channel_id=1, source_target_pairs={{1,0},{2,1},{3,2},{5,4},{6,5},{7,6},{9,8},{10,9},{11,10},{13,12},{... | collective-permute-start | bytes 19592 | tf_op jit(solution)/shard_map/ppermute | solution.py:20
  100.3 1.0 select_maximum_fusion.6
  101.3 4.9 %copy.50 = f32[48,34,256]{2,0,1:T(8,128)S(1)} copy(f32[48,34,256]{0,1,2:T(8,128)} %copy-done.3) | data formatting | bytes 3342336 | tf_op jit(solution)/shard_map/concatenate | solution.py:21
  106.2 1.0 collective-permute-done.5
  107.5 1.3 copy.49
  108.8 2.4 %select_maximum_fusion.4 = f32[50,34,258]{2,0,1:T(8,128)S(1)} fusion(f32[48,34,1]{2,0,1:T(8,128)S(1)} %copy.51, f32[48,34,256]{2,0,1:T(8,128)S(1)} %copy.50, f32[48,34,1]{2,0,1:T(8,128)} %copy.49), kind=kLoop, calls=%fused_computation.16 | loop fusion | flops 3508800 | bytes 3438624 | tf_op jit(solution)/shard_map/concatenate | solution.py:21
  111.3 9.6 %fusion.16 = f32[48,32,256]{2,0,1:T(8,128)S(1)} fusion(f32[48,32,256]{2,0,1:T(8,128)S(1)} %copy-done.8, f32[48,34,256]{2,0,1:T(8,128)S(1)} %copy.50, f32[48,34,1]{2,0,1:T(8,128)S(1)} %copy.51, f32[48,34,1]{2,0,1:T(8,128)S(1)} %copy-done.6, f32[50,34,258]{2,0,1:T(8,128)S(1)} %select_maximum_fusion.4, f32[48,1,256]{2,0,1:T(8,128)S(1)} %collective-permute-done.3, ...), kind=kLoop, calls=%fused_computation.41 | loop fusion | flops 22413312 | bytes 34812672 | tf_op jit(solution)/shard_map/add | solution.py:102
  120.9 4.0 %collective-permute-start.6 = (f32[48,1,256]{2,0,1:T(8,128)S(1)}, f32[48,1,256]{2,0,1:T(8,128)S(1)}, u32[]{:S(2)}, u32[]{:S(2)}) collective-permute-start(f32[48,1,256]{2,0,1:T(8,128)S(1)} %get-tuple-element.16), channel_id=1, source_target_pairs={{0,4},{4,8},{8,12},{12,16},{16,20},{20,24},{24,28},{28,32},{32,36}... | collective-permute-start | bytes 147464 | tf_op jit(solution)/shard_map/ppermute | solution.py:19
  125.0 1.3 collective-permute-start.7
  126.3 3.5 %collective-permute-done.7 = f32[48,1,256]{2,0,1:T(8,128)S(1)} collective-permute-done((f32[48,1,256]{2,0,1:T(8,128)S(1)}, f32[48,1,256]{2,0,1:T(8,128)S(1)}, u32[]{:S(2)}, u32[]{:S(2)}) %collective-permute-start.7) | collective-permute-done | bytes 49184 | tf_op jit(solution)/shard_map/ppermute | solution.py:20
  131.0 1.9 %collective-permute-start.9 = (f32[48,34,1]{0,1,2:T(8,128)S(1)}, f32[48,34,1]{0,1,2:T(8,128)S(1)}, u32[]{:S(2)}, u32[]{:S(2)}) collective-permute-start(f32[48,34,1]{0,1,2:T(8,128)S(1)} %copy.69), channel_id=1, source_target_pairs={{1,0},{2,1},{3,2},{5,4},{6,5},{7,6},{9,8},{10,9},{11,10},{13,12},{... | collective-permute-start | bytes 19592 | tf_op jit(solution)/shard_map/ppermute | solution.py:20
  132.9 8.0 %collective-permute-start.8 = (f32[48,34,1]{0,1,2:T(8,128)S(1)}, f32[48,34,1]{0,1,2:T(8,128)S(1)}, u32[]{:S(2)}, u32[]{:S(2)}) collective-permute-start(f32[48,34,1]{0,1,2:T(8,128)S(1)} %copy.68), channel_id=1, source_target_pairs={{0,1},{1,2},{2,3},{4,5},{5,6},{6,7},{8,9},{9,10},{10,11},{12,13},{... | collective-permute-start | bytes 19592 | tf_op jit(solution)/shard_map/ppermute | solution.py:19
  141.0 2.0 %fusion.67 = f32[64,8,256]{2,1,0:T(8,128)} fusion(f32[64,8,256]{2,1,0:T(8,128)} %all-to-all-done, f32[64,8,256]{2,1,0:T(8,128)S(1)} %copy-done.13, f32[512,256]{1,0:T(8,128)S(1)} %copy-done.11, f32[64,8]{1,0:T(8,128)S(1)} %bitcast.74), kind=kLoop, calls=%fused_computation.144 | loop fusion | flops 393216 | bytes 2099200 | tf_op jit(solution)/shard_map/mul | solution.py:92
  143.0 18.9 %all-to-all-start.3 = ((f32[64,8,256]{2,1,0:T(8,128)}), f32[64,8,256]{2,1,0:T(8,128)}, u32[]{:S(2)}, u32[]{:S(2)}) async-start(f32[64,8,256]{2,1,0:T(8,128)} %fusion.67), calls=%async_computation.3 | async-start | bytes 1048576 | tf_op jit(solution)/shard_map/all_to_all | solution.py:94
  161.9 1.3 copy.62
  163.2 1.3 copy.63
  164.5 3.2 %select_maximum_fusion = f32[50,34,258]{2,0,1:T(8,128)S(1)} fusion(f32[48,34,1]{2,0,1:T(8,128)} %copy.63, f32[48,34,1]{2,0,1:T(8,128)} %copy.62, f32[48,1,256]{2,0,1:T(8,128)S(1)} %collective-permute-done.7, f32[48,32,256]{2,0,1:T(8,128)} %copy-done.1, f32[48,1,256]{2,0,1:T(8,128)S(1)} %collective-permute-done.6), kind=kLoop, calls=%fused_computation.12 | loop fusion | flops 5263200 | bytes 3438624 | tf_op jit(solution)/shard_map/concatenate | solution.py:21
  167.7 3.0 %maximum_maximum_fusion = (f32[48,34,257]{2,0,1:T(8,128)}, f32[48,34,257]{2,0,1:T(8,128)}) fusion(f32[48,1,256]{2,0,1:T(8,128)S(1)} %collective-permute-done.7, f32[48,32,256]{2,0,1:T(8,128)S(1)} %copy-done.2, f32[48,1,256]{2,0,1:T(8,128)S(1)} %collective-permute-done.6, f32[48,34,1]{2,0,1:T(8,128)S(1)} %copy-done.4, f32[48,34,1]{2,0,1:T(8,128)S(1)} %copy-done.5), kind=kLoop, calls=%fused_computation.23 | loop fusion | flops 2516544 | bytes 5039616 | tf_op jit(solution)/shard_map/concatenate | solution.py:21
  170.7 11.8 %fusion.28 = f32[48,32,256]{2,0,1:T(8,128)} fusion(f32[48,32,256]{2,0,1:T(8,128)} %copy-done.1, f32[50,34,258]{2,0,1:T(8,128)S(1)} %select_maximum_fusion, f32[48,34,257]{2,0,1:T(8,128)} %get-tuple-element.13, f32[48,1,256]{2,0,1:T(8,128)S(1)} %collective-permute-done.7, f32[48,34,257]{2,0,1:T(8,128)} %get-tuple-element.12, ...), kind=kLoop, calls=%fused_computation.54 | loop fusion | flops 20054016 | bytes 42565632 | tf_op jit(solution)/shard_map/add | solution.py:102
  182.6 3.5 %copy.67 = f32[48,32,256]{2,1,0:T(8,128)} copy(f32[48,32,256]{2,0,1:T(8,128)} %fusion.28) | data formatting | bytes 3145728
  186.0 2.1 %gather_fusion.1 = f32[256,256]{1,0:T(8,128)S(1)} fusion(f32[512,256]{1,0:T(8,128)} %bitcast.17, s32[1024]{0:T(1024)S(1)} %pad_clamp_fusion), kind=kCustom, calls=%fused_computation.1 | custom fusion | bytes 525312 | tf_op jit(solution)/shard_map/gather | solution.py:95
  188.1 0.9 fusion.73
  (72 shorter events, 5.3 us)
Async XLA Ops:
  0.6 31.9 %copy-start = (f32[1,256,256]{2,1,0:T(8,128)S(1)}, f32[1,256,256]{2,1,0:T(8,128)}, u32[]{:S(2)}) copy-start(f32[1,256,256]{2,1,0:T(8,128)} %param.8) | copy-start | bytes 786436
  6.5 21.4 %all-to-all-start.2 = ((f32[64,8,1]{1,2,0:T(1,128)}), f32[64,8,1]{1,2,0:T(1,128)S(1)}, u32[]{:S(2)}, u32[]{:S(2)}) async-start(f32[64,8,1]{1,2,0:T(1,128)} %bitcast.14), calls=%async_computation.2 | async-start | bytes 65536 | tf_op jit(solution)/shard_map/all_to_all | solution.py:87
  27.9 40.3 %copy-start.16 = (f32[64,8,1]{1,2,0:T(1,128)}, f32[64,8,1]{1,2,0:T(1,128)S(1)}, u32[]{:S(2)}) copy-start(f32[64,8,1]{1,2,0:T(1,128)S(1)} %all-to-all-done.2) | copy-start | bytes 6148
  27.9 21.5 %all-to-all-start.1 = ((f32[64,8,256]{2,1,0:T(8,128)}), f32[64,8,256]{2,1,0:T(8,128)S(1)}, u32[]{:S(2)}, u32[]{:S(2)}) async-start(f32[64,8,256]{2,1,0:T(8,128)} %bitcast.11), calls=%async_computation.1 | async-start | bytes 1048576 | tf_op jit(solution)/shard_map/all_to_all | solution.py:85
  49.4 22.5 %copy-start.12 = (f32[64,8,256]{2,1,0:T(8,128)}, f32[64,8,256]{2,1,0:T(8,128)S(1)}, u32[]{:S(2)}) copy-start(f32[64,8,256]{2,1,0:T(8,128)S(1)} %all-to-all-done.1) | copy-start | bytes 1572868
  49.4 22.5 %all-to-all-start = ((f32[64,8,256]{2,1,0:T(8,128)}), f32[64,8,256]{2,1,0:T(8,128)}, u32[]{:S(2)}, u32[]{:S(2)}) async-start(f32[64,8,256]{2,1,0:T(8,128)} %bitcast.10), calls=%async_computation | async-start | bytes 1048576 | tf_op jit(solution)/shard_map/all_to_all | solution.py:86
  55.9 44.4 %collective-permute-start.1 = (f32[1,256]{1,0:T(1,128)S(1)}, f32[1,256]{1,0:T(1,128)S(1)}, u32[]{:S(2)}, u32[]{:S(2)}) collective-permute-start(f32[1,256]{1,0:T(1,128)S(1)} %get-tuple-element.20), channel_id=1, source_target_pairs={{0,1},{1,2},{2,3},{4,5},{5,6},{6,7},{8,9},{9,10},{10,11},{12,13},{... | collective-permute-start | bytes 3080 | tf_op jit(solution)/shard_map/ppermute | solution.py:19
  64.0 36.3 %collective-permute-start = (f32[1,256]{1,0:T(1,128)S(1)}, f32[1,256]{1,0:T(1,128)S(1)}, u32[]{:S(2)}, u32[]{:S(2)}) collective-permute-start(f32[1,256]{1,0:T(1,128)S(1)} %get-tuple-element.21), channel_id=1, source_target_pairs={{1,0},{2,1},{3,2},{5,4},{6,5},{7,6},{9,8},{10,9},{11,10},{13,12},{... | collective-permute-start | bytes 3080 | tf_op jit(solution)/shard_map/ppermute | solution.py:20
  70.1 1.8 copy-start.10
  74.5 1.1 copy-start.7
  75.6 8.1 %collective-permute-start.2 = (f32[48,1,256]{2,0,1:T(8,128)S(1)}, f32[48,1,256]{2,0,1:T(8,128)S(1)}, u32[]{:S(2)}, u32[]{:S(2)}) collective-permute-start(f32[48,1,256]{2,0,1:T(8,128)S(1)} %get-tuple-element.18), channel_id=1, source_target_pairs={{0,4},{4,8},{8,12},{12,16},{16,20},{20,24},{24,28},{28,32},{32,36}... | collective-permute-start | bytes 147464 | tf_op jit(solution)/shard_map/ppermute | solution.py:19
  77.8 5.8 %collective-permute-start.3 = (f32[48,1,256]{2,0,1:T(8,128)S(1)}, f32[48,1,256]{2,0,1:T(8,128)S(1)}, u32[]{:S(2)}, u32[]{:S(2)}) collective-permute-start(f32[48,1,256]{2,0,1:T(8,128)S(1)} %get-tuple-element.19), channel_id=1, source_target_pairs={{4,0},{8,4},{12,8},{16,12},{20,16},{24,20},{28,24},{32,28},{36,32}... | collective-permute-start | bytes 147464 | tf_op jit(solution)/shard_map/ppermute | solution.py:20
  83.8 16.5 %copy-start.14 = (f32[1,256,256]{2,1,0:T(8,128)S(1)}, f32[1,256,256]{2,1,0:T(8,128)}, u32[]{:S(2)}) copy-start(f32[1,256,256]{2,1,0:T(8,128)} %param.7) | copy-start | bytes 786436
  87.0 2.3 %copy-start.3 = (f32[48,34,256]{0,1,2:T(8,128)}, f32[48,34,256]{0,1,2:T(8,128)S(1)}, u32[]{:S(2)}) copy-start(f32[48,34,256]{0,1,2:T(8,128)S(1)} %pad_maximum_fusion) | copy-start | bytes 5013508
  89.3 18.2 %collective-permute-start.4 = (f32[48,34,1]{0,1,2:T(8,128)S(1)}, f32[48,34,1]{0,1,2:T(8,128)S(1)}, u32[]{:S(2)}, u32[]{:S(2)}) collective-permute-start(f32[48,34,1]{0,1,2:T(8,128)S(1)} %get-tuple-element.10), channel_id=1, source_target_pairs={{0,1},{1,2},{2,3},{4,5},{5,6},{6,7},{8,9},{9,10},{10,11},{12,13},{... | collective-permute-start | bytes 19592 | tf_op jit(solution)/shard_map/ppermute | solution.py:19
  98.2 9.0 %collective-permute-start.5 = (f32[48,34,1]{0,1,2:T(8,128)S(1)}, f32[48,34,1]{0,1,2:T(8,128)S(1)}, u32[]{:S(2)}, u32[]{:S(2)}) collective-permute-start(f32[48,34,1]{0,1,2:T(8,128)S(1)} %get-tuple-element.11), channel_id=1, source_target_pairs={{1,0},{2,1},{3,2},{5,4},{6,5},{7,6},{9,8},{10,9},{11,10},{13,12},{... | collective-permute-start | bytes 19592 | tf_op jit(solution)/shard_map/ppermute | solution.py:20
  100.3 5.9 %copy-start.18 = (f32[1,256]{1,0:T(1,128)}, f32[1,256]{1,0:T(1,128)S(1)}, u32[]{:S(2)}) copy-start(f32[1,256]{1,0:T(1,128)S(1)} %collective-permute-done) | copy-start | bytes 3076
  108.8 2.5 %copy-start.6 = (f32[48,34,1]{2,0,1:T(8,128)S(1)}, f32[48,34,1]{2,0,1:T(8,128)}, u32[]{:S(2)}) copy-start(f32[48,34,1]{2,0,1:T(8,128)} %copy.49) | copy-start | bytes 19588
  108.8 2.5 %copy-start.8 = (f32[48,32,256]{2,0,1:T(8,128)S(1)}, f32[48,32,256]{2,0,1:T(8,128)}, u32[]{:S(2)}) copy-start(f32[48,32,256]{2,0,1:T(8,128)} %copy-done.7) | copy-start | bytes 4718596
  108.8 2.5 %copy-start.9 = (f32[48,32,256]{2,1,0:T(8,128)S(1)}, f32[48,32,256]{2,1,0:T(8,128)}, u32[]{:S(2)}) copy-start(f32[48,32,256]{2,1,0:T(8,128)} %param.10) | copy-start | bytes 4718596
  111.3 15.0 %copy-start.17 = (f32[64,8,1]{1,2,0:T(1,128)S(1)}, f32[64,8,1]{1,2,0:T(1,128)}, u32[]{:S(2)}) copy-start(f32[64,8,1]{1,2,0:T(1,128)} %copy-done.16) | copy-start | bytes 6148
  120.9 9.0 %copy-start.1 = (f32[48,32,256]{2,0,1:T(8,128)}, f32[48,32,256]{2,0,1:T(8,128)S(1)}, u32[]{:S(2)}) copy-start(f32[48,32,256]{2,0,1:T(8,128)S(1)} %fusion.16) | copy-start | bytes 4718596
  120.9 5.4 %collective-permute-start.6 = (f32[48,1,256]{2,0,1:T(8,128)S(1)}, f32[48,1,256]{2,0,1:T(8,128)S(1)}, u32[]{:S(2)}, u32[]{:S(2)}) collective-permute-start(f32[48,1,256]{2,0,1:T(8,128)S(1)} %get-tuple-element.16), channel_id=1, source_target_pairs={{0,4},{4,8},{8,12},{12,16},{16,20},{20,24},{24,28},{28,32},{32,36}... | collective-permute-start | bytes 147464 | tf_op jit(solution)/shard_map/ppermute | solution.py:19
  125.0 4.8 %collective-permute-start.7 = (f32[48,1,256]{2,0,1:T(8,128)S(1)}, f32[48,1,256]{2,0,1:T(8,128)S(1)}, u32[]{:S(2)}, u32[]{:S(2)}) collective-permute-start(f32[48,1,256]{2,0,1:T(8,128)S(1)} %get-tuple-element.17), channel_id=1, source_target_pairs={{4,0},{8,4},{12,8},{16,12},{20,16},{24,20},{28,24},{32,28},{36,32}... | collective-permute-start | bytes 147464 | tf_op jit(solution)/shard_map/ppermute | solution.py:20
  130.2 10.7 %copy-start.11 = (f32[512,256]{1,0:T(8,128)S(1)}, f32[512,256]{1,0:T(8,128)}, u32[]{:S(2)}) copy-start(f32[512,256]{1,0:T(8,128)} %copy-done.10) | copy-start | bytes 1572868
  130.2 10.8 %copy-start.13 = (f32[64,8,256]{2,1,0:T(8,128)S(1)}, f32[64,8,256]{2,1,0:T(8,128)}, u32[]{:S(2)}) copy-start(f32[64,8,256]{2,1,0:T(8,128)} %copy-done.12) | copy-start | bytes 1572868
  131.0 32.2 %collective-permute-start.9 = (f32[48,34,1]{0,1,2:T(8,128)S(1)}, f32[48,34,1]{0,1,2:T(8,128)S(1)}, u32[]{:S(2)}, u32[]{:S(2)}) collective-permute-start(f32[48,34,1]{0,1,2:T(8,128)S(1)} %copy.69), channel_id=1, source_target_pairs={{1,0},{2,1},{3,2},{5,4},{6,5},{7,6},{9,8},{10,9},{11,10},{13,12},{... | collective-permute-start | bytes 19592 | tf_op jit(solution)/shard_map/ppermute | solution.py:20
  132.9 29.0 %collective-permute-start.8 = (f32[48,34,1]{0,1,2:T(8,128)S(1)}, f32[48,34,1]{0,1,2:T(8,128)S(1)}, u32[]{:S(2)}, u32[]{:S(2)}) collective-permute-start(f32[48,34,1]{0,1,2:T(8,128)S(1)} %copy.68), channel_id=1, source_target_pairs={{0,1},{1,2},{2,3},{4,5},{5,6},{6,7},{8,9},{9,10},{10,11},{12,13},{... | collective-permute-start | bytes 19592 | tf_op jit(solution)/shard_map/ppermute | solution.py:19
  143.0 43.1 %all-to-all-start.3 = ((f32[64,8,256]{2,1,0:T(8,128)}), f32[64,8,256]{2,1,0:T(8,128)}, u32[]{:S(2)}, u32[]{:S(2)}) async-start(f32[64,8,256]{2,1,0:T(8,128)} %fusion.67), calls=%async_computation.3 | async-start | bytes 1048576 | tf_op jit(solution)/shard_map/all_to_all | solution.py:94
  164.4 3.2 %copy-start.2 = (f32[48,32,256]{2,0,1:T(8,128)S(1)}, f32[48,32,256]{2,0,1:T(8,128)}, u32[]{:S(2)}) copy-start(f32[48,32,256]{2,0,1:T(8,128)} %copy-done.1) | copy-start | bytes 4718596
  164.4 3.2 %copy-start.4 = (f32[48,34,1]{2,0,1:T(8,128)S(1)}, f32[48,34,1]{2,0,1:T(8,128)}, u32[]{:S(2)}) copy-start(f32[48,34,1]{2,0,1:T(8,128)} %copy.62) | copy-start | bytes 19588
  164.5 3.2 %copy-start.5 = (f32[48,34,1]{2,0,1:T(8,128)S(1)}, f32[48,34,1]{2,0,1:T(8,128)}, u32[]{:S(2)}) copy-start(f32[48,34,1]{2,0,1:T(8,128)} %copy.63) | copy-start | bytes 19588
  186.0 2.1 %copy-start.15 = (f32[258,258]{1,0:T(8,128)S(1)}, f32[258,258]{1,0:T(8,128)}, u32[]{:S(2)}) copy-start(f32[258,258]{1,0:T(8,128)} %select_maximum_fusion.6) | copy-start | bytes 798772
  186.0 2.1 %copy-start.19 = (f32[1,256]{1,0:T(1,128)S(1)}, f32[1,256]{1,0:T(1,128)}, u32[]{:S(2)}) copy-start(f32[1,256]{1,0:T(1,128)} %copy-done.18) | copy-start | bytes 3076
where the time goes:
time: 190 us; the launch traced here: 189 us
  starting transfers between devices  81.6 us (43%)
  other arithmetic  41.2 us (22%)
  local copies, waits for them, and re-layouts  36.6 us (19%)
  waiting for transfers between devices  27 us (14%)
    ppermute x5, starting transfers between devices, padded_2(): before = lax.ppermute(last, axis, up)  31.2 us
    add x2, other arithmetic, local(): field = field + diffusivity * stencil_apply(padded)  21.4 us
    all_to_all x1, starting transfers between devices, local(): lax.all_to_all(flux_slots, 'span', split_axis=0, concat_axis=0, tiled=True)  18.9 us
    all_to_all x1, waiting for transfers between devices, local(): lax.all_to_all(send_temp, 'span', split_axis=0, concat_axis=0, tiled=True)  14.7 us
    concatenate x6, other arithmetic, padded_2(): array = jnp.concatenate([before, array, after], axis=dim)  12.9 us
    all_to_all x1, starting transfers between devices, local(): lax.all_to_all(send_code, 'span', split_axis=0, concat_axis=0, tiled=True)  12.6 us
    ppermute x5, starting transfers between devices, padded_2(): after = lax.ppermute(initial, axis, down)  8.54 us
    unnamed x43, local copies, waits for them, and re-layouts  7.73 us
  transfers between devices with their start and end apart: 14, of which 5 were waited for; matrix products, arithmetic and copies ran while one was open for 28% of the time, Pallas kernels for 0%

commit v1 on v0

v1 whole, which is shorter than its diff:
```python
import jax
import jax.numpy as jnp
from jax import lax
from jax.experimental import pallas as pl
from jax.experimental.pallas import tpu as pltpu
from jax.sharding import PartitionSpec as P

SHELL_RATE = 0.15
SHELL_SINK = 0.5
FACE_GAIN = 0.5
F32 = jnp.float32
BF16 = jnp.bfloat16

NB = 256
SB = 256
CX = 32
DZ = 48
CAP = 8
SPAN = 64
SLOTS = SPAN * CAP
PER = 4 * CAP + 1
EX = CX + 8
EY = SB + 128

VMEM = pl.BlockSpec(memory_space=pltpu.VMEM)


def params(mib):
    return pltpu.CompilerParams(vmem_limit_bytes=mib * 2**20)


def cost(flops, moved):
    return pl.CostEstimate(flops=flops, bytes_accessed=moved, transcendentals=0)


def split3(x):
    hi = x.astype(BF16)
    rest = x - hi.astype(F32)
    mid = rest.astype(BF16)
    low = (rest - mid.astype(F32)).astype(BF16)
    return hi, mid, low


def pick(onehot, x, dims=(((1,), (0,)), ((), ()))):
    total = None
    for part in split3(x):
        term = lax.dot_general(onehot, part, dims, preferred_element_type=F32)
        total = term if total is None else total + term
    return total


def iota(shape, dim):
    return lax.broadcasted_iota(jnp.int32, shape, dim)


def as_column(row, eye):
    return jnp.sum(jnp.where(eye, row, 0.0), axis=1, keepdims=True)


def pack_kernel(routes_ref, tile_ref, closed_ref, temp_ref, gain_ref, out_ref):
    sub, lane = iota((NB, NB), 0), iota((NB, NB), 1)
    eye = sub == lane
    target = routes_ref[...].astype(F32)
    same = as_column(target, eye) == target
    rank_row = jnp.sum(
        jnp.where(jnp.logical_and(same, sub < lane), 1.0, 0.0), axis=0, keepdims=True
    )
    rank_col = jnp.sum(
        jnp.where(jnp.logical_and(same, lane < sub), 1.0, 0.0), axis=1, keepdims=True
    )
    tile_col = as_column(tile_ref[...].astype(F32), eye)
    closed_col = as_column(closed_ref[...].astype(F32), eye)
    position = (target * CAP + rank_row).astype(jnp.int32)
    put = jnp.where(iota((SLOTS, NB), 0) == position, 1.0, 0.0).astype(BF16)
    codes = lax.dot_general(
        jnp.where(iota((SPAN, NB), 0) == routes_ref[...], 1.0, 0.0).astype(BF16),
        jnp.where(iota((NB, 128), 1) == rank_col.astype(jnp.int32), tile_col, 0.0).astype(BF16),
        (((1,), (0,)), ((), ())),
        preferred_element_type=F32,
    )
    out_ref[pl.ds(4 * CAP, SPAN, stride=PER), :] = codes
    temp = pick(put, temp_ref[...])
    gain = pick(put, gain_ref[...] * closed_col)
    for c, slots in enumerate((temp[:, :128], temp[:, 128:], gain[:, :128], gain[:, 128:])):
        for t in range(SPAN):
            out_ref[pl.ds(t * PER + c, CAP, stride=4), :] = slots[t * CAP : (t + 1) * CAP]


def edge_rows_kernel(die_ref, diff_ref, even_ref, odd_ref):
    is_even = lax.rem(lax.axis_index("span"), 2) == 0

    def layer(z, carry):
        for n, (ref, low, high) in enumerate(
            ((die_ref, 0, CX - 2), (die_ref, 1, CX - 1), (diff_ref, 0, CX - 1))
        ):
            first = ref[pl.ds(z * CX + low, 1), :]
            last = ref[pl.ds(z * CX + high, 1), :]
            even_ref[pl.ds(n * DZ + z, 1), :] = jnp.where(is_even, last, first)
            odd_ref[pl.ds(n * DZ + z, 1), :] = jnp.where(is_even, first, last)
        return carry

    lax.fori_loop(0, DZ, layer, 0, unroll=4)


def edge_columns_kernel(
    die_ref, diff_ref, even_in, odd_in, temp_ref, even_ref, odd_ref, die_rim, diff_rim
):
    span_even = lax.rem(lax.axis_index("span"), 2) == 0
    depth_even = lax.rem(lax.axis_index("depth"), 2) == 0
    sub = iota((8, SB), 0)

    def rim_of(z, spots):
        tile = jnp.zeros((8, SB), F32)
        for spot, n, up in spots:
            at = pl.ds(n * DZ + z, 1)
            row = jnp.where(span_even != up, even_in[at, :], odd_in[at, :])
            tile = jnp.where(sub == spot, row, tile)
        return tile

    lane = iota((EX, 128), 1)

    def add_layer(z, kept):
        v_left, v_right, k_left, k_right = kept
        rows, rim = pl.ds(pl.multiple_of(z * CX, CX), CX), pl.ds(pl.multiple_of(z * 8, 8), 8)
        v_rim = rim_of(z, ((0, 0, False), (1, 1, False), (6, 0, True), (7, 1, True)))
        k_rim = rim_of(z, ((0, 2, False), (7, 2, True)))
        die_rim[rim, :] = v_rim
        diff_rim[rim, :] = k_rim
        v = jnp.concatenate([die_ref[rows, :], v_rim], axis=0)
        k = jnp.concatenate([diff_ref[rows, :], k_rim], axis=0)
        v_here, k_here = lax.shift_right_logical(lane, 1) == z, lane == z
        v_left = jnp.where(v_here, pltpu.roll(v[:, :128], 2 * z, 1), v_left)
        v_right = jnp.where(v_here, pltpu.roll(v[:, 128:], 2 * z + 2, 1), v_right)
        k_left = jnp.where(k_here, pltpu.roll(k[:, :128], z, 1), k_left)
        k_right = jnp.where(k_here, pltpu.roll(k[:, 128:], z + 1, 1), k_right)
        return v_left, v_right, k_left, k_right

    none = jnp.zeros((EX, 128), F32)
    v_left, v_right, k_left, k_right = lax.fori_loop(0, DZ, add_layer, (none,) * 4)
    even_ref[:EX, :128] = jnp.where(depth_even, v_right, v_left)
    even_ref[:EX, 128:] = jnp.where(depth_even, k_right, k_left)
    odd_ref[:EX, :128] = jnp.where(depth_even, v_left, v_right)
    odd_ref[:EX, 128:] = jnp.where(depth_even, k_left, k_right)
    first, last = temp_ref[0:1, :], temp_ref[NB - 1 : NB, :]
    even_ref[EX:, :] = jnp.broadcast_to(jnp.where(depth_even, last, first), (8, SB))
    odd_ref[EX:, :] = jnp.broadcast_to(jnp.where(depth_even, first, last), (8, SB))


def across(p):
    q = p + 0.5 * (pltpu.roll(p, 1, 1) + pltpu.roll(p, p.shape[1] - 1, 1))
    return q + 0.5 * (pltpu.roll(q, 1, 0) + pltpu.roll(q, q.shape[0] - 1, 0))


def sweeps_kernel(
    die_ref, diff_ref, die_rim, diff_rim, even_in, odd_in, out_ref, top_ref, field, later, rate
):
    depth_even = lax.rem(lax.axis_index("depth"), 2) == 0
    none = jnp.zeros((EX, EY), F32)
    for ref in (field, later):
        ref[0] = none
        ref[DZ + 1] = none
    lane = iota((EX, 128), 1)

    def fill(z, carry):
        rows, rim = pl.ds(pl.multiple_of(z * CX, CX), CX), pl.ds(pl.multiple_of(z * 8, 8), 8)
        right = jnp.where(depth_even, even_in[:EX, :], odd_in[:EX, :])
        left = jnp.where(depth_even, odd_in[:EX, :], even_in[:EX, :])
        field[z + 1, :CX, :SB] = die_ref[rows, :]
        field[z + 1, CX:, :SB] = die_rim[rim, :]
        rate[z, :CX, :SB] = diff_ref[rows, :]
        rate[z, CX:, :SB] = diff_rim[rim, :]
        v_right = pltpu.roll(right[:, :128], lax.rem(128 - 2 * z, 128), 1)
        v_left = pltpu.roll(left[:, :128], 126 - 2 * z, 1)
        k_right = pltpu.roll(right[:, 128:], lax.rem(128 - z, 128), 1)
        k_left = pltpu.roll(left[:, 128:], 127 - z, 1)
        field[z + 1, :, SB:] = jnp.where(lane < 2, v_right, jnp.where(lane >= 126, v_left, 0.0))
        rate[z, :, SB:] = jnp.where(lane < 1, k_right, jnp.where(lane >= 127, k_left, 0.0))
        return carry

    lax.fori_loop(0, DZ, fill, 0)

    def first(z, carry):
        v = field[z + 1]
        p = 2.0 * v + (field[z] + field[z + 2])
        later[z + 1] = v + rate[z] * (across(p) - 16.0 * v)
        return carry

    lax.fori_loop(0, DZ, first, 0)

    def second(z, carry):
        p = 2.0 * later[z + 1] + (later[z] + later[z + 2])
        q = across(p)[:CX, :SB]
        v = later[z + 1, :CX, :SB]
        out_ref[z] = v + rate[z, :CX, :SB] * (q - 16.0 * v)
        return carry

    lax.fori_loop(0, DZ, second, 0)
    top_ref[...] = rate[0:3]


def owner_kernel(got_ref, face_ref, flux_ref, heat_ref, even_ref, odd_ref):
    codes = got_ref[pl.ds(4 * CAP, SPAN, stride=PER), :]
    lane = iota((SPAN, 128), 1).astype(F32)
    onehot = jnp.concatenate(
        [jnp.where(codes[:, k : k + 1] == lane, 1.0, 0.0) for k in range(CAP)], axis=0
    ).astype(BF16)
    face = face_ref[...]
    padded = jnp.concatenate([face, jnp.zeros((128 - CX, SB), F32)], axis=0)
    touched = pick(onehot, padded)

    def slots(c):
        return jnp.concatenate(
            [got_ref[pl.ds(k * 4 + c, SPAN, stride=PER), :] for k in range(CAP)], axis=0
        )

    temp = jnp.concatenate([slots(0), slots(1)], axis=1)
    gain = jnp.concatenate([slots(2), slots(3)], axis=1)
    flux = gain * (temp - touched)
    for k in range(CAP):
        for c in range(2):
            flux_ref[pl.ds(c * CAP + k, SPAN, stride=2 * CAP), :] = flux[
                k * SPAN : (k + 1) * SPAN, c * 128 : (c + 1) * 128
            ]
    heat = FACE_GAIN * pick(onehot, flux, (((0,), (0,)), ((), ())))[:CX]
    heat_ref[...] = heat
    is_even = lax.rem(lax.axis_index("span"), 2) == 0
    even_ref[...] = jnp.where(is_even, heat[CX - 8 :], heat[:8])
    odd_ref[...] = jnp.where(is_even, heat[:8], heat[CX - 8 :])


def heat_edges_kernel(heat_ref, even_in, odd_in, rows_ref, even_ref, odd_ref):
    span_even = lax.rem(lax.axis_index("span"), 2) == 0
    depth_even = lax.rem(lax.axis_index("depth"), 2) == 0
    below = jnp.where(span_even, even_in[...], odd_in[...])
    above = jnp.where(span_even, odd_in[...], even_in[...])
    sub = iota((8, SB), 0)
    rim = jnp.where(sub < 2, below, jnp.where(sub >= 6, above, 0.0))
    rows = jnp.concatenate([heat_ref[...], rim], axis=0)
    rows_ref[...] = rows
    even_ref[...] = jnp.where(depth_even, rows[:, 128:], rows[:, :128])
    odd_ref[...] = jnp.where(depth_even, rows[:, :128], rows[:, 128:])


def heat_kernel(base_ref, rate_ref, rows_ref, even_in, odd_in, out_ref):
    depth_even = lax.rem(lax.axis_index("depth"), 2) == 0
    right = jnp.where(depth_even, even_in[...], odd_in[...])
    left = jnp.where(depth_even, odd_in[...], even_in[...])
    lane = iota((EX, 128), 1)
    rim = jnp.where(lane < 2, right, jnp.where(lane >= 126, left, 0.0))
    heat = jnp.concatenate([rows_ref[...], rim], axis=1)
    spread = across(heat)
    first = heat + rate_ref[0] * (2.0 * spread - 16.0 * heat)
    second = rate_ref[1] * spread
    for z, (own, p) in enumerate(
        ((first, 2.0 * first + second), (second, 2.0 * second + first), (None, second))
    ):
        step = across(p)
        if own is not None:
            step = step - 16.0 * own
        step = rate_ref[z] * step
        if own is not None:
            step = own + step
        out_ref[z] = base_ref[z] + step[:CX, :SB]


def shell_kernel(routes_ref, temp_ref, even_in, odd_in, base_ref, take_ref):
    depth_even = lax.rem(lax.axis_index("depth"), 2) == 0
    below = jnp.where(depth_even, even_in[EX : EX + 1, :], odd_in[EX : EX + 1, :])
    above = jnp.where(depth_even, odd_in[EX : EX + 1, :], even_in[EX : EX + 1, :])
    temp = temp_ref[...]
    sub, lane = iota((NB, SB), 0), iota((NB, SB), 1)
    upper = jnp.where(sub == 0, above, pltpu.roll(temp, 1, 0))
    lower = jnp.where(sub == NB - 1, below, pltpu.roll(temp, NB - 1, 0))
    before = jnp.where(lane == 0, 0.0, pltpu.roll(temp, 1, 1))
    after = jnp.where(lane == SB - 1, 0.0, pltpu.roll(temp, SB - 1, 1))
    laplace = lower + upper + after + before - 4.0 * temp
    base_ref[...] = temp + SHELL_RATE * laplace
    target = routes_ref[...].astype(F32)
    target_col = as_column(target, sub == lane)
    same = jnp.logical_and(target_col == target, lane < sub)
    rank_col = jnp.sum(jnp.where(same, 1.0, 0.0), axis=1, keepdims=True)
    position = (target_col * CAP + rank_col).astype(jnp.int32)
    take_ref[...] = jnp.where(iota((NB, SLOTS), 1) == position, 1.0, 0.0).astype(BF16)


def sink_kernel(base_ref, take_ref, flux_ref, out_ref):
    take = take_ref[...]
    for c in range(2):
        flux = flux_ref[:, c * CAP : (c + 1) * CAP, :].reshape(SLOTS, 128)
        half = slice(c * 128, (c + 1) * 128)
        out_ref[:, half] = base_ref[:, half] - SHELL_SINK * pick(take, flux)


def swap(even, odd, axis):
    size = lax.axis_size(axis)
    pairs = [(i, i ^ 1) for i in range(size)]
    shifted = [(i, ((i + 1) ^ 1) - 1) for i in range(1, size - 1)]
    return lax.ppermute(even, axis, pairs), lax.ppermute(odd, axis, shifted)


def local(shell_temp, contact_gain, die_temp, diffusivity, routes, tile_rows, closed):
    temp, gain = shell_temp[0], contact_gain[0]
    target = routes.reshape(1, NB)
    die, diff = die_temp.reshape(DZ * CX, SB), diffusivity.reshape(DZ * CX, SB)
    sent = pl.pallas_call(
        pack_kernel,
        out_shape=jax.ShapeDtypeStruct((SPAN * PER, 128), F32),
        in_specs=[VMEM] * 5,
        out_specs=VMEM,
        compiler_params=params(16),
        name="pack",
    )(target, tile_rows, closed, temp, gain)
    got = lax.all_to_all(
        sent.reshape(SPAN * PER, 1, 128), "span", split_axis=0, concat_axis=0, tiled=True
    ).reshape(SPAN * PER, 128)

    rows = jax.ShapeDtypeStruct((3 * DZ, SB), F32)
    even, odd = pl.pallas_call(
        edge_rows_kernel,
        out_shape=(rows, rows),
        in_specs=[VMEM] * 2,
        out_specs=(VMEM,) * 2,
        compiler_params=params(16),
        name="edge_rows",
    )(die, diff)
    even, odd = swap(even, odd, "span")
    columns, rim = (
        jax.ShapeDtypeStruct((EX + 8, SB), F32),
        jax.ShapeDtypeStruct((DZ * 8, SB), F32),
    )
    even, odd, die_rim, diff_rim = pl.pallas_call(
        edge_columns_kernel,
        out_shape=(columns, columns, rim, rim),
        in_specs=[VMEM] * 5,
        out_specs=(VMEM,) * 4,
        compiler_params=params(16),
        name="edge_columns",
    )(die, diff, even, odd, temp)
    even, odd = swap(even, odd, "depth")
    base, top = pl.pallas_call(
        sweeps_kernel,
        out_shape=(
            jax.ShapeDtypeStruct((DZ, CX, SB), F32),
            jax.ShapeDtypeStruct((3, EX, EY), F32),
        ),
        in_specs=[VMEM] * 6,
        out_specs=(VMEM,) * 2,
        scratch_shapes=[
            pltpu.VMEM((DZ + 2, EX, EY), F32),
            pltpu.VMEM((DZ + 2, EX, EY), F32),
            pltpu.VMEM((DZ, EX, EY), F32),
        ],
        compiler_params=params(28),
        cost_estimate=cost(40 * DZ * EX * EY, 5 * DZ * CX * SB * 4),
        name="sweeps",
    )(die, diff, die_rim, diff_rim, even, odd)
    shell_base, take = pl.pallas_call(
        shell_kernel,
        out_shape=(
            jax.ShapeDtypeStruct((NB, SB), F32),
            jax.ShapeDtypeStruct((NB, SLOTS), BF16),
        ),
        in_specs=[VMEM] * 4,
        out_specs=(VMEM,) * 2,
        compiler_params=params(16),
        name="shell",
    )(target, temp, even, odd)

    got, base, shell_base = lax.optimization_barrier((got, base, shell_base))
    edge = jax.ShapeDtypeStruct((8, SB), F32)
    flux, heat, even, odd = pl.pallas_call(
        owner_kernel,
        out_shape=(
            jax.ShapeDtypeStruct((2 * SLOTS, 128), F32),
            jax.ShapeDtypeStruct((CX, SB), F32),
            edge,
            edge,
        ),
        grid=(1,),
        in_specs=[VMEM, pl.BlockSpec((CX, SB), lambda i: (0, 0))],
        out_specs=(VMEM,) * 4,
        compiler_params=params(16),
        name="owner",
    )(got, die)
    back = lax.all_to_all(flux, "span", split_axis=0, concat_axis=0, tiled=True)
    even, odd = swap(even, odd, "span")
    block = jax.ShapeDtypeStruct((EX, 128), F32)
    heat_rows, even, odd = pl.pallas_call(
        heat_edges_kernel,
        out_shape=(jax.ShapeDtypeStruct((EX, SB), F32), block, block),
        in_specs=[VMEM] * 3,
        out_specs=(VMEM,) * 3,
        compiler_params=params(8),
        name="heat_edges",
    )(heat, even, odd)
    even, odd = swap(even, odd, "depth")
    layers = pl.BlockSpec((3, CX, SB), lambda i: (0, 0, 0))
    die_next = pl.pallas_call(
        heat_kernel,
        grid=(1,),
        out_shape=jax.ShapeDtypeStruct((DZ, CX, SB), F32),
        in_specs=[layers] + [VMEM] * 4,
        out_specs=layers,
        input_output_aliases={0: 0},
        compiler_params=params(8),
        name="heat",
    )(base, top, heat_rows, even, odd)
    shell_next = pl.pallas_call(
        sink_kernel,
        out_shape=jax.ShapeDtypeStruct((NB, SB), F32),
        in_specs=[VMEM] * 3,
        out_specs=VMEM,
        compiler_params=params(16),
        name="sink",
    )(shell_base, take, back.reshape(SPAN, 2 * CAP, 128))
    return shell_next[None], die_next


def solution(mesh):
    placed = (
        P("span", "depth", None),
        P("span", "depth", None),
        P(None, "span", "depth"),
        P(None, "span", "depth"),
        P("span", "depth", None),
        P("span", "depth"),
        P("span", "depth"),
    )
    return jax.shard_map(
        local,
        mesh=mesh,
        in_specs=placed,
        out_specs=(P("span", "depth", None), P(None, "span", "depth")),
        check_vma=False,
    )
```

time: 190 us -> 114 us (0.60)
  the two profiles are of different devices: /device:TPU:1 before, /device:TPU:25 now
where the time goes in v1:
time: 114 us
  starting transfers between devices  53.3 us (47%)
  Pallas kernels  28.9 us (25%)
  waiting for transfers between devices  23.8 us (21%)
  local copies, waits for them, and re-layouts  7.09 us (6%)
    ppermute x8, starting transfers between devices, swap(): return (lax.ppermute(even, axis, pairs), lax.ppermute(odd, axis, shifted))  32.3 us
    ppermute x8, waiting for transfers between devices, swap(): return (lax.ppermute(even, axis, pairs), lax.ppermute(odd, axis, shifted))  23.8 us
    pallas_call x1, Pallas kernels, local(): pl.pallas_call(sweeps_kernel, out_shape=(jax.ShapeDtypeStruct((DZ, CX, SB...  17.2 us
    all_to_all x1, starting transfers between devices, local(): lax.all_to_all(sent.reshape(SPAN * PER, 1, 128), 'span', split_axis=0, co...  11.6 us
    all_to_all x1, starting transfers between devices, local(): back = lax.all_to_all(flux, 'span', split_axis=0, concat_axis=0, tiled=True)  9.39 us
    unnamed x30, local copies, waits for them, and re-layouts  7.09 us
    pallas_call x1, Pallas kernels, local(): pl.pallas_call(edge_columns_kernel, out_shape=(columns, columns, rim, rim...  4.4 us
  transfers between devices with their start and end apart: 10, of which 5 were waited for; matrix products, arithmetic and copies ran while one was open for 0% of the time, Pallas kernels for 22%

profile of v1, /device:TPU:25, one launch (start us, length us, event | category | flops | bytes accessed | tf_op | source)
XLA Modules:
  0.0 113.9 jit_solution(5462839259235243375)
XLA Ops:
  0.6 0.0 copy-start.3
  0.6 0.9 copy-done.3
  1.6 0.9 copy-done.8
  2.5 0.7 copy-done.11
  3.2 0.7 copy-done.13
  3.9 0.7 copy-done.14
  4.6 0.8 pack.1
  5.4 0.0 copy-start.2
  5.4 1.0 copy-done.2
  6.3 11.6 %all-to-all-start = ((f32[2112,1,128]{2,1,0:T(1,128)}), f32[2112,1,128]{2,1,0:T(1,128)}, u32[]{:S(2)}, u32[]{:S(2)}) async-start(f32[2112,1,128]{2,1,0:T(1,128)} %bitcast.18), calls=%async_computation | async-start | bytes 2162688 | tf_op jit(solution)/shard_map/all_to_all | solution.py:313
  17.9 0.0 copy-done
  17.9 0.0 copy-done.1
  18.0 0.0 copy-start.4
  18.0 0.7 edge_rows.1
  18.7 1.3 %collective-permute-start = (f32[144,256]{1,0:T(8,128)S(1)}, f32[144,256]{1,0:T(8,128)S(1)}, u32[]{:S(2)}, u32[]{:S(2)}) collective-permute-start(f32[144,256]{1,0:T(8,128)S(1)} %get-tuple-element.22), channel_id=1, source_target_pairs={{0,4},{4,0},{8,12},{12,8},{16,20},{20,16},{24,28},{28,24},{32,36},... | collective-permute-start | bytes 442376 | tf_op jit(solution)/shard_map/ppermute | solution.py:298
  20.0 6.8 %collective-permute-start.1 = (f32[144,256]{1,0:T(8,128)S(1)}, f32[144,256]{1,0:T(8,128)S(1)}, u32[]{:S(2)}, u32[]{:S(2)}) collective-permute-start(f32[144,256]{1,0:T(8,128)S(1)} %get-tuple-element.23), channel_id=1, source_target_pairs={{4,8},{8,4},{12,16},{16,12},{20,24},{24,20},{28,32},{32,28},{36,40... | collective-permute-start | bytes 442376 | tf_op jit(solution)/shard_map/ppermute | solution.py:298
  26.8 2.2 %collective-permute-done.even_in = f32[144,256]{1,0:T(8,128)S(1)} collective-permute-done((f32[144,256]{1,0:T(8,128)S(1)}, f32[144,256]{1,0:T(8,128)S(1)}, u32[]{:S(2)}, u32[]{:S(2)}) %collective-permute-start) | collective-permute-done | bytes 147488 | tf_op jit(solution)/shard_map/ppermute | solution.py:298
  28.9 14.4 %collective-permute-done.1.odd_in = f32[144,256]{1,0:T(8,128)S(1)} collective-permute-done((f32[144,256]{1,0:T(8,128)S(1)}, f32[144,256]{1,0:T(8,128)S(1)}, u32[]{:S(2)}, u32[]{:S(2)}) %collective-permute-start.1) | collective-permute-done | bytes 147488 | tf_op jit(solution)/shard_map/ppermute | solution.py:298
  43.3 0.0 copy-done.4
  43.3 4.4 %edge_columns.1 = (f32[48,256]{1,0:T(8,128)S(1)}, f32[48,256]{1,0:T(8,128)S(1)}, f32[384,256]{1,0:T(8,128)S(1)}, f32[384,256]{1,0:T(8,128)S(1)}) custom-call(f32[1536,256]{1,0:T(8,128)S(1)} %bitcast.12, f32[1536,256]{1,0:T(8,128)S(1)} %bitcast.16, f32[144,256]{1,0:T(8,128)S(1)} %collective-permute-done.even_in, ...), custom_call_target="tpu_custom_call" | custom-call | tf_op jit(solution)/shard_map/edge_columns/pallas_call | solution.py:331
  47.7 2.1 %collective-permute-start.2 = (f32[48,256]{1,0:T(8,128)S(1)}, f32[48,256]{1,0:T(8,128)S(1)}, u32[]{:S(2)}, u32[]{:S(2)}) collective-permute-start(f32[48,256]{1,0:T(8,128)S(1)} %get-tuple-element.26), channel_id=1, source_target_pairs={{0,1},{1,0},{2,3},{3,2},{4,5},{5,4},{6,7},{7,6},{8,9},{9,8},{10,11... | collective-permute-start | bytes 147464 | tf_op jit(solution)/shard_map/ppermute | solution.py:298
  49.8 6.0 %collective-permute-start.3 = (f32[48,256]{1,0:T(8,128)S(1)}, f32[48,256]{1,0:T(8,128)S(1)}, u32[]{:S(2)}, u32[]{:S(2)}) collective-permute-start(f32[48,256]{1,0:T(8,128)S(1)} %get-tuple-element.27), channel_id=1, source_target_pairs={{1,2},{2,1},{5,6},{6,5},{9,10},{10,9},{13,14},{14,13},{17,18},{18,... | collective-permute-start | bytes 147464 | tf_op jit(solution)/shard_map/ppermute | solution.py:298
  55.9 0.0 collective-permute-done.2.even_in
  55.9 3.3 %collective-permute-done.3.odd_in = f32[48,256]{1,0:T(8,128)S(1)} collective-permute-done((f32[48,256]{1,0:T(8,128)S(1)}, f32[48,256]{1,0:T(8,128)S(1)}, u32[]{:S(2)}, u32[]{:S(2)}) %collective-permute-start.3) | collective-permute-done | bytes 49184 | tf_op jit(solution)/shard_map/ppermute | solution.py:298
  59.2 0.0 copy-done.12
  59.2 0.4 shell.1
  59.6 0.0 copy-start.6
  59.6 0.7 copy-done.6
  60.3 17.2 %sweeps.1 = (f32[48,32,256]{2,1,0:T(8,128)}, f32[3,40,384]{2,1,0:T(8,128)S(1)}) custom-call(f32[1536,256]{1,0:T(8,128)S(1)} %bitcast.13, f32[1536,256]{1,0:T(8,128)S(1)} %bitcast.17, f32[384,256]{1,0:T(8,128)S(1)} %get-tuple-element.24.die_rim, f32[384,256]{1,0:T(8,128)S(1)} %get-tuple-element.25.diff_rim, f32[48,256]{1,0:T(8,128)S(1)} %collective-permute-done.2.even_in, ...), custom_call_target="tpu_custom_call" | custom-call | flops 29491200 | bytes 7864320 | tf_op jit(solution)/shard_map/sweeps/pallas_call | solution.py:340
  77.5 0.7 copy-done.9
  78.2 0.0 all-to-all-done
  78.2 2.2 %owner.1 = (f32[1024,128]{1,0:T(8,128)S(1)}, f32[32,256]{1,0:T(8,128)S(1)}, f32[8,256]{1,0:T(8,128)S(1)}, f32[8,256]{1,0:T(8,128)S(1)}) custom-call(f32[2112,128]{1,0:T(8,128)} %bitcast.5.got_ref, f32[1536,256]{1,0:T(8,128)S(1)} %bitcast.14), custom_call_target="tpu_custom_call" | custom-call | tf_op jit(solution)/shard_map/owner/pallas_call | solution.py:371
  80.4 0.0 copy-start.5
  80.4 0.8 copy-done.5
  81.2 9.4 %all-to-all-start.1 = ((f32[64,16,128]{2,1,0:T(8,128)}), f32[64,16,128]{2,1,0:T(8,128)S(1)}, u32[]{:S(2)}, u32[]{:S(2)}) async-start(f32[64,16,128]{2,1,0:T(8,128)} %bitcast.22), calls=%async_computation.1 | async-start | bytes 1048576 | tf_op jit(solution)/shard_map/all_to_all | solution.py:385
  90.6 1.3 %collective-permute-start.4 = (f32[8,256]{1,0:T(8,128)S(1)}, f32[8,256]{1,0:T(8,128)S(1)}, u32[]{:S(2)}, u32[]{:S(2)}) collective-permute-start(f32[8,256]{1,0:T(8,128)S(1)} %get-tuple-element.37), channel_id=1, source_target_pairs={{0,4},{4,0},{8,12},{12,8},{16,20},{20,16},{24,28},{28,24},{32,36},... | collective-permute-start | bytes 24584 | tf_op jit(solution)/shard_map/ppermute | solution.py:298
  91.9 6.7 %collective-permute-start.5 = (f32[8,256]{1,0:T(8,128)S(1)}, f32[8,256]{1,0:T(8,128)S(1)}, u32[]{:S(2)}, u32[]{:S(2)}) collective-permute-start(f32[8,256]{1,0:T(8,128)S(1)} %get-tuple-element.38), channel_id=1, source_target_pairs={{4,8},{8,4},{12,16},{16,12},{20,24},{24,20},{28,32},{32,28},{36,40... | collective-permute-start | bytes 24584 | tf_op jit(solution)/shard_map/ppermute | solution.py:298
  98.5 0.0 collective-permute-done.4.even_in
  98.5 2.5 %collective-permute-done.5.odd_in = f32[8,256]{1,0:T(8,128)S(1)} collective-permute-done((f32[8,256]{1,0:T(8,128)S(1)}, f32[8,256]{1,0:T(8,128)S(1)}, u32[]{:S(2)}, u32[]{:S(2)}) %collective-permute-start.5) | collective-permute-done | bytes 8224 | tf_op jit(solution)/shard_map/ppermute | solution.py:298
  101.1 0.1 collective-permute-start.6
  101.2 8.0 %collective-permute-start.7 = (f32[40,128]{1,0:T(8,128)S(1)}, f32[40,128]{1,0:T(8,128)S(1)}, u32[]{:S(2)}, u32[]{:S(2)}) collective-permute-start(f32[40,128]{1,0:T(8,128)S(1)} %get-tuple-element.41), channel_id=1, source_target_pairs={{1,2},{2,1},{5,6},{6,5},{9,10},{10,9},{13,14},{14,13},{17,18},{18,... | collective-permute-start | bytes 61448 | tf_op jit(solution)/shard_map/ppermute | solution.py:298
  109.2 0.0 collective-permute-done.6.even_in
  109.2 1.4 %collective-permute-done.7.odd_in = f32[40,128]{1,0:T(8,128)S(1)} collective-permute-done((f32[40,128]{1,0:T(8,128)S(1)}, f32[40,128]{1,0:T(8,128)S(1)}, u32[]{:S(2)}, u32[]{:S(2)}) %collective-permute-start.7) | collective-permute-done | bytes 20512 | tf_op jit(solution)/shard_map/ppermute | solution.py:298
  110.7 0.0 copy-done.10
  110.7 1.9 %heat.1 = f32[48,32,256]{2,1,0:T(8,128)} custom-call(f32[48,32,256]{2,1,0:T(8,128)} %get-tuple-element.34.base_ref, f32[3,40,384]{2,1,0:T(8,128)S(1)} %copy-done.10, f32[40,256]{1,0:T(8,128)S(1)} %get-tuple-element.39.rows_ref, f32[40,128]{1,0:T(8,128)S(1)} %collective-permute-done.6.even_in, ...), custom_call_target="tpu_custom_call", output_to_operand_aliasing={{}: (0, {})} | custom-call | tf_op jit(solution)/shard_map/heat/pallas_call | solution.py:398
  112.6 0.0 all-to-all-done.1.flux_ref
  112.6 0.0 copy-done.7
  112.6 1.3 %sink.1 = f32[256,256]{1,0:T(8,128)} custom-call(f32[256,256]{1,0:T(8,128)S(1)} %get-tuple-element.30.base_ref, bf16[256,512]{1,0:T(8,128)(2,1)S(1)} %copy-done.7, f32[64,16,128]{2,1,0:T(8,128)S(1)} %all-to-all-done.1.flux_ref), custom_call_target="tpu_custom_call" | custom-call | tf_op jit(solution)/shard_map/sink/pallas_call | solution.py:408
  (11 shorter events, 0.0 us)
Async XLA Ops:
  0.6 1.0 copy-start.3
  1.6 0.9 copy-start.8
  2.5 0.7 copy-start.11
  3.2 0.7 copy-start.13
  3.9 0.7 copy-start.14
  4.6 13.4 %copy-start = (f32[48,32,256]{2,1,0:T(8,128)S(1)}, f32[48,32,256]{2,1,0:T(8,128)}, u32[]{:S(2)}) copy-start(f32[48,32,256]{2,1,0:T(8,128)} %param.9) | copy-start | bytes 4718596
  4.6 13.4 %copy-start.1 = (f32[48,32,256]{2,1,0:T(8,128)S(1)}, f32[48,32,256]{2,1,0:T(8,128)}, u32[]{:S(2)}) copy-start(f32[48,32,256]{2,1,0:T(8,128)} %param.10) | copy-start | bytes 4718596
  5.4 1.0 copy-start.2
  6.3 71.9 %all-to-all-start = ((f32[2112,1,128]{2,1,0:T(1,128)}), f32[2112,1,128]{2,1,0:T(1,128)}, u32[]{:S(2)}, u32[]{:S(2)}) async-start(f32[2112,1,128]{2,1,0:T(1,128)} %bitcast.18), calls=%async_computation | async-start | bytes 2162688 | tf_op jit(solution)/shard_map/all_to_all | solution.py:313
  18.0 25.3 %copy-start.4 = (f32[1,256,256]{2,1,0:T(8,128)S(1)}, f32[1,256,256]{2,1,0:T(8,128)}, u32[]{:S(2)}) copy-start(f32[1,256,256]{2,1,0:T(8,128)} %param.7) | copy-start | bytes 786436
  18.7 10.3 %collective-permute-start = (f32[144,256]{1,0:T(8,128)S(1)}, f32[144,256]{1,0:T(8,128)S(1)}, u32[]{:S(2)}, u32[]{:S(2)}) collective-permute-start(f32[144,256]{1,0:T(8,128)S(1)} %get-tuple-element.22), channel_id=1, source_target_pairs={{0,4},{4,0},{8,12},{12,8},{16,20},{20,16},{24,28},{28,24},{32,36},... | collective-permute-start | bytes 442376 | tf_op jit(solution)/shard_map/ppermute | solution.py:298
  20.0 39.2 %copy-start.12 = (s32[1,256,1]{1,2,0:T(1,128)S(1)}, s32[1,256,1]{1,2,0:T(1,128)}, u32[]{:S(2)}) copy-start(s32[1,256,1]{1,2,0:T(1,128)} %param.11) | copy-start | bytes 3076
  20.0 23.3 %collective-permute-start.1 = (f32[144,256]{1,0:T(8,128)S(1)}, f32[144,256]{1,0:T(8,128)S(1)}, u32[]{:S(2)}, u32[]{:S(2)}) collective-permute-start(f32[144,256]{1,0:T(8,128)S(1)} %get-tuple-element.23), channel_id=1, source_target_pairs={{4,8},{8,4},{12,16},{16,12},{20,24},{24,20},{28,32},{32,28},{36,40... | collective-permute-start | bytes 442376 | tf_op jit(solution)/shard_map/ppermute | solution.py:298
  47.7 8.2 %collective-permute-start.2 = (f32[48,256]{1,0:T(8,128)S(1)}, f32[48,256]{1,0:T(8,128)S(1)}, u32[]{:S(2)}, u32[]{:S(2)}) collective-permute-start(f32[48,256]{1,0:T(8,128)S(1)} %get-tuple-element.26), channel_id=1, source_target_pairs={{0,1},{1,0},{2,3},{3,2},{4,5},{5,4},{6,7},{7,6},{8,9},{9,8},{10,11... | collective-permute-start | bytes 147464 | tf_op jit(solution)/shard_map/ppermute | solution.py:298
  49.8 9.3 %collective-permute-start.3 = (f32[48,256]{1,0:T(8,128)S(1)}, f32[48,256]{1,0:T(8,128)S(1)}, u32[]{:S(2)}, u32[]{:S(2)}) collective-permute-start(f32[48,256]{1,0:T(8,128)S(1)} %get-tuple-element.27), channel_id=1, source_target_pairs={{1,2},{2,1},{5,6},{6,5},{9,10},{10,9},{13,14},{14,13},{17,18},{18,... | collective-permute-start | bytes 147464 | tf_op jit(solution)/shard_map/ppermute | solution.py:298
  59.6 0.7 copy-start.6
  77.5 0.7 copy-start.9
  78.2 32.5 %copy-start.10 = (f32[3,40,384]{2,1,0:T(8,128)S(1)}, f32[3,40,384]{2,1,0:T(8,128)}, u32[]{:S(2)}) copy-start(f32[3,40,384]{2,1,0:T(8,128)} %copy-done.9) | copy-start | bytes 552964
  80.4 0.8 copy-start.5
  81.2 31.4 %all-to-all-start.1 = ((f32[64,16,128]{2,1,0:T(8,128)}), f32[64,16,128]{2,1,0:T(8,128)S(1)}, u32[]{:S(2)}, u32[]{:S(2)}) async-start(f32[64,16,128]{2,1,0:T(8,128)} %bitcast.22), calls=%async_computation.1 | async-start | bytes 1048576 | tf_op jit(solution)/shard_map/all_to_all | solution.py:385
  90.6 7.9 %collective-permute-start.4 = (f32[8,256]{1,0:T(8,128)S(1)}, f32[8,256]{1,0:T(8,128)S(1)}, u32[]{:S(2)}, u32[]{:S(2)}) collective-permute-start(f32[8,256]{1,0:T(8,128)S(1)} %get-tuple-element.37), channel_id=1, source_target_pairs={{0,4},{4,0},{8,12},{12,8},{16,20},{20,16},{24,28},{28,24},{32,36},... | collective-permute-start | bytes 24584 | tf_op jit(solution)/shard_map/ppermute | solution.py:298
  91.9 9.2 %collective-permute-start.5 = (f32[8,256]{1,0:T(8,128)S(1)}, f32[8,256]{1,0:T(8,128)S(1)}, u32[]{:S(2)}, u32[]{:S(2)}) collective-permute-start(f32[8,256]{1,0:T(8,128)S(1)} %get-tuple-element.38), channel_id=1, source_target_pairs={{4,8},{8,4},{12,16},{16,12},{20,24},{24,20},{28,32},{32,28},{36,40... | collective-permute-start | bytes 24584 | tf_op jit(solution)/shard_map/ppermute | solution.py:298
  101.1 8.2 %collective-permute-start.6 = (f32[40,128]{1,0:T(8,128)S(1)}, f32[40,128]{1,0:T(8,128)S(1)}, u32[]{:S(2)}, u32[]{:S(2)}) collective-permute-start(f32[40,128]{1,0:T(8,128)S(1)} %get-tuple-element.40), channel_id=1, source_target_pairs={{0,1},{1,0},{2,3},{3,2},{4,5},{5,4},{6,7},{7,6},{8,9},{9,8},{10,11... | collective-permute-start | bytes 61448 | tf_op jit(solution)/shard_map/ppermute | solution.py:298
  101.2 9.5 %collective-permute-start.7 = (f32[40,128]{1,0:T(8,128)S(1)}, f32[40,128]{1,0:T(8,128)S(1)}, u32[]{:S(2)}, u32[]{:S(2)}) collective-permute-start(f32[40,128]{1,0:T(8,128)S(1)} %get-tuple-element.41), channel_id=1, source_target_pairs={{1,2},{2,1},{5,6},{6,5},{9,10},{10,9},{13,14},{14,13},{17,18},{18,... | collective-permute-start | bytes 61448 | tf_op jit(solution)/shard_map/ppermute | solution.py:298
  110.7 1.9 %copy-start.7 = (bf16[256,512]{1,0:T(8,128)(2,1)S(1)}, bf16[256,512]{1,0:T(8,128)(2,1)}, u32[]{:S(2)}) copy-start(bf16[256,512]{1,0:T(8,128)(2,1)} %copy-done.6) | copy-start | bytes 786436

commit v2 on v1

--- a/solution.py
+++ b/solution.py
@@ -22,7 +22,11 @@
 EX = CX + 8
 EY = SB + 128
 
+CHUNKS = 4
+
 VMEM = pl.BlockSpec(memory_space=pltpu.VMEM)
+HBM = pl.BlockSpec(memory_space=pltpu.HBM)
+ANY = pl.BlockSpec(memory_space=pl.ANY)
 
 
 def params(mib):
@@ -57,9 +61,29 @@
     return jnp.sum(jnp.where(eye, row, 0.0), axis=1, keepdims=True)
 
 
-def pack_kernel(routes_ref, tile_ref, closed_ref, temp_ref, gain_ref, out_ref):
+def pack_kernel(
+    routes_hbm, tile_hbm, closed_hbm, temp_hbm, gain_hbm, after_hbm, out_hbm,
+    routes_ref, tile_ref, closed_ref, temp_ref, gain_ref, out_ref, sems, out_sems,
+):
+    del after_hbm
+    loads = [
+        pltpu.make_async_copy(source, target, sems.at[n])
+        for n, (source, target) in enumerate(
+            (
+                (routes_hbm, routes_ref),
+                (tile_hbm, tile_ref),
+                (closed_hbm, closed_ref),
+                (temp_hbm, temp_ref),
+                (gain_hbm, gain_ref),
+            )
+        )
+    ]
+    for load in loads:
+        load.start()
     sub, lane = iota((NB, NB), 0), iota((NB, NB), 1)
     eye = sub == lane
+    for load in loads[:3]:
+        load.wait()
     target = routes_ref[...].astype(F32)
     same = as_column(target, eye) == target
     rank_row = jnp.sum(
@@ -71,7 +95,6 @@
     tile_col = as_column(tile_ref[...].astype(F32), eye)
     closed_col = as_column(closed_ref[...].astype(F32), eye)
     position = (target * CAP + rank_row).astype(jnp.int32)
-    put = jnp.where(iota((SLOTS, NB), 0) == position, 1.0, 0.0).astype(BF16)
     codes = lax.dot_general(
         jnp.where(iota((SPAN, NB), 0) == routes_ref[...], 1.0, 0.0).astype(BF16),
         jnp.where(iota((NB, 128), 1) == rank_col.astype(jnp.int32), tile_col, 0.0).astype(BF16),
@@ -79,27 +102,41 @@
         preferred_element_type=F32,
     )
     out_ref[pl.ds(4 * CAP, SPAN, stride=PER), :] = codes
-    temp = pick(put, temp_ref[...])
-    gain = pick(put, gain_ref[...] * closed_col)
-    for c, slots in enumerate((temp[:, :128], temp[:, 128:], gain[:, :128], gain[:, 128:])):
-        for t in range(SPAN):
-            out_ref[pl.ds(t * PER + c, CAP, stride=4), :] = slots[t * CAP : (t + 1) * CAP]
-
-
-def edge_rows_kernel(die_ref, diff_ref, even_ref, odd_ref):
+    for load in loads[3:]:
+        load.wait()
+    parts = split3(jnp.concatenate([temp_ref[...], gain_ref[...] * closed_col], axis=1))
+    chunk = SPAN // CHUNKS
+    stores = []
+    for g in range(CHUNKS):
+        first = g * chunk * CAP
+        put = jnp.where(iota((chunk * CAP, NB), 0) + first == position, 1.0, 0.0).astype(BF16)
+        slots = sum(jnp.dot(put, part, preferred_element_type=F32) for part in parts)
+        for c in range(4):
+            for t in range(chunk):
+                out_ref[pl.ds((g * chunk + t) * PER + c, CAP, stride=4), :] = slots[
+                    t * CAP : (t + 1) * CAP, c * 128 : (c + 1) * 128
+                ]
+        rows = pl.ds(g * chunk * PER, chunk * PER)
+        stores.append(pltpu.make_async_copy(out_ref.at[rows], out_hbm.at[rows], out_sems.at[g]))
+        stores[-1].start()
+    for store in stores:
+        store.wait()
+
+
+def edge_rows_kernel(die_first, die_last, diff_first, diff_last, even_ref, odd_ref):
     is_even = lax.rem(lax.axis_index("span"), 2) == 0
 
     def layer(z, carry):
-        for n, (ref, low, high) in enumerate(
-            ((die_ref, 0, CX - 2), (die_ref, 1, CX - 1), (diff_ref, 0, CX - 1))
+        for n, (first, low, last, high) in enumerate(
+            ((die_first, 0, die_last, 6), (die_first, 1, die_last, 7), (diff_first, 0, diff_last, 7))
         ):
-            first = ref[pl.ds(z * CX + low, 1), :]
-            last = ref[pl.ds(z * CX + high, 1), :]
-            even_ref[pl.ds(n * DZ + z, 1), :] = jnp.where(is_even, last, first)
-            odd_ref[pl.ds(n * DZ + z, 1), :] = jnp.where(is_even, first, last)
+            top = first[z, low : low + 1, :]
+            bottom = last[z, high : high + 1, :]
+            even_ref[pl.ds(n * DZ + z, 1), :] = jnp.where(is_even, bottom, top)
+            odd_ref[pl.ds(n * DZ + z, 1), :] = jnp.where(is_even, top, bottom)
         return carry
 
-    lax.fori_loop(0, DZ, layer, 0, unroll=4)
+    lax.fori_loop(0, DZ, layer, 0, unroll=8)
 
 
 def edge_columns_kernel(
@@ -136,7 +173,7 @@
         return v_left, v_right, k_left, k_right
 
     none = jnp.zeros((EX, 128), F32)
-    v_left, v_right, k_left, k_right = lax.fori_loop(0, DZ, add_layer, (none,) * 4)
+    v_left, v_right, k_left, k_right = lax.fori_loop(0, DZ, add_layer, (none,) * 4, unroll=8)
     even_ref[:EX, :128] = jnp.where(depth_even, v_right, v_left)
     even_ref[:EX, 128:] = jnp.where(depth_even, k_right, k_left)
     odd_ref[:EX, :128] = jnp.where(depth_even, v_left, v_right)
@@ -177,7 +214,7 @@
         rate[z, :, SB:] = jnp.where(lane < 1, k_right, jnp.where(lane >= 127, k_left, 0.0))
         return carry
 
-    lax.fori_loop(0, DZ, fill, 0)
+    lax.fori_loop(0, DZ, fill, 0, unroll=8)
 
     def first(z, carry):
         v = field[z + 1]
@@ -185,7 +222,7 @@
         later[z + 1] = v + rate[z] * (across(p) - 16.0 * v)
         return carry
 
-    lax.fori_loop(0, DZ, first, 0)
+    lax.fori_loop(0, DZ, first, 0, unroll=4)
 
     def second(z, carry):
         p = 2.0 * later[z + 1] + (later[z] + later[z + 2])
@@ -194,7 +231,7 @@
         out_ref[z] = v + rate[z, :CX, :SB] * (q - 16.0 * v)
         return carry
 
-    lax.fori_loop(0, DZ, second, 0)
+    lax.fori_loop(0, DZ, second, 0, unroll=4)
     top_ref[...] = rate[0:3]
 
 
@@ -302,28 +339,43 @@
     temp, gain = shell_temp[0], contact_gain[0]
     target = routes.reshape(1, NB)
     die, diff = die_temp.reshape(DZ * CX, SB), diffusivity.reshape(DZ * CX, SB)
-    sent = pl.pallas_call(
-        pack_kernel,
-        out_shape=jax.ShapeDtypeStruct((SPAN * PER, 128), F32),
-        in_specs=[VMEM] * 5,
-        out_specs=VMEM,
-        compiler_params=params(16),
-        name="pack",
-    )(target, tile_rows, closed, temp, gain)
-    got = lax.all_to_all(
-        sent.reshape(SPAN * PER, 1, 128), "span", split_axis=0, concat_axis=0, tiled=True
-    ).reshape(SPAN * PER, 128)
-
     rows = jax.ShapeDtypeStruct((3 * DZ, SB), F32)
     even, odd = pl.pallas_call(
         edge_rows_kernel,
         out_shape=(rows, rows),
-        in_specs=[VMEM] * 2,
+        grid=(1,),
+        in_specs=[
+            pl.BlockSpec((DZ, 8, SB), lambda i: (0, 0, 0)),
+            pl.BlockSpec((DZ, 8, SB), lambda i: (0, CX // 8 - 1, 0)),
+        ]
+        * 2,
         out_specs=(VMEM,) * 2,
-        compiler_params=params(16),
+        compiler_params=params(60),
         name="edge_rows",
-    )(die, diff)
+    )(die_temp, die_temp, diffusivity, diffusivity)
+    sent = pl.pallas_call(
+        pack_kernel,
+        out_shape=jax.ShapeDtypeStruct((SPAN * PER, 128), F32),
+        in_specs=[HBM] * 5 + [ANY],
+        out_specs=HBM,
+        scratch_shapes=[
+            pltpu.VMEM((1, NB), jnp.int32),
+            pltpu.VMEM((1, NB), jnp.int32),
+            pltpu.VMEM((1, NB), jnp.int32),
+            pltpu.VMEM((NB, SB), F32),
+            pltpu.VMEM((NB, SB), F32),
+            pltpu.VMEM((SPAN * PER, 128), F32),
+            pltpu.SemaphoreType.DMA((5,)),
+            pltpu.SemaphoreType.DMA((CHUNKS,)),
+        ],
+        compiler_params=params(60),
+        cost_estimate=cost(6 * SLOTS * NB * 2 * SB, 4 * 2**20),
+        name="pack",
+    )(target, tile_rows, closed, temp, gain, even)
     even, odd = swap(even, odd, "span")
+    got = lax.all_to_all(
+        sent.reshape(SPAN * PER, 1, 128), "span", split_axis=0, concat_axis=0, tiled=True
+    ).reshape(SPAN * PER, 128)
     columns, rim = (
         jax.ShapeDtypeStruct((EX + 8, SB), F32),
         jax.ShapeDtypeStruct((DZ * 8, SB), F32),
@@ -334,6 +386,7 @@
         in_specs=[VMEM] * 5,
         out_specs=(VMEM,) * 4,
         compiler_params=params(16),
+        cost_estimate=cost(10**12, 2**32),
         name="edge_columns",
     )(die, diff, even, odd, temp)
     even, odd = swap(even, odd, "depth")
@@ -350,7 +403,7 @@
             pltpu.VMEM((DZ + 2, EX, EY), F32),
             pltpu.VMEM((DZ, EX, EY), F32),
         ],
-        compiler_params=params(28),
+        compiler_params=params(20),
         cost_estimate=cost(40 * DZ * EX * EY, 5 * DZ * CX * SB * 4),
         name="sweeps",
     )(die, diff, die_rim, diff_rim, even, odd)
@@ -379,7 +432,7 @@
         grid=(1,),
         in_specs=[VMEM, pl.BlockSpec((CX, SB), lambda i: (0, 0))],
         out_specs=(VMEM,) * 4,
-        compiler_params=params(16),
+        compiler_params=params(60),
         name="owner",
     )(got, die)
     back = lax.all_to_all(flux, "span", split_axis=0, concat_axis=0, tiled=True)
@@ -391,6 +444,7 @@
         in_specs=[VMEM] * 3,
         out_specs=(VMEM,) * 3,
         compiler_params=params(8),
+        cost_estimate=cost(10**12, 2**32),
         name="heat_edges",
     )(heat, even, odd)
     even, odd = swap(even, odd, "depth")

time: 114 us -> 90.3 us (0.79)
  the two profiles are of different devices: /device:TPU:25 before, /device:TPU:1 now
where the time goes in v2:
time: 90.3 us; the launch traced here: 89.8 us
  starting transfers between devices  42.2 us (47%)
  Pallas kernels  22.9 us (25%)
  waiting for transfers between devices  21.6 us (24%)
  local copies, waits for them, and re-layouts  2.18 us (2%)
    ppermute x8, waiting for transfers between devices, swap(): return (lax.ppermute(even, axis, pairs), lax.ppermute(odd, axis, shifted))  19.9 us
    ppermute x8, starting transfers between devices, swap(): return (lax.ppermute(even, axis, pairs), lax.ppermute(odd, axis, shifted))  17.5 us
    all_to_all x1, starting transfers between devices, local(): lax.all_to_all(sent.reshape(SPAN * PER, 1, 128), 'span', split_axis=0, co...  12.5 us
    all_to_all x1, starting transfers between devices, local(): back = lax.all_to_all(flux, 'span', split_axis=0, concat_axis=0, tiled=True)  12.2 us
    pallas_call x1, Pallas kernels, local(): pl.pallas_call(sweeps_kernel, out_shape=(jax.ShapeDtypeStruct((DZ, CX, SB...  8.06 us
    pallas_call x1, Pallas kernels, local(): pl.pallas_call(owner_kernel, out_shape=(jax.ShapeDtypeStruct((2 * SLOTS,...  2.74 us
    pallas_call x1, Pallas kernels, local(): pl.pallas_call(pack_kernel, out_shape=jax.ShapeDtypeStruct((SPAN * PER, 1...  2.64 us
    pallas_call x1, Pallas kernels, local(): pl.pallas_call(edge_rows_kernel, out_shape=(rows, rows), grid=(1,), in_sp...  2.44 us
  transfers between devices with their start and end apart: 10, of which 3 were waited for; matrix products, arithmetic and copies ran while one was open for 0% of the time, Pallas kernels for 17%

profile of v2, /device:TPU:1, one launch (start us, length us, event | category | flops | bytes accessed | tf_op | source)
XLA Modules:
  0.0 89.8 jit_solution(9717238357643197201)
XLA Ops:
  0.6 2.4 %edge_rows.1 = (f32[144,256]{1,0:T(8,128)}, f32[144,256]{1,0:T(8,128)}) custom-call(f32[48,32,256]{2,1,0:T(8,128)} %die_last.1, f32[48,32,256]{2,1,0:T(8,128)} %die_last.1, f32[48,32,256]{2,1,0:T(8,128)} %diff_last.1, f32[48,32,256]{2,1,0:T(8,128)} %diff_last.1), custom_call_target="tpu_custom_call" | custom-call | tf_op jit(solution)/shard_map/edge_rows/pallas_call | solution.py:343
  3.1 2.0 %collective-permute-start = (f32[144,256]{1,0:T(8,128)}, f32[144,256]{1,0:T(8,128)S(1)}, u32[]{:S(2)}, u32[]{:S(2)}) collective-permute-start(f32[144,256]{1,0:T(8,128)} %get-tuple-element.22.after_hbm), channel_id=1, source_target_pairs={{0,4},{4,0},{8,12},{12,8},{16,20},{20,16},{24,28},{28,24},{32,36},... | collective-permute-start | bytes 442376 | tf_op jit(solution)/shard_map/ppermute | solution.py:335
  5.1 1.3 %collective-permute-start.1 = (f32[144,256]{1,0:T(8,128)}, f32[144,256]{1,0:T(8,128)}, u32[]{:S(2)}, u32[]{:S(2)}) collective-permute-start(f32[144,256]{1,0:T(8,128)} %get-tuple-element.23), channel_id=1, source_target_pairs={{4,8},{8,4},{12,16},{16,12},{20,24},{24,20},{28,32},{32,28},{36,40... | collective-permute-start | bytes 442376 | tf_op jit(solution)/shard_map/ppermute | solution.py:335
  6.4 0.0 copy-start
  6.4 0.0 copy-start.1
  6.4 0.0 copy-start.2
  6.4 2.6 %pack.1 = f32[2112,128]{1,0:T(8,128)} custom-call(s32[1,256]{1,0:T(1,128)} %bitcast.19, s32[1,256]{1,0:T(1,128)} %tile_hbm.1, s32[1,256]{1,0:T(1,128)} %closed_hbm.1, f32[256,256]{1,0:T(8,128)} %bitcast.16, f32[256,256]{1,0:T(8,128)} %bitcast.24, f32[144,256]{1,0:T(8,128)} %get-tuple-element.22.after_hbm), custom_call_target="tpu_custom_call" | custom-call | flops 402653184 | bytes 4194304 | tf_op jit(solution)/shard_map/pack/pallas_call | solution.py:356
  9.1 12.5 %all-to-all-start = ((f32[2112,1,128]{2,1,0:T(1,128)}), f32[2112,1,128]{2,1,0:T(1,128)}, u32[]{:S(2)}, u32[]{:S(2)}) async-start(f32[2112,1,128]{2,1,0:T(1,128)} %bitcast.21), calls=%async_computation | async-start | bytes 2162688 | tf_op jit(solution)/shard_map/all_to_all | solution.py:376
  21.6 0.0 collective-permute-done.even_in
  21.6 0.0 collective-permute-done.1.odd_in
  21.6 0.0 copy-done
  21.6 0.0 copy-done.1
  21.6 0.0 copy-done.2
  21.7 0.0 copy-start.7
  21.7 2.4 %edge_columns.1 = (f32[48,256]{1,0:T(8,128)S(1)}, f32[48,256]{1,0:T(8,128)S(1)}, f32[384,256]{1,0:T(8,128)S(1)}, f32[384,256]{1,0:T(8,128)S(1)}) custom-call(f32[1536,256]{1,0:T(8,128)S(1)} %bitcast.12, f32[1536,256]{1,0:T(8,128)S(1)} %bitcast.14, f32[144,256]{1,0:T(8,128)S(1)} %collective-permute-done.even_in, f32[144,256]{1,0:T(8,128)} %collective-permute-done.1.odd_in, ...), custom_call_target="tpu_custom_call" | custom-call | flops 999999995904 | bytes 4294967296 | tf_op jit(solution)/shard_map/edge_columns/pallas_call | solution.py:383
  24.1 1.6 %collective-permute-start.2 = (f32[48,256]{1,0:T(8,128)S(1)}, f32[48,256]{1,0:T(8,128)S(1)}, u32[]{:S(2)}, u32[]{:S(2)}) collective-permute-start(f32[48,256]{1,0:T(8,128)S(1)} %get-tuple-element.26), channel_id=1, source_target_pairs={{0,1},{1,0},{2,3},{3,2},{4,5},{5,4},{6,7},{7,6},{8,9},{9,8},{10,11... | collective-permute-start | bytes 147464 | tf_op jit(solution)/shard_map/ppermute | solution.py:335
  25.7 8.1 %collective-permute-start.3 = (f32[48,256]{1,0:T(8,128)S(1)}, f32[48,256]{1,0:T(8,128)S(1)}, u32[]{:S(2)}, u32[]{:S(2)}) collective-permute-start(f32[48,256]{1,0:T(8,128)S(1)} %get-tuple-element.27), channel_id=1, source_target_pairs={{1,2},{2,1},{5,6},{6,5},{9,10},{10,9},{13,14},{14,13},{17,18},{18,... | collective-permute-start | bytes 147464 | tf_op jit(solution)/shard_map/ppermute | solution.py:335
  33.7 0.0 collective-permute-done.2.even_in
  33.7 13.4 %collective-permute-done.3.odd_in = f32[48,256]{1,0:T(8,128)S(1)} collective-permute-done((f32[48,256]{1,0:T(8,128)S(1)}, f32[48,256]{1,0:T(8,128)S(1)}, u32[]{:S(2)}, u32[]{:S(2)}) %collective-permute-start.3) | collective-permute-done | bytes 49184 | tf_op jit(solution)/shard_map/ppermute | solution.py:335
  47.1 0.0 copy-done.7
  47.1 0.4 shell.1
  47.6 0.0 copy-start.3
  47.6 0.7 copy-done.3
  48.3 0.0 copy-start.5
  48.3 0.7 copy-done.5
  49.0 8.1 %sweeps.1 = (f32[48,32,256]{2,1,0:T(8,128)}, f32[3,40,384]{2,1,0:T(8,128)S(1)}) custom-call(f32[1536,256]{1,0:T(8,128)S(1)} %bitcast.13, f32[1536,256]{1,0:T(8,128)S(1)} %bitcast.15, f32[384,256]{1,0:T(8,128)S(1)} %get-tuple-element.24.die_rim, f32[384,256]{1,0:T(8,128)S(1)} %get-tuple-element.25.diff_rim, f32[48,256]{1,0:T(8,128)S(1)} %collective-permute-done.2.even_in, ...), custom_call_target="tpu_custom_call" | custom-call | flops 29491200 | bytes 7864320 | tf_op jit(solution)/shard_map/sweeps/pallas_call | solution.py:393
  57.1 0.0 all-to-all-done
  57.1 2.7 %owner.1 = (f32[1024,128]{1,0:T(8,128)}, f32[32,256]{1,0:T(8,128)}, f32[8,256]{1,0:T(8,128)}, f32[8,256]{1,0:T(8,128)}) custom-call(f32[2112,128]{1,0:T(8,128)} %bitcast.5.got_ref, f32[1536,256]{1,0:T(8,128)} %bitcast.11), custom_call_target="tpu_custom_call" | custom-call | tf_op jit(solution)/shard_map/owner/pallas_call | solution.py:424
  59.8 1.1 %collective-permute-start.4 = (f32[8,256]{1,0:T(8,128)}, f32[8,256]{1,0:T(8,128)S(1)}, u32[]{:S(2)}, u32[]{:S(2)}) collective-permute-start(f32[8,256]{1,0:T(8,128)} %get-tuple-element.37), channel_id=1, source_target_pairs={{0,4},{4,0},{8,12},{12,8},{16,20},{20,16},{24,28},{28,24},{32,36},... | collective-permute-start | bytes 24584 | tf_op jit(solution)/shard_map/ppermute | solution.py:335
  60.9 0.6 collective-permute-start.5
  61.6 12.2 %all-to-all-start.1 = ((f32[64,16,128]{2,1,0:T(8,128)}), f32[64,16,128]{2,1,0:T(8,128)}, u32[]{:S(2)}, u32[]{:S(2)}) async-start(f32[64,16,128]{2,1,0:T(8,128)} %bitcast.22), calls=%async_computation.1 | async-start | bytes 1048576 | tf_op jit(solution)/shard_map/all_to_all | solution.py:438
  73.8 0.0 collective-permute-done.4.even_in
  73.8 0.0 collective-permute-done.5.odd_in
  73.8 0.0 copy-start.8
  73.9 0.7 copy-done.8
  74.6 0.1 collective-permute-start.6
  74.7 2.6 %collective-permute-start.7 = (f32[40,128]{1,0:T(8,128)S(1)}, f32[40,128]{1,0:T(8,128)S(1)}, u32[]{:S(2)}, u32[]{:S(2)}) collective-permute-start(f32[40,128]{1,0:T(8,128)S(1)} %get-tuple-element.41), channel_id=1, source_target_pairs={{1,2},{2,1},{5,6},{6,5},{9,10},{10,9},{13,14},{14,13},{17,18},{18,... | collective-permute-start | bytes 61448 | tf_op jit(solution)/shard_map/ppermute | solution.py:335
  77.3 0.0 collective-permute-done.6.even_in
  77.3 6.5 %collective-permute-done.7.odd_in = f32[40,128]{1,0:T(8,128)S(1)} collective-permute-done((f32[40,128]{1,0:T(8,128)S(1)}, f32[40,128]{1,0:T(8,128)S(1)}, u32[]{:S(2)}, u32[]{:S(2)}) %collective-permute-start.7) | collective-permute-done | bytes 20512 | tf_op jit(solution)/shard_map/ppermute | solution.py:335
  83.8 0.0 copy-start.4
  83.8 0.0 copy-start.6
  83.8 1.9 %heat.1 = f32[48,32,256]{2,1,0:T(8,128)} custom-call(f32[48,32,256]{2,1,0:T(8,128)} %get-tuple-element.34.base_ref, f32[3,40,384]{2,1,0:T(8,128)S(1)} %get-tuple-element.35.rate_ref, f32[40,256]{1,0:T(8,128)S(1)} %get-tuple-element.39.rows_ref, f32[40,128]{1,0:T(8,128)S(1)} %collective-permute-done.6.even_in, ...), custom_call_target="tpu_custom_call", output_to_operand_aliasing={{}: (0, {})} | custom-call | tf_op jit(solution)/shard_map/heat/pallas_call | solution.py:452
  85.6 1.8 %all-to-all-done.1.flux_ref = f32[64,16,128]{2,1,0:T(8,128)} async-done(((f32[64,16,128]{2,1,0:T(8,128)}), f32[64,16,128]{2,1,0:T(8,128)}, u32[]{:S(2)}, u32[]{:S(2)}) %all-to-all-start.1) | async-done | bytes 524320 | tf_op jit(solution)/shard_map/all_to_all | solution.py:438
  87.4 0.0 copy-done.4
  87.4 0.0 copy-done.6
  87.4 2.3 %sink.1 = f32[256,256]{1,0:T(8,128)} custom-call(f32[256,256]{1,0:T(8,128)S(1)} %copy-done.4, bf16[256,512]{1,0:T(8,128)(2,1)S(1)} %copy-done.6, f32[64,16,128]{2,1,0:T(8,128)} %all-to-all-done.1.flux_ref), custom_call_target="tpu_custom_call" | custom-call | tf_op jit(solution)/shard_map/sink/pallas_call | solution.py:462
  (1 shorter events, 0.0 us)
Async XLA Ops:
  3.1 18.5 %collective-permute-start = (f32[144,256]{1,0:T(8,128)}, f32[144,256]{1,0:T(8,128)S(1)}, u32[]{:S(2)}, u32[]{:S(2)}) collective-permute-start(f32[144,256]{1,0:T(8,128)} %get-tuple-element.22.after_hbm), channel_id=1, source_target_pairs={{0,4},{4,0},{8,12},{12,8},{16,20},{20,16},{24,28},{28,24},{32,36},... | collective-permute-start | bytes 442376 | tf_op jit(solution)/shard_map/ppermute | solution.py:335
  5.1 16.5 %collective-permute-start.1 = (f32[144,256]{1,0:T(8,128)}, f32[144,256]{1,0:T(8,128)}, u32[]{:S(2)}, u32[]{:S(2)}) collective-permute-start(f32[144,256]{1,0:T(8,128)} %get-tuple-element.23), channel_id=1, source_target_pairs={{4,8},{8,4},{12,16},{16,12},{20,24},{24,20},{28,32},{32,28},{36,40... | collective-permute-start | bytes 442376 | tf_op jit(solution)/shard_map/ppermute | solution.py:335
  6.4 15.2 %copy-start = (f32[48,32,256]{2,1,0:T(8,128)S(1)}, f32[48,32,256]{2,1,0:T(8,128)}, u32[]{:S(2)}) copy-start(f32[48,32,256]{2,1,0:T(8,128)} %die_last.1) | copy-start | bytes 4718596
  6.4 15.2 %copy-start.1 = (f32[48,32,256]{2,1,0:T(8,128)S(1)}, f32[48,32,256]{2,1,0:T(8,128)}, u32[]{:S(2)}) copy-start(f32[48,32,256]{2,1,0:T(8,128)} %diff_last.1) | copy-start | bytes 4718596
  6.4 15.2 %copy-start.2 = (f32[1,256,256]{2,1,0:T(8,128)S(1)}, f32[1,256,256]{2,1,0:T(8,128)}, u32[]{:S(2)}) copy-start(f32[1,256,256]{2,1,0:T(8,128)} %param.7) | copy-start | bytes 786436
  9.1 48.0 %all-to-all-start = ((f32[2112,1,128]{2,1,0:T(1,128)}), f32[2112,1,128]{2,1,0:T(1,128)}, u32[]{:S(2)}, u32[]{:S(2)}) async-start(f32[2112,1,128]{2,1,0:T(1,128)} %bitcast.21), calls=%async_computation | async-start | bytes 2162688 | tf_op jit(solution)/shard_map/all_to_all | solution.py:376
  21.7 25.5 %copy-start.7 = (s32[1,256,1]{1,2,0:T(1,128)S(1)}, s32[1,256,1]{1,2,0:T(1,128)}, u32[]{:S(2)}) copy-start(s32[1,256,1]{1,2,0:T(1,128)} %param.11) | copy-start | bytes 3076
  24.1 9.7 %collective-permute-start.2 = (f32[48,256]{1,0:T(8,128)S(1)}, f32[48,256]{1,0:T(8,128)S(1)}, u32[]{:S(2)}, u32[]{:S(2)}) collective-permute-start(f32[48,256]{1,0:T(8,128)S(1)} %get-tuple-element.26), channel_id=1, source_target_pairs={{0,1},{1,0},{2,3},{3,2},{4,5},{5,4},{6,7},{7,6},{8,9},{9,8},{10,11... | collective-permute-start | bytes 147464 | tf_op jit(solution)/shard_map/ppermute | solution.py:335
  25.7 21.5 %collective-permute-start.3 = (f32[48,256]{1,0:T(8,128)S(1)}, f32[48,256]{1,0:T(8,128)S(1)}, u32[]{:S(2)}, u32[]{:S(2)}) collective-permute-start(f32[48,256]{1,0:T(8,128)S(1)} %get-tuple-element.27), channel_id=1, source_target_pairs={{1,2},{2,1},{5,6},{6,5},{9,10},{10,9},{13,14},{14,13},{17,18},{18,... | collective-permute-start | bytes 147464 | tf_op jit(solution)/shard_map/ppermute | solution.py:335
  47.6 0.7 copy-start.3
  48.3 0.7 copy-start.5
  59.8 14.0 %collective-permute-start.4 = (f32[8,256]{1,0:T(8,128)}, f32[8,256]{1,0:T(8,128)S(1)}, u32[]{:S(2)}, u32[]{:S(2)}) collective-permute-start(f32[8,256]{1,0:T(8,128)} %get-tuple-element.37), channel_id=1, source_target_pairs={{0,4},{4,0},{8,12},{12,8},{16,20},{20,16},{24,28},{28,24},{32,36},... | collective-permute-start | bytes 24584 | tf_op jit(solution)/shard_map/ppermute | solution.py:335
  60.9 12.9 %collective-permute-start.5 = (f32[8,256]{1,0:T(8,128)}, f32[8,256]{1,0:T(8,128)S(1)}, u32[]{:S(2)}, u32[]{:S(2)}) collective-permute-start(f32[8,256]{1,0:T(8,128)} %get-tuple-element.38), channel_id=1, source_target_pairs={{4,8},{8,4},{12,16},{16,12},{20,24},{24,20},{28,32},{32,28},{36,40... | collective-permute-start | bytes 24584 | tf_op jit(solution)/shard_map/ppermute | solution.py:335
  61.6 25.8 %all-to-all-start.1 = ((f32[64,16,128]{2,1,0:T(8,128)}), f32[64,16,128]{2,1,0:T(8,128)}, u32[]{:S(2)}, u32[]{:S(2)}) async-start(f32[64,16,128]{2,1,0:T(8,128)} %bitcast.22), calls=%async_computation.1 | async-start | bytes 1048576 | tf_op jit(solution)/shard_map/all_to_all | solution.py:438
  73.8 0.8 copy-start.8
  74.6 2.7 %collective-permute-start.6 = (f32[40,128]{1,0:T(8,128)S(1)}, f32[40,128]{1,0:T(8,128)S(1)}, u32[]{:S(2)}, u32[]{:S(2)}) collective-permute-start(f32[40,128]{1,0:T(8,128)S(1)} %get-tuple-element.40), channel_id=1, source_target_pairs={{0,1},{1,0},{2,3},{3,2},{4,5},{5,4},{6,7},{7,6},{8,9},{9,8},{10,11... | collective-permute-start | bytes 61448 | tf_op jit(solution)/shard_map/ppermute | solution.py:335
  74.7 9.0 %collective-permute-start.7 = (f32[40,128]{1,0:T(8,128)S(1)}, f32[40,128]{1,0:T(8,128)S(1)}, u32[]{:S(2)}, u32[]{:S(2)}) collective-permute-start(f32[40,128]{1,0:T(8,128)S(1)} %get-tuple-element.41), channel_id=1, source_target_pairs={{1,2},{2,1},{5,6},{6,5},{9,10},{10,9},{13,14},{14,13},{17,18},{18,... | collective-permute-start | bytes 61448 | tf_op jit(solution)/shard_map/ppermute | solution.py:335
  83.8 3.7 %copy-start.4 = (f32[256,256]{1,0:T(8,128)S(1)}, f32[256,256]{1,0:T(8,128)}, u32[]{:S(2)}) copy-start(f32[256,256]{1,0:T(8,128)} %copy-done.3) | copy-start | bytes 786436
  83.8 3.7 %copy-start.6 = (bf16[256,512]{1,0:T(8,128)(2,1)S(1)}, bf16[256,512]{1,0:T(8,128)(2,1)}, u32[]{:S(2)}) copy-start(bf16[256,512]{1,0:T(8,128)(2,1)} %copy-done.5) | copy-start | bytes 786436

commit v3 on v2

v3 whole, which is shorter than its diff:
```python
import jax
import jax.numpy as jnp
from jax import lax
from jax.experimental import pallas as pl
from jax.experimental.pallas import tpu as pltpu
from jax.sharding import PartitionSpec as P

SHELL_RATE = 0.15
SHELL_SINK = 0.5
FACE_GAIN = 0.5
F32 = jnp.float32
BF16 = jnp.bfloat16

NB = 256
SB = 256
CX = 32
DZ = 48
CAP = 8
SPAN = 64
SLOTS = SPAN * CAP
PER = 4 * CAP + 1
EX = CX + 8
EY = SB + 128

CHUNKS = 4
UNROLL = 3
GROUP = 4

VMEM = pl.BlockSpec(memory_space=pltpu.VMEM)
HBM = pl.BlockSpec(memory_space=pltpu.HBM)
ANY = pl.BlockSpec(memory_space=pl.ANY)


def whole(*shape):
    return pl.BlockSpec(shape, lambda i: (0,) * len(shape))


def params(mib):
    return pltpu.CompilerParams(vmem_limit_bytes=mib * 2**20)


def cost(flops, moved):
    return pl.CostEstimate(flops=flops, bytes_accessed=moved, transcendentals=0)


def split(x):
    high = x.astype(BF16)
    return high, (x - high.astype(F32)).astype(BF16)


def pick(onehot, x, dims=(((1,), (0,)), ((), ()))):
    total = None
    for part in split(x):
        term = lax.dot_general(onehot, part, dims, preferred_element_type=F32)
        total = term if total is None else total + term
    return total


def iota(shape, dim):
    return lax.broadcasted_iota(jnp.int32, shape, dim)


def as_column(row, eye):
    return jnp.sum(jnp.where(eye, row, 0.0), axis=1, keepdims=True)


def pack_kernel(
    routes_hbm, tile_hbm, closed_hbm, temp_hbm, gain_hbm, out_hbm,
    routes_ref, tile_ref, closed_ref, temp_ref, gain_ref, out_ref, sems, out_sems,
):
    loads = [
        pltpu.make_async_copy(source, target, sems.at[n])
        for n, (source, target) in enumerate(
            (
                (routes_hbm, routes_ref),
                (tile_hbm, tile_ref),
                (closed_hbm, closed_ref),
                (temp_hbm, temp_ref),
                (gain_hbm, gain_ref),
            )
        )
    ]
    for load in loads:
        load.start()
    sub, lane = iota((NB, NB), 0), iota((NB, NB), 1)
    eye = sub == lane
    for load in loads[:3]:
        load.wait()
    target = routes_ref[...].astype(F32)
    same = as_column(target, eye) == target
    rank_row = jnp.sum(
        jnp.where(jnp.logical_and(same, sub < lane), 1.0, 0.0), axis=0, keepdims=True
    )
    rank_col = jnp.sum(
        jnp.where(jnp.logical_and(same, lane < sub), 1.0, 0.0), axis=1, keepdims=True
    )
    tile_col = as_column(tile_ref[...].astype(F32), eye)
    closed_col = as_column(closed_ref[...].astype(F32), eye)
    position = (target * CAP + rank_row).astype(jnp.int32)
    codes = lax.dot_general(
        jnp.where(iota((SPAN, NB), 0) == routes_ref[...], 1.0, 0.0).astype(BF16),
        jnp.where(iota((NB, 128), 1) == rank_col.astype(jnp.int32), tile_col, 0.0).astype(BF16),
        (((1,), (0,)), ((), ())),
        preferred_element_type=F32,
    )
    out_ref[pl.ds(4 * CAP, SPAN, stride=PER), :] = codes
    for load in loads[3:]:
        load.wait()
    parts = split(jnp.concatenate([temp_ref[...], gain_ref[...] * closed_col], axis=1))
    chunk = SPAN // CHUNKS
    stores = []
    for g in range(CHUNKS):
        first = g * chunk * CAP
        put = jnp.where(iota((chunk * CAP, NB), 0) + first == position, 1.0, 0.0).astype(BF16)
        slots = sum(jnp.dot(put, part, preferred_element_type=F32) for part in parts)
        for c in range(4):
            for t in range(chunk):
                out_ref[pl.ds((g * chunk + t) * PER + c, CAP, stride=4), :] = slots[
                    t * CAP : (t + 1) * CAP, c * 128 : (c + 1) * 128
                ]
        rows = pl.ds(g * chunk * PER, chunk * PER)
        stores.append(pltpu.make_async_copy(out_ref.at[rows], out_hbm.at[rows], out_sems.at[g]))
        stores[-1].start()
    for store in stores:
        store.wait()


def edge_rows_kernel(die_first, die_last, diff_first, diff_last, even_ref, odd_ref):
    is_even = lax.rem(lax.axis_index("span"), 2) == 0

    def layer(z, carry):
        for n, (first, low, last, high) in enumerate(
            ((die_first, 0, die_last, 6), (die_first, 1, die_last, 7), (diff_first, 0, diff_last, 7))
        ):
            top = first[z, low : low + 1, :]
            bottom = last[z, high : high + 1, :]
            even_ref[pl.ds(n * DZ + z, 1), :] = jnp.where(is_even, bottom, top)
            odd_ref[pl.ds(n * DZ + z, 1), :] = jnp.where(is_even, top, bottom)
        return carry

    lax.fori_loop(0, DZ, layer, 0, unroll=8)


def edge_columns_kernel(
    die_ref, diff_ref, even_in, odd_in, temp_ref, even_ref, odd_ref, die_rim, diff_rim, face_ref
):
    span_even = lax.rem(lax.axis_index("span"), 2) == 0
    depth_even = lax.rem(lax.axis_index("depth"), 2) == 0
    sub = iota((8, SB), 0)

    def rim_of(z, spots):
        tile = jnp.zeros((8, SB), F32)
        for spot, n, up in spots:
            at = pl.ds(n * DZ + z, 1)
            row = jnp.where(span_even != up, even_in[at, :], odd_in[at, :])
            tile = jnp.where(sub == spot, row, tile)
        return tile

    lane = iota((EX, 128), 1)

    def add_layer(z, kept):
        v_left, v_right, k_left, k_right = kept
        rows, rim = pl.ds(pl.multiple_of(z * CX, CX), CX), pl.ds(pl.multiple_of(z * 8, 8), 8)
        v_rim = rim_of(z, ((0, 0, False), (1, 1, False), (6, 0, True), (7, 1, True)))
        k_rim = rim_of(z, ((0, 2, False), (7, 2, True)))
        die_rim[rim, :] = v_rim
        diff_rim[rim, :] = k_rim
        v = jnp.concatenate([die_ref[rows, :], v_rim], axis=0)
        k = jnp.concatenate([diff_ref[rows, :], k_rim], axis=0)
        v_here, k_here = lax.shift_right_logical(lane, 1) == z, lane == z
        v_left = jnp.where(v_here, pltpu.roll(v[:, :128], 2 * z, 1), v_left)
        v_right = jnp.where(v_here, pltpu.roll(v[:, 128:], 2 * z + 2, 1), v_right)
        k_left = jnp.where(k_here, pltpu.roll(k[:, :128], z, 1), k_left)
        k_right = jnp.where(k_here, pltpu.roll(k[:, 128:], z + 1, 1), k_right)
        return v_left, v_right, k_left, k_right

    none = jnp.zeros((EX, 128), F32)
    v_left, v_right, k_left, k_right = lax.fori_loop(0, DZ, add_layer, (none,) * 4, unroll=8)
    even_ref[:EX, :128] = jnp.where(depth_even, v_right, v_left)
    even_ref[:EX, 128:] = jnp.where(depth_even, k_right, k_left)
    odd_ref[:EX, :128] = jnp.where(depth_even, v_left, v_right)
    odd_ref[:EX, 128:] = jnp.where(depth_even, k_left, k_right)
    first, last = temp_ref[0:1, :], temp_ref[NB - 1 : NB, :]
    even_ref[EX:, :] = jnp.broadcast_to(jnp.where(depth_even, last, first), (8, SB))
    odd_ref[EX:, :] = jnp.broadcast_to(jnp.where(depth_even, first, last), (8, SB))
    face_ref[...] = die_ref[:CX, :]


def across(p):
    q = p + 0.5 * (pltpu.roll(p, 1, 1) + pltpu.roll(p, p.shape[1] - 1, 1))
    return q + 0.5 * (pltpu.roll(q, 1, 0) + pltpu.roll(q, q.shape[0] - 1, 0))


def sweeps_kernel(
    die_hbm, diff_hbm, die_rim, diff_rim, heat_ref, even_in, odd_in, out_hbm,
    die_ref, diff_ref, out_ref, field, later, rate, sems, out_sems,
):
    some = DZ // CHUNKS
    loads = []
    for n in range(CHUNKS):
        for m, (source, target) in enumerate(((die_hbm, die_ref), (diff_hbm, diff_ref))):
            rows = pl.ds(n * some * CX, some * CX)
            loads.append(
                pltpu.make_async_copy(source.at[rows], target.at[rows], sems.at[2 * n + m])
            )
            loads[-1].start()
    depth_even = lax.rem(lax.axis_index("depth"), 2) == 0
    none = jnp.zeros((EX, EY), F32)
    for ref in (field, later):
        ref[0] = none
        ref[DZ + 1] = none
    lane = iota((EX, 128), 1)
    right = jnp.where(depth_even, even_in[:EX, :], odd_in[:EX, :])
    left = jnp.where(depth_even, odd_in[:EX, :], even_in[:EX, :])
    for n in range(CHUNKS):
        loads[2 * n].wait()
        loads[2 * n + 1].wait()
        for z in range(n * some, (n + 1) * some):
            field[z + 1, :CX, :SB] = die_ref[z * CX : (z + 1) * CX, :]
            field[z + 1, CX:, :SB] = die_rim[z * 8 : (z + 1) * 8, :]
            rate[z, :CX, :SB] = diff_ref[z * CX : (z + 1) * CX, :]
            rate[z, CX:, :SB] = diff_rim[z * 8 : (z + 1) * 8, :]
            v_right = pltpu.roll(right[:, :128], (128 - 2 * z) % 128, 1)
            v_left = pltpu.roll(left[:, :128], 126 - 2 * z, 1)
            k_right = pltpu.roll(right[:, 128:], (128 - z) % 128, 1)
            k_left = pltpu.roll(left[:, 128:], 127 - z, 1)
            field[z + 1, :, SB:] = jnp.where(
                lane < 2, v_right, jnp.where(lane >= 126, v_left, 0.0)
            )
            rate[z, :, SB:] = jnp.where(lane < 1, k_right, jnp.where(lane >= 127, k_left, 0.0))
    h_right = pltpu.roll(right[:, :128], 128 - 2 * DZ, 1)
    h_left = pltpu.roll(left[:, :128], 126 - 2 * DZ, 1)
    field[1, :, :SB] += heat_ref[...]
    field[1, :, SB:] += jnp.where(lane < 2, h_right, jnp.where(lane >= 126, h_left, 0.0))

    gap = jnp.abs(iota((EY, EY), 0) - iota((EY, EY), 1))
    band = jnp.where(
        gap == 0, 1.0, jnp.where(jnp.logical_or(gap == 1, gap == EY - 1), 0.5, 0.0)
    ).astype(BF16)

    def around(ref, start, width):
        layers = []
        for n in range(GROUP):
            z = start + n
            layers.append(2.0 * ref[z + 1] + (ref[z] + ref[z + 2]))
        p = jnp.concatenate(layers, axis=0)
        high, low = split(p)
        q = jnp.dot(high, band[:, :width], preferred_element_type=F32)
        q = q + jnp.dot(low, band[:, :width], preferred_element_type=F32)
        for n in range(GROUP):
            own = q[n * EX : (n + 1) * EX]
            yield own + 0.5 * (pltpu.roll(own, 1, 0) + pltpu.roll(own, EX - 1, 0))

    def first(g, carry):
        for n, q in enumerate(around(field, g * GROUP, EY)):
            z = g * GROUP + n
            v = field[z + 1]
            later[z + 1] = v + rate[z] * (q - 16.0 * v)
        return carry

    lax.fori_loop(0, DZ // GROUP, first, 0, unroll=4 * UNROLL)

    def second(g, carry):
        for n, q in enumerate(around(later, g * GROUP, SB)):
            z = g * GROUP + n
            v = later[z + 1, :CX, :SB]
            out_ref[z] = v + rate[z, :CX, :SB] * (q[:CX] - 16.0 * v)
        return carry

    stores = []
    for n in range(CHUNKS):
        lax.fori_loop(
            n * some // GROUP, (n + 1) * some // GROUP, second, 0, unroll=UNROLL
        )
        layers = pl.ds(n * some, some)
        stores.append(pltpu.make_async_copy(out_ref.at[layers], out_hbm.at[layers], out_sems.at[n]))
        stores[-1].start()
    for store in stores:
        store.wait()


def owner_kernel(
    got_hbm, face_ref, flux_hbm, heat_ref, even_ref, odd_ref,
    got_ref, flux_ref, sems, out_sem,
):
    rows = SPAN * PER // CHUNKS
    loads = [
        pltpu.make_async_copy(
            got_hbm.at[pl.ds(n * rows, rows)], got_ref.at[pl.ds(n * rows, rows)], sems.at[n]
        )
        for n in range(CHUNKS)
    ]
    for load in loads:
        load.start()
    lane = iota((SPAN, 128), 1).astype(F32)
    faces = jnp.concatenate([face_ref[...], jnp.zeros((128 - CX, SB), F32)], axis=0)
    for load in loads:
        load.wait()
    codes = got_ref[pl.ds(4 * CAP, SPAN, stride=PER), :]
    onehot = jnp.concatenate(
        [jnp.where(codes[:, k : k + 1] == lane, 1.0, 0.0) for k in range(CAP)], axis=0
    ).astype(BF16)
    touched = pick(onehot, faces)

    def slots(c):
        return jnp.concatenate(
            [got_ref[pl.ds(k * 4 + c, SPAN, stride=PER), :] for k in range(CAP)], axis=0
        )

    temp = jnp.concatenate([slots(0), slots(1)], axis=1)
    gain = jnp.concatenate([slots(2), slots(3)], axis=1)
    flux = gain * (temp - touched)
    for k in range(CAP):
        for c in range(2):
            flux_ref[pl.ds(c * CAP + k, SPAN, stride=2 * CAP), :] = flux[
                k * SPAN : (k + 1) * SPAN, c * 128 : (c + 1) * 128
            ]
    store = pltpu.make_async_copy(flux_ref, flux_hbm, out_sem)
    store.start()
    heat = FACE_GAIN * pick(onehot, flux, (((0,), (0,)), ((), ())))[:CX]
    heat_ref[...] = heat
    is_even = lax.rem(lax.axis_index("span"), 2) == 0
    even_ref[...] = jnp.where(is_even, heat[CX - 8 :], heat[:8])
    odd_ref[...] = jnp.where(is_even, heat[:8], heat[CX - 8 :])
    store.wait()


def heat_edges_kernel(
    heat_ref, even_in, odd_in, even_packed, odd_packed, rows_ref, even_ref, odd_ref
):
    span_even = lax.rem(lax.axis_index("span"), 2) == 0
    depth_even = lax.rem(lax.axis_index("depth"), 2) == 0
    below = jnp.where(span_even, even_in[...], odd_in[...])
    above = jnp.where(span_even, odd_in[...], even_in[...])
    sub = iota((8, SB), 0)
    rim = jnp.where(sub < 2, below, jnp.where(sub >= 6, above, 0.0))
    rows = jnp.concatenate([heat_ref[...], rim], axis=0)
    rows_ref[...] = rows
    here = lax.shift_right_logical(iota((EX, 128), 1), 1) == DZ
    left = pltpu.roll(rows[:, :128], 2 * DZ, 1)
    right = pltpu.roll(rows[:, 128:], 2 * DZ + 2, 1)
    for packed, out, one, other in (
        (even_packed, even_ref, right, left),
        (odd_packed, odd_ref, left, right),
    ):
        edge = jnp.where(depth_even, one, other)
        out[:EX, :128] = jnp.where(here, edge, packed[:EX, :128])
        out[:EX, 128:] = packed[:EX, 128:]
        out[EX:, :] = packed[EX:, :]


def shell_kernel(
    routes_ref, temp_ref, even_in, odd_in, flux_hbm, out_ref, flux_ref, sems
):
    some = SPAN // CHUNKS
    loads = [
        pltpu.make_async_copy(
            flux_hbm.at[pl.ds(n * some, some)], flux_ref.at[pl.ds(n * some, some)], sems.at[n]
        )
        for n in range(CHUNKS)
    ]
    for load in loads:
        load.start()
    depth_even = lax.rem(lax.axis_index("depth"), 2) == 0
    below = jnp.where(depth_even, even_in[EX : EX + 1, :], odd_in[EX : EX + 1, :])
    above = jnp.where(depth_even, odd_in[EX : EX + 1, :], even_in[EX : EX + 1, :])
    temp = temp_ref[...]
    sub, lane = iota((NB, SB), 0), iota((NB, SB), 1)
    upper = jnp.where(sub == 0, above, pltpu.roll(temp, 1, 0))
    lower = jnp.where(sub == NB - 1, below, pltpu.roll(temp, NB - 1, 0))
    before = jnp.where(lane == 0, 0.0, pltpu.roll(temp, 1, 1))
    after = jnp.where(lane == SB - 1, 0.0, pltpu.roll(temp, SB - 1, 1))
    laplace = lower + upper + after + before - 4.0 * temp
    out_ref[...] = temp + SHELL_RATE * laplace
    target = routes_ref[...].astype(F32)
    target_col = as_column(target, sub == lane)
    same = jnp.logical_and(target_col == target, lane < sub)
    rank_col = jnp.sum(jnp.where(same, 1.0, 0.0), axis=1, keepdims=True)
    position = (target_col * CAP + rank_col).astype(jnp.int32)
    slots = SLOTS // CHUNKS
    total = jnp.zeros((NB, SB), F32)
    for n in range(CHUNKS):
        take = jnp.where(iota((NB, slots), 1) + n * slots == position, 1.0, 0.0).astype(BF16)
        loads[n].wait()
        rows = slice(n * some, (n + 1) * some)
        flux = jnp.concatenate(
            [
                flux_ref[rows, c * CAP : (c + 1) * CAP, :].reshape(slots, 128)
                for c in range(2)
            ],
            axis=1,
        )
        total = total + pick(take, flux)
    out_ref[...] -= SHELL_SINK * total


def swap(even, odd, axis):
    size = lax.axis_size(axis)
    pairs = [(i, i ^ 1) for i in range(size)]
    shifted = [(i, ((i + 1) ^ 1) - 1) for i in range(1, size - 1)]
    return lax.ppermute(even, axis, pairs), lax.ppermute(odd, axis, shifted)


def local(shell_temp, contact_gain, die_temp, diffusivity, routes, tile_rows, closed):
    temp, gain = shell_temp[0], contact_gain[0]
    target = routes.reshape(1, NB)
    die, diff = die_temp.reshape(DZ * CX, SB), diffusivity.reshape(DZ * CX, SB)
    rows = jax.ShapeDtypeStruct((3 * DZ, SB), F32)
    even, odd = pl.pallas_call(
        edge_rows_kernel,
        out_shape=(rows, rows),
        grid=(1,),
        in_specs=[
            pl.BlockSpec((DZ, 8, SB), lambda i: (0, 0, 0)),
            pl.BlockSpec((DZ, 8, SB), lambda i: (0, CX // 8 - 1, 0)),
        ]
        * 2,
        out_specs=(VMEM,) * 2,
        compiler_params=params(60),
        name="edge_rows",
    )(die_temp, die_temp, diffusivity, diffusivity)
    sent = pl.pallas_call(
        pack_kernel,
        out_shape=pltpu.HBM((SPAN * PER, 128), F32),
        in_specs=[HBM] * 5,
        out_specs=HBM,
        scratch_shapes=[
            pltpu.VMEM((1, NB), jnp.int32),
            pltpu.VMEM((1, NB), jnp.int32),
            pltpu.VMEM((1, NB), jnp.int32),
            pltpu.VMEM((NB, SB), F32),
            pltpu.VMEM((NB, SB), F32),
            pltpu.VMEM((SPAN * PER, 128), F32),
            pltpu.SemaphoreType.DMA((5,)),
            pltpu.SemaphoreType.DMA((CHUNKS,)),
        ],
        compiler_params=params(60),
        cost_estimate=cost(6 * SLOTS * NB * 2 * SB, 4 * 2**20),
        name="pack",
    )(target, tile_rows, closed, temp, gain)
    got = lax.all_to_all(
        sent.reshape(SPAN * PER, 1, 128), "span", split_axis=0, concat_axis=0, tiled=True
    ).reshape(SPAN * PER, 128)
    even, odd = swap(even, odd, "span")
    columns, rim = pltpu.HBM((EX + 8, SB), F32), pltpu.HBM((DZ * 8, SB), F32)
    even_packed, odd_packed, die_rim, diff_rim, face = pl.pallas_call(
        edge_columns_kernel,
        out_shape=(columns, columns, rim, rim, pltpu.HBM((CX, SB), F32)),
        grid=(1,),
        in_specs=[VMEM] * 5,
        out_specs=(whole(EX + 8, SB),) * 2 + (whole(DZ * 8, SB),) * 2 + (whole(CX, SB),),
        compiler_params=params(16),
        name="edge_columns",
    )(die, diff, even, odd, temp)

    edge = jax.ShapeDtypeStruct((8, SB), F32)
    flux, heat, even, odd = pl.pallas_call(
        owner_kernel,
        out_shape=(
            pltpu.HBM((2 * SLOTS, 128), F32),
            jax.ShapeDtypeStruct((CX, SB), F32),
            edge,
            edge,
        ),
        grid=(1,),
        in_specs=[HBM, whole(CX, SB)],
        out_specs=(HBM, VMEM, VMEM, VMEM),
        scratch_shapes=[
            pltpu.VMEM((SPAN * PER, 128), F32),
            pltpu.VMEM((2 * SLOTS, 128), F32),
            pltpu.SemaphoreType.DMA((CHUNKS,)),
            pltpu.SemaphoreType.DMA,
        ],
        compiler_params=params(16),
        name="owner",
    )(got, face)
    back = lax.all_to_all(
        flux.reshape(SPAN, 2 * CAP, 128), "span", split_axis=0, concat_axis=0, tiled=True
    )
    even, odd = swap(even, odd, "span")
    heat_rows, even, odd = pl.pallas_call(
        heat_edges_kernel,
        out_shape=(jax.ShapeDtypeStruct((EX, SB), F32),)
        + (jax.ShapeDtypeStruct((EX + 8, SB), F32),) * 2,
        in_specs=[VMEM] * 5,
        out_specs=(VMEM,) * 3,
        compiler_params=params(8),
        cost_estimate=cost(10**12, 2**32),
        name="heat_edges",
    )(heat, even, odd, even_packed, odd_packed)
    even, odd = swap(even, odd, "depth")
    die_next = pl.pallas_call(
        sweeps_kernel,
        out_shape=pltpu.HBM((DZ, CX, SB), F32),
        grid=(1,),
        in_specs=[HBM, HBM, whole(DZ * 8, SB), whole(DZ * 8, SB)] + [VMEM] * 3,
        out_specs=HBM,
        scratch_shapes=[
            pltpu.VMEM((DZ * CX, SB), F32),
            pltpu.VMEM((DZ * CX, SB), F32),
            pltpu.VMEM((DZ, CX, SB), F32),
            pltpu.VMEM((DZ + 2, EX, EY), F32),
            pltpu.VMEM((DZ + 2, EX, EY), F32),
            pltpu.VMEM((DZ, EX, EY), F32),
            pltpu.SemaphoreType.DMA((2 * CHUNKS,)),
            pltpu.SemaphoreType.DMA((CHUNKS,)),
        ],
        compiler_params=params(24),
        name="sweeps",
    )(die, diff, die_rim, diff_rim, heat_rows, even, odd)
    shell_next = pl.pallas_call(
        shell_kernel,
        out_shape=pltpu.HBM((NB, SB), F32),
        grid=(1,),
        in_specs=[VMEM, VMEM, VMEM, VMEM, HBM],
        out_specs=whole(NB, SB),
        scratch_shapes=[
            pltpu.VMEM((SPAN, 2 * CAP, 128), F32),
            pltpu.SemaphoreType.DMA((CHUNKS,)),
        ],
        compiler_params=params(16),
        name="shell",
    )(target, temp, even, odd, back)
    return shell_next[None], die_next


def solution(mesh):
    placed = (
        P("span", "depth", None),
        P("span", "depth", None),
        P(None, "span", "depth"),
        P(None, "span", "depth"),
        P("span", "depth", None),
        P("span", "depth"),
        P("span", "depth"),
    )
    return jax.shard_map(
        local,
        mesh=mesh,
        in_specs=placed,
        out_specs=(P("span", "depth", None), P(None, "span", "depth")),
        check_vma=False,
    )
```

time: 90.3 us -> 86.5 us (0.958)
  waiting for transfers between devices: 21.6 us -> 26.8 us
  starting transfers between devices: 42.2 us -> 38.1 us
  Pallas kernels: 22.9 us -> 19.5 us
  local copies, waits for them, and re-layouts: 2.18 us -> 0.81 us
    all_to_all x1, waiting for transfers between devices: 0.01 us -> 14.1 us  [local(): lax.all_to_all(sent.reshape(SPAN * PER, 1, 128), 'span', split_axis=0, co...]
    ppermute x8 -> x6, waiting for transfers between devices: 19.9 us -> 12.7 us  [swap(): return (lax.ppermute(even, axis, pairs), lax.ppermute(odd, axis, shifted))]
    ppermute x8 -> x6, starting transfers between devices: 17.5 us -> 11.7 us  [swap(): return (lax.ppermute(even, axis, pairs), lax.ppermute(odd, axis, shifted))]
    pallas_call x6 -> x4, Pallas kernels: 18.1 us -> 14.4 us  [the longest x1 6.99 us: local(): pl.pallas_call(sweeps_kernel, out_shape=pltpu.HBM((DZ, CX, SB), F32), gri...]
    all_to_all x1, waiting for transfers between devices: 1.76 us -> 0.01 us  [local(): lax.all_to_all(flux.reshape(SPAN, 2 * CAP, 128), 'span', split_axis=0, co...]
    all_to_all x1, starting transfers between devices: 12.2 us -> 13.6 us  [local(): lax.all_to_all(flux.reshape(SPAN, 2 * CAP, 128), 'span', split_axis=0, co...]
    unnamed x18 -> x20, local copies, waits for them, and re-layouts: 2.18 us -> 0.81 us
  transfers between devices with their start and end apart: 10 -> 8, of which waited for: 3 -> 3; matrix products, arithmetic and copies ran while one was open for 0% -> 0% of each run, Pallas kernels for 17% -> 14%
where the time goes in v3:
time: 86.5 us; the launch traced here: 86 us
  starting transfers between devices  38.1 us (44%)
  waiting for transfers between devices  26.8 us (31%)
  Pallas kernels  19.5 us (23%)
    all_to_all x1, waiting for transfers between devices, local(): lax.all_to_all(sent.reshape(SPAN * PER, 1, 128), 'span', split_axis=0, co...  14.1 us
    all_to_all x1, starting transfers between devices, local(): lax.all_to_all(flux.reshape(SPAN, 2 * CAP, 128), 'span', split_axis=0, co...  13.6 us
    all_to_all x1, starting transfers between devices, local(): lax.all_to_all(sent.reshape(SPAN * PER, 1, 128), 'span', split_axis=0, co...  12.8 us
    ppermute x6, waiting for transfers between devices, swap(): return (lax.ppermute(even, axis, pairs), lax.ppermute(odd, axis, shifted))  12.7 us
    ppermute x6, starting transfers between devices, swap(): return (lax.ppermute(even, axis, pairs), lax.ppermute(odd, axis, shifted))  11.7 us
    pallas_call x1, Pallas kernels, local(): pl.pallas_call(sweeps_kernel, out_shape=pltpu.HBM((DZ, CX, SB), F32), gri...  6.99 us
    pallas_call x1, Pallas kernels, local(): pl.pallas_call(edge_rows_kernel, out_shape=(rows, rows), grid=(1,), in_sp...  2.57 us
    pallas_call x1, Pallas kernels, local(): pl.pallas_call(owner_kernel, out_shape=(pltpu.HBM((2 * SLOTS, 128), F32),...  2.55 us
  transfers between devices with their start and end apart: 8, of which 3 were waited for; matrix products, arithmetic and copies ran while one was open for 0% of the time, Pallas kernels for 14%

profile of v3, /device:TPU:1, one launch (start us, length us, event | category | flops | bytes accessed | tf_op | source)
XLA Modules:
  0.0 86.0 jit_solution(5362445324574383568)
XLA Ops:
  0.6 2.4 %pack.1 = f32[2112,128]{1,0:T(8,128)} custom-call(s32[1,256]{1,0:T(1,128)} %bitcast.18, s32[1,256]{1,0:T(1,128)} %tile_hbm.1, s32[1,256]{1,0:T(1,128)} %closed_hbm.1, f32[256,256]{1,0:T(8,128)} %bitcast.15, f32[256,256]{1,0:T(8,128)} %bitcast.22), custom_call_target="tpu_custom_call" | custom-call | flops 402653184 | bytes 4194304 | tf_op jit(solution)/shard_map/pack/pallas_call | solution.py:422
  3.0 12.8 %all-to-all-start = ((f32[2112,1,128]{2,1,0:T(1,128)}), f32[2112,1,128]{2,1,0:T(1,128)}, u32[]{:S(2)}, u32[]{:S(2)}) async-start(f32[2112,1,128]{2,1,0:T(1,128)} %bitcast.20), calls=%async_computation | async-start | bytes 2162688 | tf_op jit(solution)/shard_map/all_to_all | solution.py:441
  15.8 0.0 copy-start
  15.9 0.0 copy-start.2
  15.9 0.0 copy-start.3
  15.9 2.6 %edge_rows.1 = (f32[144,256]{1,0:T(8,128)}, f32[144,256]{1,0:T(8,128)}) custom-call(f32[48,32,256]{2,1,0:T(8,128)} %die_last.1, f32[48,32,256]{2,1,0:T(8,128)} %die_last.1, f32[48,32,256]{2,1,0:T(8,128)} %diff_last.1, f32[48,32,256]{2,1,0:T(8,128)} %diff_last.1), custom_call_target="tpu_custom_call" | custom-call | tf_op jit(solution)/shard_map/edge_rows/pallas_call | solution.py:409
  18.4 0.9 %collective-permute-start = (f32[144,256]{1,0:T(8,128)}, f32[144,256]{1,0:T(8,128)S(1)}, u32[]{:S(2)}, u32[]{:S(2)}) collective-permute-start(f32[144,256]{1,0:T(8,128)} %get-tuple-element.16), channel_id=1, source_target_pairs={{0,4},{4,0},{8,12},{12,8},{16,20},{20,16},{24,28},{28,24},{32,36},... | collective-permute-start | bytes 442376 | tf_op jit(solution)/shard_map/ppermute | solution.py:401
  19.4 0.7 collective-permute-start.1
  20.1 7.9 %collective-permute-done.even_in = f32[144,256]{1,0:T(8,128)S(1)} collective-permute-done((f32[144,256]{1,0:T(8,128)}, f32[144,256]{1,0:T(8,128)S(1)}, u32[]{:S(2)}, u32[]{:S(2)}) %collective-permute-start) | collective-permute-done | bytes 147488 | tf_op jit(solution)/shard_map/ppermute | solution.py:401
  28.0 0.0 collective-permute-done.1.odd_in
  28.0 0.0 copy-done
  28.0 0.0 copy-done.2
  28.0 0.0 copy-done.3
  28.0 2.4 %edge_columns.1 = (f32[48,256]{1,0:T(8,128)}, f32[48,256]{1,0:T(8,128)}, f32[384,256]{1,0:T(8,128)}, f32[384,256]{1,0:T(8,128)}, f32[32,256]{1,0:T(8,128)}) custom-call(f32[1536,256]{1,0:T(8,128)S(1)} %bitcast.11, f32[1536,256]{1,0:T(8,128)S(1)} %bitcast.13, f32[144,256]{1,0:T(8,128)S(1)} %collective-permute-done.even_in, ...), custom_call_target="tpu_custom_call" | custom-call | tf_op jit(solution)/shard_map/edge_columns/pallas_call | solution.py:446
  30.4 14.1 %all-to-all-done = f32[2112,1,128]{2,1,0:T(1,128)} async-done(((f32[2112,1,128]{2,1,0:T(1,128)}), f32[2112,1,128]{2,1,0:T(1,128)}, u32[]{:S(2)}, u32[]{:S(2)}) %all-to-all-start) | async-done | bytes 1081376 | tf_op jit(solution)/shard_map/all_to_all | solution.py:441
  44.5 0.0 copy-start.6
  44.5 0.8 copy-done.6
  45.3 0.0 copy-start.8
  45.3 0.0 copy-start.9
  45.3 2.5 %owner.1 = (f32[1024,128]{1,0:T(8,128)}, f32[32,256]{1,0:T(8,128)S(1)}, f32[8,256]{1,0:T(8,128)S(1)}, f32[8,256]{1,0:T(8,128)S(1)}) custom-call(f32[2112,128]{1,0:T(8,128)} %bitcast.5.got_hbm, f32[32,256]{1,0:T(8,128)S(1)} %copy-done.6), custom_call_target="tpu_custom_call" | custom-call | tf_op jit(solution)/shard_map/owner/pallas_call | solution.py:457
  47.8 0.4 collective-permute-start.2
  48.2 0.6 collective-permute-start.3
  48.9 13.6 %all-to-all-start.1 = ((f32[64,16,128]{2,1,0:T(8,128)}), f32[64,16,128]{2,1,0:T(8,128)}, u32[]{:S(2)}, u32[]{:S(2)}) async-start(f32[64,16,128]{2,1,0:T(8,128)} %bitcast.21), calls=%async_computation.1 | async-start | bytes 1048576 | tf_op jit(solution)/shard_map/all_to_all | solution.py:477
  62.5 0.0 collective-permute-done.2.even_in
  62.5 0.0 collective-permute-done.3.odd_in
  62.5 0.0 copy-done.8
  62.6 0.0 copy-done.9
  62.6 0.0 copy-start.1
  62.6 0.0 copy-start.4
  62.6 0.0 copy-start.5
  62.6 0.1 heat_edges.1
  62.7 2.9 %collective-permute-start.4 = (f32[48,256]{1,0:T(8,128)S(1)}, f32[48,256]{1,0:T(8,128)S(1)}, u32[]{:S(2)}, u32[]{:S(2)}) collective-permute-start(f32[48,256]{1,0:T(8,128)S(1)} %get-tuple-element.24), channel_id=1, source_target_pairs={{0,1},{1,0},{2,3},{3,2},{4,5},{5,4},{6,7},{7,6},{8,9},{9,8},{10,11... | collective-permute-start | bytes 147464 | tf_op jit(solution)/shard_map/ppermute | solution.py:401
  65.6 6.2 %collective-permute-start.5 = (f32[48,256]{1,0:T(8,128)S(1)}, f32[48,256]{1,0:T(8,128)S(1)}, u32[]{:S(2)}, u32[]{:S(2)}) collective-permute-start(f32[48,256]{1,0:T(8,128)S(1)} %get-tuple-element.25), channel_id=1, source_target_pairs={{1,2},{2,1},{5,6},{6,5},{9,10},{10,9},{13,14},{14,13},{17,18},{18,... | collective-permute-start | bytes 147464 | tf_op jit(solution)/shard_map/ppermute | solution.py:401
  71.7 0.0 collective-permute-done.4.even_in
  71.8 4.7 %collective-permute-done.5.odd_in = f32[48,256]{1,0:T(8,128)S(1)} collective-permute-done((f32[48,256]{1,0:T(8,128)S(1)}, f32[48,256]{1,0:T(8,128)S(1)}, u32[]{:S(2)}, u32[]{:S(2)}) %collective-permute-start.5) | collective-permute-done | bytes 49184 | tf_op jit(solution)/shard_map/ppermute | solution.py:401
  76.5 0.0 copy-done.1
  76.5 0.0 copy-done.4
  76.5 0.0 copy-done.5
  76.5 0.0 copy-start.7
  76.5 7.0 %sweeps.1 = f32[48,32,256]{2,1,0:T(8,128)} custom-call(f32[1536,256]{1,0:T(8,128)S(1)} %bitcast.12, f32[1536,256]{1,0:T(8,128)S(1)} %bitcast.14, f32[384,256]{1,0:T(8,128)S(1)} %copy-done.4, f32[384,256]{1,0:T(8,128)S(1)} %copy-done.5, f32[40,256]{1,0:T(8,128)S(1)} %get-tuple-element.29.heat_ref, f32[48,256]{1,0:T(8,128)S(1)} %collective-permute-done.4.even_in, ...), custom_call_target="tpu_custom_call" | custom-call | tf_op jit(solution)/shard_map/sweeps/pallas_call | solution.py:492
  83.5 0.0 all-to-all-done.1.flux_hbm
  83.5 0.0 copy-done.7
  83.5 2.5 %shell.1 = f32[256,256]{1,0:T(8,128)} custom-call(s32[1,256]{1,0:T(1,128)S(1)} %bitcast.19, f32[256,256]{1,0:T(8,128)S(1)} %bitcast.17, f32[48,256]{1,0:T(8,128)S(1)} %collective-permute-done.4.even_in, f32[48,256]{1,0:T(8,128)S(1)} %collective-permute-done.5.odd_in, f32[64,16,128]{2,1,0:T(8,128)} %all-to-all-done.1.flux_hbm), custom_call_target="tpu_custom_call" | custom-call | tf_op jit(solution)/shard_map/shell/pallas_call | solution.py:511
Async XLA Ops:
  3.0 41.5 %all-to-all-start = ((f32[2112,1,128]{2,1,0:T(1,128)}), f32[2112,1,128]{2,1,0:T(1,128)}, u32[]{:S(2)}, u32[]{:S(2)}) async-start(f32[2112,1,128]{2,1,0:T(1,128)} %bitcast.20), calls=%async_computation | async-start | bytes 2162688 | tf_op jit(solution)/shard_map/all_to_all | solution.py:441
  15.8 12.1 %copy-start = (f32[48,32,256]{2,1,0:T(8,128)S(1)}, f32[48,32,256]{2,1,0:T(8,128)}, u32[]{:S(2)}) copy-start(f32[48,32,256]{2,1,0:T(8,128)} %die_last.1) | copy-start | bytes 4718596
  15.9 12.1 %copy-start.2 = (f32[48,32,256]{2,1,0:T(8,128)S(1)}, f32[48,32,256]{2,1,0:T(8,128)}, u32[]{:S(2)}) copy-start(f32[48,32,256]{2,1,0:T(8,128)} %diff_last.1) | copy-start | bytes 4718596
  15.9 12.1 %copy-start.3 = (f32[1,256,256]{2,1,0:T(8,128)S(1)}, f32[1,256,256]{2,1,0:T(8,128)}, u32[]{:S(2)}) copy-start(f32[1,256,256]{2,1,0:T(8,128)} %param.7) | copy-start | bytes 786436
  18.4 9.5 %collective-permute-start = (f32[144,256]{1,0:T(8,128)}, f32[144,256]{1,0:T(8,128)S(1)}, u32[]{:S(2)}, u32[]{:S(2)}) collective-permute-start(f32[144,256]{1,0:T(8,128)} %get-tuple-element.16), channel_id=1, source_target_pairs={{0,4},{4,0},{8,12},{12,8},{16,20},{20,16},{24,28},{28,24},{32,36},... | collective-permute-start | bytes 442376 | tf_op jit(solution)/shard_map/ppermute | solution.py:401
  19.4 8.6 %collective-permute-start.1 = (f32[144,256]{1,0:T(8,128)}, f32[144,256]{1,0:T(8,128)S(1)}, u32[]{:S(2)}, u32[]{:S(2)}) collective-permute-start(f32[144,256]{1,0:T(8,128)} %get-tuple-element.17), channel_id=1, source_target_pairs={{4,8},{8,4},{12,16},{16,12},{20,24},{24,20},{28,32},{32,28},{36,40... | collective-permute-start | bytes 442376 | tf_op jit(solution)/shard_map/ppermute | solution.py:401
  44.5 0.8 copy-start.6
  45.3 17.3 %copy-start.8 = (f32[48,256]{1,0:T(8,128)S(1)}, f32[48,256]{1,0:T(8,128)}, u32[]{:S(2)}) copy-start(f32[48,256]{1,0:T(8,128)} %get-tuple-element.22.even_packed) | copy-start | bytes 147460
  45.3 17.3 %copy-start.9 = (f32[48,256]{1,0:T(8,128)S(1)}, f32[48,256]{1,0:T(8,128)}, u32[]{:S(2)}) copy-start(f32[48,256]{1,0:T(8,128)} %get-tuple-element.23.odd_packed) | copy-start | bytes 147460
  47.8 14.7 %collective-permute-start.2 = (f32[8,256]{1,0:T(8,128)S(1)}, f32[8,256]{1,0:T(8,128)S(1)}, u32[]{:S(2)}, u32[]{:S(2)}) collective-permute-start(f32[8,256]{1,0:T(8,128)S(1)} %get-tuple-element.20), channel_id=1, source_target_pairs={{0,4},{4,0},{8,12},{12,8},{16,20},{20,16},{24,28},{28,24},{32,36},... | collective-permute-start | bytes 24584 | tf_op jit(solution)/shard_map/ppermute | solution.py:401
  48.2 14.3 %collective-permute-start.3 = (f32[8,256]{1,0:T(8,128)S(1)}, f32[8,256]{1,0:T(8,128)S(1)}, u32[]{:S(2)}, u32[]{:S(2)}) collective-permute-start(f32[8,256]{1,0:T(8,128)S(1)} %get-tuple-element.21), channel_id=1, source_target_pairs={{4,8},{8,4},{12,16},{16,12},{20,24},{24,20},{28,32},{32,28},{36,40... | collective-permute-start | bytes 24584 | tf_op jit(solution)/shard_map/ppermute | solution.py:401
  48.9 34.6 %all-to-all-start.1 = ((f32[64,16,128]{2,1,0:T(8,128)}), f32[64,16,128]{2,1,0:T(8,128)}, u32[]{:S(2)}, u32[]{:S(2)}) async-start(f32[64,16,128]{2,1,0:T(8,128)} %bitcast.21), calls=%async_computation.1 | async-start | bytes 1048576 | tf_op jit(solution)/shard_map/all_to_all | solution.py:477
  62.6 13.9 %copy-start.1 = (f32[48,32,256]{2,1,0:T(8,128)S(1)}, f32[48,32,256]{2,1,0:T(8,128)}, u32[]{:S(2)}) copy-start(f32[48,32,256]{2,1,0:T(8,128)} %die_last.1) | copy-start | bytes 4718596
  62.6 13.9 %copy-start.4 = (f32[384,256]{1,0:T(8,128)S(1)}, f32[384,256]{1,0:T(8,128)}, u32[]{:S(2)}) copy-start(f32[384,256]{1,0:T(8,128)} %get-tuple-element.27.die_rim) | copy-start | bytes 1179652
  62.6 13.9 %copy-start.5 = (f32[384,256]{1,0:T(8,128)S(1)}, f32[384,256]{1,0:T(8,128)}, u32[]{:S(2)}) copy-start(f32[384,256]{1,0:T(8,128)} %get-tuple-element.28.diff_rim) | copy-start | bytes 1179652
  62.7 9.1 %collective-permute-start.4 = (f32[48,256]{1,0:T(8,128)S(1)}, f32[48,256]{1,0:T(8,128)S(1)}, u32[]{:S(2)}, u32[]{:S(2)}) collective-permute-start(f32[48,256]{1,0:T(8,128)S(1)} %get-tuple-element.24), channel_id=1, source_target_pairs={{0,1},{1,0},{2,3},{3,2},{4,5},{5,4},{6,7},{7,6},{8,9},{9,8},{10,11... | collective-permute-start | bytes 147464 | tf_op jit(solution)/shard_map/ppermute | solution.py:401
  65.6 10.9 %collective-permute-start.5 = (f32[48,256]{1,0:T(8,128)S(1)}, f32[48,256]{1,0:T(8,128)S(1)}, u32[]{:S(2)}, u32[]{:S(2)}) collective-permute-start(f32[48,256]{1,0:T(8,128)S(1)} %get-tuple-element.25), channel_id=1, source_target_pairs={{1,2},{2,1},{5,6},{6,5},{9,10},{10,9},{13,14},{14,13},{17,18},{18,... | collective-permute-start | bytes 147464 | tf_op jit(solution)/shard_map/ppermute | solution.py:401
  76.5 7.0 %copy-start.7 = (s32[1,256,1]{1,2,0:T(1,128)S(1)}, s32[1,256,1]{1,2,0:T(1,128)}, u32[]{:S(2)}) copy-start(s32[1,256,1]{1,2,0:T(1,128)} %param.11) | copy-start | bytes 3076

commit v4 on v3

--- a/solution.py
+++ b/solution.py
@@ -167,11 +167,11 @@
         diff_rim[rim, :] = k_rim
         v = jnp.concatenate([die_ref[rows, :], v_rim], axis=0)
         k = jnp.concatenate([diff_ref[rows, :], k_rim], axis=0)
-        v_here, k_here = lax.shift_right_logical(lane, 1) == z, lane == z
-        v_left = jnp.where(v_here, pltpu.roll(v[:, :128], 2 * z, 1), v_left)
-        v_right = jnp.where(v_here, pltpu.roll(v[:, 128:], 2 * z + 2, 1), v_right)
-        k_left = jnp.where(k_here, pltpu.roll(k[:, :128], z, 1), k_left)
-        k_right = jnp.where(k_here, pltpu.roll(k[:, 128:], z + 1, 1), k_right)
+        here = lax.shift_right_logical(lane, 1) == z
+        v_left = jnp.where(here, pltpu.roll(v[:, :128], 2 * z, 1), v_left)
+        v_right = jnp.where(here, pltpu.roll(v[:, 128:], 2 * z + 2, 1), v_right)
+        k_left = jnp.where(here, pltpu.roll(k[:, :128], 2 * z, 1), k_left)
+        k_right = jnp.where(here, pltpu.roll(k[:, 128:], 2 * z + 2, 1), k_right)
         return v_left, v_right, k_left, k_right
 
     none = jnp.zeros((EX, 128), F32)
@@ -192,9 +192,10 @@
 
 
 def sweeps_kernel(
-    die_hbm, diff_hbm, die_rim, diff_rim, heat_ref, even_in, odd_in, out_hbm,
-    die_ref, diff_ref, out_ref, field, later, rate, sems, out_sems,
+    die_hbm, diff_hbm, die_rim, diff_rim, after_ref, out_ref,
+    die_ref, diff_ref, field, later, rate, sems,
 ):
+    del after_ref
     some = DZ // CHUNKS
     loads = []
     for n in range(CHUNKS):
@@ -204,55 +205,36 @@
                 pltpu.make_async_copy(source.at[rows], target.at[rows], sems.at[2 * n + m])
             )
             loads[-1].start()
-    depth_even = lax.rem(lax.axis_index("depth"), 2) == 0
-    none = jnp.zeros((EX, EY), F32)
+    none = jnp.zeros((EX, SB), F32)
     for ref in (field, later):
         ref[0] = none
         ref[DZ + 1] = none
-    lane = iota((EX, 128), 1)
-    right = jnp.where(depth_even, even_in[:EX, :], odd_in[:EX, :])
-    left = jnp.where(depth_even, odd_in[:EX, :], even_in[:EX, :])
     for n in range(CHUNKS):
         loads[2 * n].wait()
         loads[2 * n + 1].wait()
         for z in range(n * some, (n + 1) * some):
-            field[z + 1, :CX, :SB] = die_ref[z * CX : (z + 1) * CX, :]
-            field[z + 1, CX:, :SB] = die_rim[z * 8 : (z + 1) * 8, :]
-            rate[z, :CX, :SB] = diff_ref[z * CX : (z + 1) * CX, :]
-            rate[z, CX:, :SB] = diff_rim[z * 8 : (z + 1) * 8, :]
-            v_right = pltpu.roll(right[:, :128], (128 - 2 * z) % 128, 1)
-            v_left = pltpu.roll(left[:, :128], 126 - 2 * z, 1)
-            k_right = pltpu.roll(right[:, 128:], (128 - z) % 128, 1)
-            k_left = pltpu.roll(left[:, 128:], 127 - z, 1)
-            field[z + 1, :, SB:] = jnp.where(
-                lane < 2, v_right, jnp.where(lane >= 126, v_left, 0.0)
-            )
-            rate[z, :, SB:] = jnp.where(lane < 1, k_right, jnp.where(lane >= 127, k_left, 0.0))
-    h_right = pltpu.roll(right[:, :128], 128 - 2 * DZ, 1)
-    h_left = pltpu.roll(left[:, :128], 126 - 2 * DZ, 1)
-    field[1, :, :SB] += heat_ref[...]
-    field[1, :, SB:] += jnp.where(lane < 2, h_right, jnp.where(lane >= 126, h_left, 0.0))
-
-    gap = jnp.abs(iota((EY, EY), 0) - iota((EY, EY), 1))
-    band = jnp.where(
-        gap == 0, 1.0, jnp.where(jnp.logical_or(gap == 1, gap == EY - 1), 0.5, 0.0)
-    ).astype(BF16)
-
-    def around(ref, start, width):
+            field[z + 1, :CX] = die_ref[z * CX : (z + 1) * CX, :]
+            field[z + 1, CX:] = die_rim[z * 8 : (z + 1) * 8, :]
+            rate[z, :CX] = diff_ref[z * CX : (z + 1) * CX, :]
+            rate[z, CX:] = diff_rim[z * 8 : (z + 1) * 8, :]
+    gap = jnp.abs(iota((SB, SB), 0) - iota((SB, SB), 1))
+    band = jnp.where(gap == 0, 1.0, jnp.where(gap == 1, 0.5, 0.0)).astype(BF16)
+
+    def around(ref, start):
         layers = []
         for n in range(GROUP):
             z = start + n
             layers.append(2.0 * ref[z + 1] + (ref[z] + ref[z + 2]))
         p = jnp.concatenate(layers, axis=0)
         high, low = split(p)
-        q = jnp.dot(high, band[:, :width], preferred_element_type=F32)
-        q = q + jnp.dot(low, band[:, :width], preferred_element_type=F32)
+        q = jnp.dot(high, band, preferred_element_type=F32)
+        q = q + jnp.dot(low, band, preferred_element_type=F32)
         for n in range(GROUP):
             own = q[n * EX : (n + 1) * EX]
             yield own + 0.5 * (pltpu.roll(own, 1, 0) + pltpu.roll(own, EX - 1, 0))
 
     def first(g, carry):
-        for n, q in enumerate(around(field, g * GROUP, EY)):
+        for n, q in enumerate(around(field, g * GROUP)):
             z = g * GROUP + n
             v = field[z + 1]
             later[z + 1] = v + rate[z] * (q - 16.0 * v)
@@ -261,19 +243,98 @@
     lax.fori_loop(0, DZ // GROUP, first, 0, unroll=4 * UNROLL)
 
     def second(g, carry):
-        for n, q in enumerate(around(later, g * GROUP, SB)):
+        for n, q in enumerate(around(later, g * GROUP)):
             z = g * GROUP + n
-            v = later[z + 1, :CX, :SB]
-            out_ref[z] = v + rate[z, :CX, :SB] * (q[:CX] - 16.0 * v)
+            v = later[z + 1, :CX]
+            out_ref[z] = v + rate[z, :CX] * (q[:CX] - 16.0 * v)
         return carry
 
+    lax.fori_loop(0, DZ // GROUP, second, 0, unroll=4 * UNROLL)
+
+
+def smooth(x):
+    z = 2.0 * x + (pltpu.roll(x, 2, 1) + pltpu.roll(x, 126, 1))
+    return z + 0.5 * (pltpu.roll(z, 1, 0) + pltpu.roll(z, EX - 1, 0))
+
+
+def finish_kernel(
+    base_ref, diff_top, diff_rim, heat_ref, even_own, odd_own, even_in, odd_in, out_hbm,
+    out_ref, out_sems,
+):
+    some = DZ // CHUNKS
+    depth_even = lax.rem(lax.axis_index("depth"), 2) == 0
+    lane = iota((EX, 128), 1)
+    die = lane < 2 * DZ
+    first_lane = jnp.logical_and(die, lax.rem(lane, 2) == 0)
+    second_lane = jnp.logical_and(die, lax.rem(lane, 2) == 1)
+
+    def parts(even_ref, odd_ref, when):
+        v = jnp.where(when, even_ref[:EX, :128], odd_ref[:EX, :128])
+        return v, jnp.where(when, even_ref[:EX, 128:], odd_ref[:EX, 128:])
+
+    right_v, right_k = parts(even_own, odd_own, depth_even)
+    left_v, left_k = parts(even_own, odd_own, jnp.logical_not(depth_even))
+    after_v, after_k = parts(even_in, odd_in, depth_even)
+    before_v, before_k = parts(even_in, odd_in, jnp.logical_not(depth_even))
+
+    def up(x):
+        return pltpu.roll(x, 1, 1)
+
+    def down(x):
+        return pltpu.roll(x, 127, 1)
+
+    def change(own_v, own_k, out_v, out_k, outer, inner, to_outer, to_inner):
+        own_w, out_w = smooth(jnp.where(die, own_v, 0.0)), smooth(jnp.where(die, out_v, 0.0))
+        near = out_v + out_k * (
+            out_w + 0.5 * (to_outer(out_w) + to_outer(own_w)) - 16.0 * out_v
+        )
+        near = jnp.where(outer, near, 0.0)
+        moved = jnp.where(inner, 0.5 * own_k * to_inner(out_w), 0.0)
+        spread = smooth(moved)
+        edge = moved + own_k * (spread - 16.0 * moved + 0.5 * to_inner(smooth(near)))
+        return jnp.where(inner, edge, jnp.where(die, 0.5 * own_k * to_outer(spread), 0.0))
+
+    left = change(left_v, left_k, before_v, before_k, second_lane, first_lane, up, down)
+    right = change(right_v, right_k, after_v, after_k, first_lane, second_lane, down, up)
+
+    h_right, h_left = pltpu.roll(after_v, 128 - 2 * DZ, 1), pltpu.roll(before_v, 126 - 2 * DZ, 1)
+    rim = jnp.where(lane < 2, h_right, jnp.where(lane >= 126, h_left, 0.0))
+    heat = jnp.concatenate([heat_ref[...], rim], axis=1)
+    rates = []
+    for z in range(3):
+        k_right = pltpu.roll(after_k, (128 - 2 * z) % 128, 1)
+        k_left = pltpu.roll(before_k, 126 - 2 * z, 1)
+        k_rim = jnp.where(lane < 1, k_right, jnp.where(lane >= 127, k_left, 0.0))
+        own = jnp.concatenate([diff_top[z], diff_rim[z * 8 : (z + 1) * 8, :]], axis=0)
+        rates.append(jnp.concatenate([own, k_rim], axis=1))
+    around = across(heat)
+    first = heat + rates[0] * (2.0 * around - 16.0 * heat)
+    second = rates[1] * around
+    added = []
+    for rate, own, p in (
+        (rates[0], first, 2.0 * first + second),
+        (rates[1], second, 2.0 * second + first),
+        (rates[2], 0.0, second),
+    ):
+        added.append((own + rate * (across(p) - 16.0 * own))[:CX, :SB])
+
+    left, right = left[:CX], right[:CX]
+    edge = iota((CX, 128), 1)
     stores = []
     for n in range(CHUNKS):
-        lax.fori_loop(
-            n * some // GROUP, (n + 1) * some // GROUP, second, 0, unroll=UNROLL
+        for z in range(n * some, (n + 1) * some):
+            at_left = pltpu.roll(left, (128 - 2 * z) % 128, 1)
+            at_right = pltpu.roll(right, 126 - 2 * z, 1)
+            near = jnp.where(edge < 2, at_left, 0.0)
+            far = jnp.where(edge >= 126, at_right, 0.0)
+            step = jnp.concatenate([near, far], axis=1)
+            if z < 3:
+                step = step + added[z]
+            out_ref[z] = base_ref[z] + step
+        layers = pl.ds(n * some, some)
+        stores.append(
+            pltpu.make_async_copy(out_ref.at[layers], out_hbm.at[layers], out_sems.at[n])
         )
-        layers = pl.ds(n * some, some)
-        stores.append(pltpu.make_async_copy(out_ref.at[layers], out_hbm.at[layers], out_sems.at[n]))
         stores[-1].start()
     for store in stores:
         store.wait()
@@ -488,26 +549,43 @@
         cost_estimate=cost(10**12, 2**32),
         name="heat_edges",
     )(heat, even, odd, even_packed, odd_packed)
-    even, odd = swap(even, odd, "depth")
-    die_next = pl.pallas_call(
+    base = pl.pallas_call(
         sweeps_kernel,
-        out_shape=pltpu.HBM((DZ, CX, SB), F32),
+        out_shape=jax.ShapeDtypeStruct((DZ, CX, SB), F32),
         grid=(1,),
-        in_specs=[HBM, HBM, whole(DZ * 8, SB), whole(DZ * 8, SB)] + [VMEM] * 3,
-        out_specs=HBM,
+        in_specs=[HBM, HBM, whole(DZ * 8, SB), whole(DZ * 8, SB), VMEM],
+        out_specs=VMEM,
         scratch_shapes=[
             pltpu.VMEM((DZ * CX, SB), F32),
             pltpu.VMEM((DZ * CX, SB), F32),
-            pltpu.VMEM((DZ, CX, SB), F32),
-            pltpu.VMEM((DZ + 2, EX, EY), F32),
-            pltpu.VMEM((DZ + 2, EX, EY), F32),
-            pltpu.VMEM((DZ, EX, EY), F32),
+            pltpu.VMEM((DZ + 2, EX, SB), F32),
+            pltpu.VMEM((DZ + 2, EX, SB), F32),
+            pltpu.VMEM((DZ, EX, SB), F32),
             pltpu.SemaphoreType.DMA((2 * CHUNKS,)),
-            pltpu.SemaphoreType.DMA((CHUNKS,)),
         ],
         compiler_params=params(24),
         name="sweeps",
-    )(die, diff, die_rim, diff_rim, heat_rows, even, odd)
+    )(die, diff, die_rim, diff_rim, heat_rows)
+    even_own, odd_own = even, odd
+    even, odd = swap(even, odd, "depth")
+    die_next = pl.pallas_call(
+        finish_kernel,
+        out_shape=pltpu.HBM((DZ, CX, SB), F32),
+        grid=(1,),
+        in_specs=[
+            VMEM,
+            whole(3, CX, SB),
+            pl.BlockSpec((24, SB), lambda i: (0, 0)),
+        ]
+        + [VMEM] * 5,
+        out_specs=HBM,
+        scratch_shapes=[
+            pltpu.VMEM((DZ, CX, SB), F32),
+            pltpu.SemaphoreType.DMA((CHUNKS,)),
+        ],
+        compiler_params=params(16),
+        name="finish",
+    )(base, diffusivity, diff_rim, heat_rows, even_own, odd_own, even, odd)
     shell_next = pl.pallas_call(
         shell_kernel,
         out_shape=pltpu.HBM((NB, SB), F32),

time: 86.5 us -> 83.2 us (0.962)
  the two profiles are of different devices: /device:TPU:1 before, /device:TPU:2 now
where the time goes in v4:
time: 83.2 us; the launch traced here: 82.7 us
  starting transfers between devices  33.9 us (41%)
  waiting for transfers between devices  28 us (34%)
  Pallas kernels  18.6 us (22%)
  local copies, waits for them, and re-layouts  1.37 us (2%)
    all_to_all x1, waiting for transfers between devices, local(): lax.all_to_all(sent.reshape(SPAN * PER, 1, 128), 'span', split_axis=0, co...  13.8 us
    all_to_all x1, starting transfers between devices, local(): lax.all_to_all(flux.reshape(SPAN, 2 * CAP, 128), 'span', split_axis=0, co...  12.5 us
    all_to_all x1, starting transfers between devices, local(): lax.all_to_all(sent.reshape(SPAN * PER, 1, 128), 'span', split_axis=0, co...  12.3 us
    ppermute x6, starting transfers between devices, swap(): return (lax.ppermute(even, axis, pairs), lax.ppermute(odd, axis, shifted))  9.12 us
    all_to_all x1, waiting for transfers between devices, local(): lax.all_to_all(flux.reshape(SPAN, 2 * CAP, 128), 'span', split_axis=0, co...  8.59 us
    ppermute x6, waiting for transfers between devices, swap(): return (lax.ppermute(even, axis, pairs), lax.ppermute(odd, axis, shifted))  5.65 us
    pallas_call x1, Pallas kernels, local(): pl.pallas_call(sweeps_kernel, out_shape=jax.ShapeDtypeStruct((DZ, CX, SB)...  4.32 us
    pallas_call x1, Pallas kernels, local(): pl.pallas_call(edge_rows_kernel, out_shape=(rows, rows), grid=(1,), in_sp...  2.57 us
  transfers between devices with their start and end apart: 8, of which 4 were waited for; matrix products, arithmetic and copies ran while one was open for 0% of the time, Pallas kernels for 14%

profile of v4, /device:TPU:2, one launch (start us, length us, event | category | flops | bytes accessed | tf_op | source)
XLA Modules:
  0.0 82.7 jit_solution(3554163299799000503)
XLA Ops:
  0.6 2.4 %pack.1 = f32[2112,128]{1,0:T(8,128)} custom-call(s32[1,256]{1,0:T(1,128)} %bitcast.18, s32[1,256]{1,0:T(1,128)} %tile_hbm.1, s32[1,256]{1,0:T(1,128)} %closed_hbm.1, f32[256,256]{1,0:T(8,128)} %bitcast.15, f32[256,256]{1,0:T(8,128)} %bitcast.22), custom_call_target="tpu_custom_call" | custom-call | flops 402653184 | bytes 4194304 | tf_op jit(solution)/shard_map/pack/pallas_call | solution.py:483
  3.0 12.3 %all-to-all-start = ((f32[2112,1,128]{2,1,0:T(1,128)}), f32[2112,1,128]{2,1,0:T(1,128)}, u32[]{:S(2)}, u32[]{:S(2)}) async-start(f32[2112,1,128]{2,1,0:T(1,128)} %bitcast.20), calls=%async_computation | async-start | bytes 2162688 | tf_op jit(solution)/shard_map/all_to_all | solution.py:502
  15.3 0.0 copy-start
  15.3 0.0 copy-start.2
  15.3 0.0 copy-start.3
  15.3 2.6 %edge_rows.1 = (f32[144,256]{1,0:T(8,128)}, f32[144,256]{1,0:T(8,128)}) custom-call(f32[48,32,256]{2,1,0:T(8,128)} %die_last.1, f32[48,32,256]{2,1,0:T(8,128)} %die_last.1, f32[48,32,256]{2,1,0:T(8,128)} %diff_top.1, f32[48,32,256]{2,1,0:T(8,128)} %diff_top.1), custom_call_target="tpu_custom_call" | custom-call | tf_op jit(solution)/shard_map/edge_rows/pallas_call | solution.py:470
  17.9 0.5 collective-permute-start
  18.4 4.0 %collective-permute-start.1 = (f32[144,256]{1,0:T(8,128)}, f32[144,256]{1,0:T(8,128)S(1)}, u32[]{:S(2)}, u32[]{:S(2)}) collective-permute-start(f32[144,256]{1,0:T(8,128)} %get-tuple-element.17), channel_id=1, source_target_pairs={{4,8},{8,4},{12,16},{16,12},{20,24},{24,20},{28,32},{32,28},{36,40... | collective-permute-start | bytes 442376 | tf_op jit(solution)/shard_map/ppermute | solution.py:462
  22.4 3.9 %collective-permute-done.even_in = f32[144,256]{1,0:T(8,128)S(1)} collective-permute-done((f32[144,256]{1,0:T(8,128)}, f32[144,256]{1,0:T(8,128)S(1)}, u32[]{:S(2)}, u32[]{:S(2)}) %collective-permute-start) | collective-permute-done | bytes 147488 | tf_op jit(solution)/shard_map/ppermute | solution.py:462
  26.3 1.7 %collective-permute-done.1.odd_in = f32[144,256]{1,0:T(8,128)S(1)} collective-permute-done((f32[144,256]{1,0:T(8,128)}, f32[144,256]{1,0:T(8,128)S(1)}, u32[]{:S(2)}, u32[]{:S(2)}) %collective-permute-start.1) | collective-permute-done | bytes 147488 | tf_op jit(solution)/shard_map/ppermute | solution.py:462
  28.1 0.0 copy-done
  28.1 0.0 copy-done.2
  28.1 0.0 copy-done.3
  28.1 2.4 %edge_columns.1 = (f32[48,256]{1,0:T(8,128)}, f32[48,256]{1,0:T(8,128)}, f32[384,256]{1,0:T(8,128)}, f32[384,256]{1,0:T(8,128)}, f32[32,256]{1,0:T(8,128)}) custom-call(f32[1536,256]{1,0:T(8,128)S(1)} %bitcast.13, f32[1536,256]{1,0:T(8,128)S(1)} %bitcast.11, f32[144,256]{1,0:T(8,128)S(1)} %collective-permute-done.even_in, ...), custom_call_target="tpu_custom_call" | custom-call | tf_op jit(solution)/shard_map/edge_columns/pallas_call | solution.py:507
  30.5 13.8 %all-to-all-done = f32[2112,1,128]{2,1,0:T(1,128)} async-done(((f32[2112,1,128]{2,1,0:T(1,128)}), f32[2112,1,128]{2,1,0:T(1,128)}, u32[]{:S(2)}, u32[]{:S(2)}) %all-to-all-start) | async-done | bytes 1081376 | tf_op jit(solution)/shard_map/all_to_all | solution.py:502
  44.3 0.0 copy-start.6
  44.3 0.8 copy-done.6
  45.0 0.0 copy-start.8
  45.0 0.0 copy-start.9
  45.0 2.5 %owner.1 = (f32[1024,128]{1,0:T(8,128)}, f32[32,256]{1,0:T(8,128)S(1)}, f32[8,256]{1,0:T(8,128)S(1)}, f32[8,256]{1,0:T(8,128)S(1)}) custom-call(f32[2112,128]{1,0:T(8,128)} %bitcast.5.got_hbm, f32[32,256]{1,0:T(8,128)S(1)} %copy-done.6), custom_call_target="tpu_custom_call" | custom-call | tf_op jit(solution)/shard_map/owner/pallas_call | solution.py:518
  47.6 1.5 %collective-permute-start.2 = (f32[8,256]{1,0:T(8,128)S(1)}, f32[8,256]{1,0:T(8,128)S(1)}, u32[]{:S(2)}, u32[]{:S(2)}) collective-permute-start(f32[8,256]{1,0:T(8,128)S(1)} %get-tuple-element.20), channel_id=1, source_target_pairs={{0,4},{4,0},{8,12},{12,8},{16,20},{20,16},{24,28},{28,24},{32,36},... | collective-permute-start | bytes 24584 | tf_op jit(solution)/shard_map/ppermute | solution.py:462
  49.1 2.2 %collective-permute-start.3 = (f32[8,256]{1,0:T(8,128)S(1)}, f32[8,256]{1,0:T(8,128)S(1)}, u32[]{:S(2)}, u32[]{:S(2)}) collective-permute-start(f32[8,256]{1,0:T(8,128)S(1)} %get-tuple-element.21), channel_id=1, source_target_pairs={{4,8},{8,4},{12,16},{16,12},{20,24},{24,20},{28,32},{32,28},{36,40... | collective-permute-start | bytes 24584 | tf_op jit(solution)/shard_map/ppermute | solution.py:462
  51.3 12.5 %all-to-all-start.1 = ((f32[64,16,128]{2,1,0:T(8,128)}), f32[64,16,128]{2,1,0:T(8,128)}, u32[]{:S(2)}, u32[]{:S(2)}) async-start(f32[64,16,128]{2,1,0:T(8,128)} %bitcast.21), calls=%async_computation.1 | async-start | bytes 1048576 | tf_op jit(solution)/shard_map/all_to_all | solution.py:538
  63.8 0.0 collective-permute-done.2.even_in
  63.8 0.0 collective-permute-done.3.odd_in
  63.9 0.0 copy-done.8
  63.9 0.0 copy-done.9
  63.9 0.0 copy-start.1
  63.9 0.0 copy-start.4
  63.9 0.0 copy-start.5
  63.9 0.1 heat_edges.1
  64.0 0.1 collective-permute-start.4
  64.1 0.8 collective-permute-start.5
  64.9 0.4 copy-done.1
  65.3 0.1 copy-done.4
  65.3 0.1 copy-done.5
  65.5 4.3 %sweeps.1.base_ref = f32[48,32,256]{2,1,0:T(8,128)S(1)} custom-call(f32[1536,256]{1,0:T(8,128)S(1)} %bitcast.14, f32[1536,256]{1,0:T(8,128)S(1)} %bitcast.12, f32[384,256]{1,0:T(8,128)S(1)} %copy-done.5, f32[384,256]{1,0:T(8,128)S(1)} %copy-done.4, f32[40,256]{1,0:T(8,128)S(1)} %get-tuple-element.29.after_ref.heat_ref), custom_call_target="tpu_custom_call" | custom-call | tf_op jit(solution)/shard_map/sweeps/pallas_call | solution.py:552
  69.8 0.0 copy-start.7
  69.8 0.0 collective-permute-done.4.even_in
  69.8 0.0 collective-permute-done.5.odd_in
  69.8 1.8 %finish.1 = f32[48,32,256]{2,1,0:T(8,128)} custom-call(f32[48,32,256]{2,1,0:T(8,128)S(1)} %sweeps.1.base_ref, f32[48,32,256]{2,1,0:T(8,128)S(1)} %copy-done.1, f32[384,256]{1,0:T(8,128)S(1)} %copy-done.4, f32[40,256]{1,0:T(8,128)S(1)} %get-tuple-element.29.after_ref.heat_ref, f32[48,256]{1,0:T(8,128)S(1)} %get-tuple-element.24.even_own, ...), custom_call_target="tpu_custom_call" | custom-call | tf_op jit(solution)/shard_map/finish/pallas_call | solution.py:571
  71.6 8.6 %all-to-all-done.1.flux_hbm = f32[64,16,128]{2,1,0:T(8,128)} async-done(((f32[64,16,128]{2,1,0:T(8,128)}), f32[64,16,128]{2,1,0:T(8,128)}, u32[]{:S(2)}, u32[]{:S(2)}) %all-to-all-start.1) | async-done | bytes 524320 | tf_op jit(solution)/shard_map/all_to_all | solution.py:538
  80.2 0.0 copy-done.7
  80.2 2.5 %shell.1 = f32[256,256]{1,0:T(8,128)} custom-call(s32[1,256]{1,0:T(1,128)S(1)} %bitcast.19, f32[256,256]{1,0:T(8,128)S(1)} %bitcast.17, f32[48,256]{1,0:T(8,128)S(1)} %collective-permute-done.4.even_in, f32[48,256]{1,0:T(8,128)S(1)} %collective-permute-done.5.odd_in, f32[64,16,128]{2,1,0:T(8,128)} %all-to-all-done.1.flux_hbm), custom_call_target="tpu_custom_call" | custom-call | tf_op jit(solution)/shard_map/shell/pallas_call | solution.py:589
Async XLA Ops:
  3.0 41.2 %all-to-all-start = ((f32[2112,1,128]{2,1,0:T(1,128)}), f32[2112,1,128]{2,1,0:T(1,128)}, u32[]{:S(2)}, u32[]{:S(2)}) async-start(f32[2112,1,128]{2,1,0:T(1,128)} %bitcast.20), calls=%async_computation | async-start | bytes 2162688 | tf_op jit(solution)/shard_map/all_to_all | solution.py:502
  15.3 12.8 %copy-start = (f32[48,32,256]{2,1,0:T(8,128)S(1)}, f32[48,32,256]{2,1,0:T(8,128)}, u32[]{:S(2)}) copy-start(f32[48,32,256]{2,1,0:T(8,128)} %diff_top.1) | copy-start | bytes 4718596
  15.3 12.8 %copy-start.2 = (f32[48,32,256]{2,1,0:T(8,128)S(1)}, f32[48,32,256]{2,1,0:T(8,128)}, u32[]{:S(2)}) copy-start(f32[48,32,256]{2,1,0:T(8,128)} %die_last.1) | copy-start | bytes 4718596
  15.3 12.8 %copy-start.3 = (f32[1,256,256]{2,1,0:T(8,128)S(1)}, f32[1,256,256]{2,1,0:T(8,128)}, u32[]{:S(2)}) copy-start(f32[1,256,256]{2,1,0:T(8,128)} %param.7) | copy-start | bytes 786436
  17.9 8.4 %collective-permute-start = (f32[144,256]{1,0:T(8,128)}, f32[144,256]{1,0:T(8,128)S(1)}, u32[]{:S(2)}, u32[]{:S(2)}) collective-permute-start(f32[144,256]{1,0:T(8,128)} %get-tuple-element.16), channel_id=1, source_target_pairs={{0,4},{4,0},{8,12},{12,8},{16,20},{20,16},{24,28},{28,24},{32,36},... | collective-permute-start | bytes 442376 | tf_op jit(solution)/shard_map/ppermute | solution.py:462
  18.4 9.7 %collective-permute-start.1 = (f32[144,256]{1,0:T(8,128)}, f32[144,256]{1,0:T(8,128)S(1)}, u32[]{:S(2)}, u32[]{:S(2)}) collective-permute-start(f32[144,256]{1,0:T(8,128)} %get-tuple-element.17), channel_id=1, source_target_pairs={{4,8},{8,4},{12,16},{16,12},{20,24},{24,20},{28,32},{32,28},{36,40... | collective-permute-start | bytes 442376 | tf_op jit(solution)/shard_map/ppermute | solution.py:462
  44.3 0.8 copy-start.6
  45.0 18.8 %copy-start.8 = (f32[48,256]{1,0:T(8,128)S(1)}, f32[48,256]{1,0:T(8,128)}, u32[]{:S(2)}) copy-start(f32[48,256]{1,0:T(8,128)} %get-tuple-element.22.even_packed) | copy-start | bytes 147460
  45.0 18.8 %copy-start.9 = (f32[48,256]{1,0:T(8,128)S(1)}, f32[48,256]{1,0:T(8,128)}, u32[]{:S(2)}) copy-start(f32[48,256]{1,0:T(8,128)} %get-tuple-element.23.odd_packed) | copy-start | bytes 147460
  47.6 16.2 %collective-permute-start.2 = (f32[8,256]{1,0:T(8,128)S(1)}, f32[8,256]{1,0:T(8,128)S(1)}, u32[]{:S(2)}, u32[]{:S(2)}) collective-permute-start(f32[8,256]{1,0:T(8,128)S(1)} %get-tuple-element.20), channel_id=1, source_target_pairs={{0,4},{4,0},{8,12},{12,8},{16,20},{20,16},{24,28},{28,24},{32,36},... | collective-permute-start | bytes 24584 | tf_op jit(solution)/shard_map/ppermute | solution.py:462
  49.1 14.7 %collective-permute-start.3 = (f32[8,256]{1,0:T(8,128)S(1)}, f32[8,256]{1,0:T(8,128)S(1)}, u32[]{:S(2)}, u32[]{:S(2)}) collective-permute-start(f32[8,256]{1,0:T(8,128)S(1)} %get-tuple-element.21), channel_id=1, source_target_pairs={{4,8},{8,4},{12,16},{16,12},{20,24},{24,20},{28,32},{32,28},{36,40... | collective-permute-start | bytes 24584 | tf_op jit(solution)/shard_map/ppermute | solution.py:462
  51.3 28.9 %all-to-all-start.1 = ((f32[64,16,128]{2,1,0:T(8,128)}), f32[64,16,128]{2,1,0:T(8,128)}, u32[]{:S(2)}, u32[]{:S(2)}) async-start(f32[64,16,128]{2,1,0:T(8,128)} %bitcast.21), calls=%async_computation.1 | async-start | bytes 1048576 | tf_op jit(solution)/shard_map/all_to_all | solution.py:538
  63.9 1.4 %copy-start.1 = (f32[48,32,256]{2,1,0:T(8,128)S(1)}, f32[48,32,256]{2,1,0:T(8,128)}, u32[]{:S(2)}) copy-start(f32[48,32,256]{2,1,0:T(8,128)} %diff_top.1) | copy-start | bytes 4718596
  63.9 1.5 %copy-start.4 = (f32[384,256]{1,0:T(8,128)S(1)}, f32[384,256]{1,0:T(8,128)}, u32[]{:S(2)}) copy-start(f32[384,256]{1,0:T(8,128)} %get-tuple-element.28.diff_rim) | copy-start | bytes 1179652
  63.9 1.6 %copy-start.5 = (f32[384,256]{1,0:T(8,128)S(1)}, f32[384,256]{1,0:T(8,128)}, u32[]{:S(2)}) copy-start(f32[384,256]{1,0:T(8,128)} %get-tuple-element.27.die_rim) | copy-start | bytes 1179652
  64.0 5.8 %collective-permute-start.4 = (f32[48,256]{1,0:T(8,128)S(1)}, f32[48,256]{1,0:T(8,128)S(1)}, u32[]{:S(2)}, u32[]{:S(2)}) collective-permute-start(f32[48,256]{1,0:T(8,128)S(1)} %get-tuple-element.24.even_own), channel_id=1, source_target_pairs={{0,1},{1,0},{2,3},{3,2},{4,5},{5,4},{6,7},{7,6},{8,9},{9,8},{10,11... | collective-permute-start | bytes 147464 | tf_op jit(solution)/shard_map/ppermute | solution.py:462
  64.1 5.7 %collective-permute-start.5 = (f32[48,256]{1,0:T(8,128)S(1)}, f32[48,256]{1,0:T(8,128)S(1)}, u32[]{:S(2)}, u32[]{:S(2)}) collective-permute-start(f32[48,256]{1,0:T(8,128)S(1)} %get-tuple-element.25.odd_own), channel_id=1, source_target_pairs={{1,2},{2,1},{5,6},{6,5},{9,10},{10,9},{13,14},{14,13},{17,18},{18,... | collective-permute-start | bytes 147464 | tf_op jit(solution)/shard_map/ppermute | solution.py:462
  69.8 10.4 %copy-start.7 = (s32[1,256,1]{1,2,0:T(1,128)S(1)}, s32[1,256,1]{1,2,0:T(1,128)}, u32[]{:S(2)}) copy-start(s32[1,256,1]{1,2,0:T(1,128)} %param.11) | copy-start | bytes 3076

commit v5 on v4

--- a/solution.py
+++ b/solution.py
@@ -341,8 +341,8 @@
 
 
 def owner_kernel(
-    got_hbm, face_ref, flux_hbm, heat_ref, even_ref, odd_ref,
-    got_ref, flux_ref, sems, out_sem,
+    got_hbm, face_hbm, flux_hbm, heat_hbm, even_hbm, odd_hbm,
+    got_ref, face_ref, flux_ref, heat_ref, even_ref, odd_ref, sems, out_sems,
 ):
     rows = SPAN * PER // CHUNKS
     loads = [
@@ -351,12 +351,13 @@
         )
         for n in range(CHUNKS)
     ]
+    loads.append(pltpu.make_async_copy(face_hbm, face_ref, sems.at[CHUNKS]))
     for load in loads:
         load.start()
     lane = iota((SPAN, 128), 1).astype(F32)
-    faces = jnp.concatenate([face_ref[...], jnp.zeros((128 - CX, SB), F32)], axis=0)
     for load in loads:
         load.wait()
+    faces = jnp.concatenate([face_ref[...], jnp.zeros((128 - CX, SB), F32)], axis=0)
     codes = got_ref[pl.ds(4 * CAP, SPAN, stride=PER), :]
     onehot = jnp.concatenate(
         [jnp.where(codes[:, k : k + 1] == lane, 1.0, 0.0) for k in range(CAP)], axis=0
@@ -376,13 +377,23 @@
             flux_ref[pl.ds(c * CAP + k, SPAN, stride=2 * CAP), :] = flux[
                 k * SPAN : (k + 1) * SPAN, c * 128 : (c + 1) * 128
             ]
-    store = pltpu.make_async_copy(flux_ref, flux_hbm, out_sem)
+    store = pltpu.make_async_copy(flux_ref, flux_hbm, out_sems.at[3])
     store.start()
     heat = FACE_GAIN * pick(onehot, flux, (((0,), (0,)), ((), ())))[:CX]
     heat_ref[...] = heat
     is_even = lax.rem(lax.axis_index("span"), 2) == 0
     even_ref[...] = jnp.where(is_even, heat[CX - 8 :], heat[:8])
     odd_ref[...] = jnp.where(is_even, heat[:8], heat[CX - 8 :])
+    small = [
+        pltpu.make_async_copy(source, target, out_sems.at[n])
+        for n, (source, target) in enumerate(
+            ((heat_ref, heat_hbm), (even_ref, even_hbm), (odd_ref, odd_hbm))
+        )
+    ]
+    for copy in small:
+        copy.start()
+    for copy in small:
+        copy.wait()
     store.wait()
 
 
@@ -514,25 +525,29 @@
         name="edge_columns",
     )(die, diff, even, odd, temp)
 
-    edge = jax.ShapeDtypeStruct((8, SB), F32)
+    edge = pltpu.HBM((8, SB), F32)
     flux, heat, even, odd = pl.pallas_call(
         owner_kernel,
         out_shape=(
             pltpu.HBM((2 * SLOTS, 128), F32),
-            jax.ShapeDtypeStruct((CX, SB), F32),
+            pltpu.HBM((CX, SB), F32),
             edge,
             edge,
         ),
         grid=(1,),
-        in_specs=[HBM, whole(CX, SB)],
-        out_specs=(HBM, VMEM, VMEM, VMEM),
+        in_specs=[HBM] * 2,
+        out_specs=(HBM,) * 4,
         scratch_shapes=[
             pltpu.VMEM((SPAN * PER, 128), F32),
+            pltpu.VMEM((CX, SB), F32),
             pltpu.VMEM((2 * SLOTS, 128), F32),
-            pltpu.SemaphoreType.DMA((CHUNKS,)),
-            pltpu.SemaphoreType.DMA,
+            pltpu.VMEM((CX, SB), F32),
+            pltpu.VMEM((8, SB), F32),
+            pltpu.VMEM((8, SB), F32),
+            pltpu.SemaphoreType.DMA((CHUNKS + 1,)),
+            pltpu.SemaphoreType.DMA((4,)),
         ],
-        compiler_params=params(16),
+        compiler_params=params(60),
         name="owner",
     )(got, face)
     back = lax.all_to_all(

time: 83.2 us -> 81.5 us (0.980)
  the two profiles are of different devices: /device:TPU:2 before, /device:TPU:1 now
where the time goes in v5:
time: 81.5 us; the launch traced here: 80.5 us
  starting transfers between devices  38.1 us (47%)
  waiting for transfers between devices  22 us (27%)
  Pallas kernels  18.7 us (23%)
  between operations  0.85 us (1%)
    all_to_all x1, waiting for transfers between devices, local(): lax.all_to_all(sent.reshape(SPAN * PER, 1, 128), 'span', split_axis=0, co...  14.1 us
    all_to_all x1, starting transfers between devices, local(): lax.all_to_all(flux.reshape(SPAN, 2 * CAP, 128), 'span', split_axis=0, co...  13.6 us
    all_to_all x1, starting transfers between devices, local(): lax.all_to_all(sent.reshape(SPAN * PER, 1, 128), 'span', split_axis=0, co...  12.8 us
    ppermute x6, starting transfers between devices, swap(): return (lax.ppermute(even, axis, pairs), lax.ppermute(odd, axis, shifted))  11.7 us
    ppermute x6, waiting for transfers between devices, swap(): return (lax.ppermute(even, axis, pairs), lax.ppermute(odd, axis, shifted))  7.92 us
    pallas_call x1, Pallas kernels, local(): pl.pallas_call(sweeps_kernel, out_shape=jax.ShapeDtypeStruct((DZ, CX, SB)...  4.32 us
    pallas_call x1, Pallas kernels, local(): pl.pallas_call(owner_kernel, out_shape=(pltpu.HBM((2 * SLOTS, 128), F32),...  2.62 us
    pallas_call x1, Pallas kernels, local(): pl.pallas_call(edge_rows_kernel, out_shape=(rows, rows), grid=(1,), in_sp...  2.57 us
  transfers between devices with their start and end apart: 8, of which 2 were waited for; matrix products, arithmetic and copies ran while one was open for 0% of the time, Pallas kernels for 14%

profile of v5, /device:TPU:1, one launch (start us, length us, event | category | flops | bytes accessed | tf_op | source)
XLA Modules:
  0.0 80.5 jit_solution(1393615239325120899)
XLA Ops:
  0.6 2.4 %pack.1 = f32[2112,128]{1,0:T(8,128)} custom-call(s32[1,256]{1,0:T(1,128)} %bitcast.18, s32[1,256]{1,0:T(1,128)} %tile_hbm.1, s32[1,256]{1,0:T(1,128)} %closed_hbm.1, f32[256,256]{1,0:T(8,128)} %bitcast.15, f32[256,256]{1,0:T(8,128)} %bitcast.22), custom_call_target="tpu_custom_call" | custom-call | flops 402653184 | bytes 4194304 | tf_op jit(solution)/shard_map/pack/pallas_call | solution.py:494
  3.0 12.8 %all-to-all-start = ((f32[2112,1,128]{2,1,0:T(1,128)}), f32[2112,1,128]{2,1,0:T(1,128)}, u32[]{:S(2)}, u32[]{:S(2)}) async-start(f32[2112,1,128]{2,1,0:T(1,128)} %bitcast.20), calls=%async_computation | async-start | bytes 2162688 | tf_op jit(solution)/shard_map/all_to_all | solution.py:513
  15.8 0.0 copy-start
  15.9 0.0 copy-start.2
  15.9 0.0 copy-start.3
  15.9 2.6 %edge_rows.1 = (f32[144,256]{1,0:T(8,128)}, f32[144,256]{1,0:T(8,128)}) custom-call(f32[48,32,256]{2,1,0:T(8,128)} %die_last.1, f32[48,32,256]{2,1,0:T(8,128)} %die_last.1, f32[48,32,256]{2,1,0:T(8,128)} %diff_top.1, f32[48,32,256]{2,1,0:T(8,128)} %diff_top.1), custom_call_target="tpu_custom_call" | custom-call | tf_op jit(solution)/shard_map/edge_rows/pallas_call | solution.py:481
  18.4 0.9 %collective-permute-start = (f32[144,256]{1,0:T(8,128)}, f32[144,256]{1,0:T(8,128)S(1)}, u32[]{:S(2)}, u32[]{:S(2)}) collective-permute-start(f32[144,256]{1,0:T(8,128)} %get-tuple-element.16), channel_id=1, source_target_pairs={{0,4},{4,0},{8,12},{12,8},{16,20},{20,16},{24,28},{28,24},{32,36},... | collective-permute-start | bytes 442376 | tf_op jit(solution)/shard_map/ppermute | solution.py:473
  19.4 0.7 collective-permute-start.1
  20.1 7.9 %collective-permute-done.even_in = f32[144,256]{1,0:T(8,128)S(1)} collective-permute-done((f32[144,256]{1,0:T(8,128)}, f32[144,256]{1,0:T(8,128)S(1)}, u32[]{:S(2)}, u32[]{:S(2)}) %collective-permute-start) | collective-permute-done | bytes 147488 | tf_op jit(solution)/shard_map/ppermute | solution.py:473
  28.0 0.0 collective-permute-done.1.odd_in
  28.0 0.0 copy-done
  28.0 0.0 copy-done.2
  28.0 0.0 copy-done.3
  28.0 2.4 %edge_columns.1 = (f32[48,256]{1,0:T(8,128)}, f32[48,256]{1,0:T(8,128)}, f32[384,256]{1,0:T(8,128)}, f32[384,256]{1,0:T(8,128)}, f32[32,256]{1,0:T(8,128)}) custom-call(f32[1536,256]{1,0:T(8,128)S(1)} %bitcast.13, f32[1536,256]{1,0:T(8,128)S(1)} %bitcast.11, f32[144,256]{1,0:T(8,128)S(1)} %collective-permute-done.even_in, ...), custom_call_target="tpu_custom_call" | custom-call | tf_op jit(solution)/shard_map/edge_columns/pallas_call | solution.py:518
  30.4 0.0 copy-start.7
  30.4 0.0 copy-start.8
  30.4 14.1 %all-to-all-done = f32[2112,1,128]{2,1,0:T(1,128)} async-done(((f32[2112,1,128]{2,1,0:T(1,128)}), f32[2112,1,128]{2,1,0:T(1,128)}, u32[]{:S(2)}, u32[]{:S(2)}) %all-to-all-start) | async-done | bytes 1081376 | tf_op jit(solution)/shard_map/all_to_all | solution.py:513
  44.5 2.6 %owner.1 = (f32[1024,128]{1,0:T(8,128)}, f32[32,256]{1,0:T(8,128)}, f32[8,256]{1,0:T(8,128)}, f32[8,256]{1,0:T(8,128)}) custom-call(f32[2112,128]{1,0:T(8,128)} %bitcast.5.got_hbm, f32[32,256]{1,0:T(8,128)} %get-tuple-element.18.face_hbm), custom_call_target="tpu_custom_call" | custom-call | tf_op jit(solution)/shard_map/owner/pallas_call | solution.py:529
  47.1 0.4 collective-permute-start.2
  47.6 0.6 collective-permute-start.3
  48.2 13.6 %all-to-all-start.1 = ((f32[64,16,128]{2,1,0:T(8,128)}), f32[64,16,128]{2,1,0:T(8,128)}, u32[]{:S(2)}, u32[]{:S(2)}) async-start(f32[64,16,128]{2,1,0:T(8,128)} %bitcast.21), calls=%async_computation.1 | async-start | bytes 1048576 | tf_op jit(solution)/shard_map/all_to_all | solution.py:553
  61.9 0.0 collective-permute-done.2.even_in
  61.9 0.0 collective-permute-done.3.odd_in
  61.9 0.0 copy-done.7
  61.9 0.0 copy-done.8
  61.9 0.0 copy-start.9
  61.9 0.7 copy-done.9
  62.7 0.0 copy-start.1
  62.7 0.0 copy-start.4
  62.7 0.0 copy-start.5
  62.7 0.1 heat_edges.1
  62.8 2.9 %collective-permute-start.4 = (f32[48,256]{1,0:T(8,128)S(1)}, f32[48,256]{1,0:T(8,128)S(1)}, u32[]{:S(2)}, u32[]{:S(2)}) collective-permute-start(f32[48,256]{1,0:T(8,128)S(1)} %get-tuple-element.24.even_own), channel_id=1, source_target_pairs={{0,1},{1,0},{2,3},{3,2},{4,5},{5,4},{6,7},{7,6},{8,9},{9,8},{10,11... | collective-permute-start | bytes 147464 | tf_op jit(solution)/shard_map/ppermute | solution.py:473
  65.6 6.2 %collective-permute-start.5 = (f32[48,256]{1,0:T(8,128)S(1)}, f32[48,256]{1,0:T(8,128)S(1)}, u32[]{:S(2)}, u32[]{:S(2)}) collective-permute-start(f32[48,256]{1,0:T(8,128)S(1)} %get-tuple-element.25.odd_own), channel_id=1, source_target_pairs={{1,2},{2,1},{5,6},{6,5},{9,10},{10,9},{13,14},{14,13},{17,18},{18,... | collective-permute-start | bytes 147464 | tf_op jit(solution)/shard_map/ppermute | solution.py:473
  71.8 0.0 copy-done.1
  71.8 0.0 copy-done.4
  71.8 0.0 copy-done.5
  71.8 4.3 %sweeps.1.base_ref = f32[48,32,256]{2,1,0:T(8,128)S(1)} custom-call(f32[1536,256]{1,0:T(8,128)S(1)} %bitcast.14, f32[1536,256]{1,0:T(8,128)S(1)} %bitcast.12, f32[384,256]{1,0:T(8,128)S(1)} %copy-done.5, f32[384,256]{1,0:T(8,128)S(1)} %copy-done.4, f32[40,256]{1,0:T(8,128)S(1)} %get-tuple-element.29.after_ref.heat_ref), custom_call_target="tpu_custom_call" | custom-call | tf_op jit(solution)/shard_map/sweeps/pallas_call | solution.py:567
  76.1 0.0 copy-start.6
  76.2 0.0 collective-permute-done.4.even_in
  76.2 0.0 collective-permute-done.5.odd_in
  76.2 1.8 %finish.1 = f32[48,32,256]{2,1,0:T(8,128)} custom-call(f32[48,32,256]{2,1,0:T(8,128)S(1)} %sweeps.1.base_ref, f32[48,32,256]{2,1,0:T(8,128)S(1)} %copy-done.1, f32[384,256]{1,0:T(8,128)S(1)} %copy-done.4, f32[40,256]{1,0:T(8,128)S(1)} %get-tuple-element.29.after_ref.heat_ref, f32[48,256]{1,0:T(8,128)S(1)} %get-tuple-element.24.even_own, ...), custom_call_target="tpu_custom_call" | custom-call | tf_op jit(solution)/shard_map/finish/pallas_call | solution.py:586
  78.0 0.0 all-to-all-done.1.flux_hbm
  78.0 0.0 copy-done.6
  78.0 2.5 %shell.1 = f32[256,256]{1,0:T(8,128)} custom-call(s32[1,256]{1,0:T(1,128)S(1)} %bitcast.19, f32[256,256]{1,0:T(8,128)S(1)} %bitcast.17, f32[48,256]{1,0:T(8,128)S(1)} %collective-permute-done.4.even_in, f32[48,256]{1,0:T(8,128)S(1)} %collective-permute-done.5.odd_in, f32[64,16,128]{2,1,0:T(8,128)} %all-to-all-done.1.flux_hbm), custom_call_target="tpu_custom_call" | custom-call | tf_op jit(solution)/shard_map/shell/pallas_call | solution.py:604
Async XLA Ops:
  3.0 41.5 %all-to-all-start = ((f32[2112,1,128]{2,1,0:T(1,128)}), f32[2112,1,128]{2,1,0:T(1,128)}, u32[]{:S(2)}, u32[]{:S(2)}) async-start(f32[2112,1,128]{2,1,0:T(1,128)} %bitcast.20), calls=%async_computation | async-start | bytes 2162688 | tf_op jit(solution)/shard_map/all_to_all | solution.py:513
  15.8 12.1 %copy-start = (f32[48,32,256]{2,1,0:T(8,128)S(1)}, f32[48,32,256]{2,1,0:T(8,128)}, u32[]{:S(2)}) copy-start(f32[48,32,256]{2,1,0:T(8,128)} %diff_top.1) | copy-start | bytes 4718596
  15.9 12.1 %copy-start.2 = (f32[48,32,256]{2,1,0:T(8,128)S(1)}, f32[48,32,256]{2,1,0:T(8,128)}, u32[]{:S(2)}) copy-start(f32[48,32,256]{2,1,0:T(8,128)} %die_last.1) | copy-start | bytes 4718596
  15.9 12.1 %copy-start.3 = (f32[1,256,256]{2,1,0:T(8,128)S(1)}, f32[1,256,256]{2,1,0:T(8,128)}, u32[]{:S(2)}) copy-start(f32[1,256,256]{2,1,0:T(8,128)} %param.7) | copy-start | bytes 786436
  18.4 9.5 %collective-permute-start = (f32[144,256]{1,0:T(8,128)}, f32[144,256]{1,0:T(8,128)S(1)}, u32[]{:S(2)}, u32[]{:S(2)}) collective-permute-start(f32[144,256]{1,0:T(8,128)} %get-tuple-element.16), channel_id=1, source_target_pairs={{0,4},{4,0},{8,12},{12,8},{16,20},{20,16},{24,28},{28,24},{32,36},... | collective-permute-start | bytes 442376 | tf_op jit(solution)/shard_map/ppermute | solution.py:473
  19.4 8.6 %collective-permute-start.1 = (f32[144,256]{1,0:T(8,128)}, f32[144,256]{1,0:T(8,128)S(1)}, u32[]{:S(2)}, u32[]{:S(2)}) collective-permute-start(f32[144,256]{1,0:T(8,128)} %get-tuple-element.17), channel_id=1, source_target_pairs={{4,8},{8,4},{12,16},{16,12},{20,24},{24,20},{28,32},{32,28},{36,40... | collective-permute-start | bytes 442376 | tf_op jit(solution)/shard_map/ppermute | solution.py:473
  30.4 31.5 %copy-start.7 = (f32[48,256]{1,0:T(8,128)S(1)}, f32[48,256]{1,0:T(8,128)}, u32[]{:S(2)}) copy-start(f32[48,256]{1,0:T(8,128)} %get-tuple-element.22.even_packed) | copy-start | bytes 147460
  30.4 31.5 %copy-start.8 = (f32[48,256]{1,0:T(8,128)S(1)}, f32[48,256]{1,0:T(8,128)}, u32[]{:S(2)}) copy-start(f32[48,256]{1,0:T(8,128)} %get-tuple-element.23.odd_packed) | copy-start | bytes 147460
  47.1 14.7 %collective-permute-start.2 = (f32[8,256]{1,0:T(8,128)}, f32[8,256]{1,0:T(8,128)S(1)}, u32[]{:S(2)}, u32[]{:S(2)}) collective-permute-start(f32[8,256]{1,0:T(8,128)} %get-tuple-element.20), channel_id=1, source_target_pairs={{0,4},{4,0},{8,12},{12,8},{16,20},{20,16},{24,28},{28,24},{32,36},... | collective-permute-start | bytes 24584 | tf_op jit(solution)/shard_map/ppermute | solution.py:473
  47.6 14.3 %collective-permute-start.3 = (f32[8,256]{1,0:T(8,128)}, f32[8,256]{1,0:T(8,128)S(1)}, u32[]{:S(2)}, u32[]{:S(2)}) collective-permute-start(f32[8,256]{1,0:T(8,128)} %get-tuple-element.21), channel_id=1, source_target_pairs={{4,8},{8,4},{12,16},{16,12},{20,24},{24,20},{28,32},{32,28},{36,40... | collective-permute-start | bytes 24584 | tf_op jit(solution)/shard_map/ppermute | solution.py:473
  48.2 29.8 %all-to-all-start.1 = ((f32[64,16,128]{2,1,0:T(8,128)}), f32[64,16,128]{2,1,0:T(8,128)}, u32[]{:S(2)}, u32[]{:S(2)}) async-start(f32[64,16,128]{2,1,0:T(8,128)} %bitcast.21), calls=%async_computation.1 | async-start | bytes 1048576 | tf_op jit(solution)/shard_map/all_to_all | solution.py:553
  61.9 0.8 copy-start.9
  62.7 9.1 %copy-start.1 = (f32[48,32,256]{2,1,0:T(8,128)S(1)}, f32[48,32,256]{2,1,0:T(8,128)}, u32[]{:S(2)}) copy-start(f32[48,32,256]{2,1,0:T(8,128)} %diff_top.1) | copy-start | bytes 4718596
  62.7 9.1 %copy-start.4 = (f32[384,256]{1,0:T(8,128)S(1)}, f32[384,256]{1,0:T(8,128)}, u32[]{:S(2)}) copy-start(f32[384,256]{1,0:T(8,128)} %get-tuple-element.28.diff_rim) | copy-start | bytes 1179652
  62.7 9.1 %copy-start.5 = (f32[384,256]{1,0:T(8,128)S(1)}, f32[384,256]{1,0:T(8,128)}, u32[]{:S(2)}) copy-start(f32[384,256]{1,0:T(8,128)} %get-tuple-element.27.die_rim) | copy-start | bytes 1179652
  62.8 13.4 %collective-permute-start.4 = (f32[48,256]{1,0:T(8,128)S(1)}, f32[48,256]{1,0:T(8,128)S(1)}, u32[]{:S(2)}, u32[]{:S(2)}) collective-permute-start(f32[48,256]{1,0:T(8,128)S(1)} %get-tuple-element.24.even_own), channel_id=1, source_target_pairs={{0,1},{1,0},{2,3},{3,2},{4,5},{5,4},{6,7},{7,6},{8,9},{9,8},{10,11... | collective-permute-start | bytes 147464 | tf_op jit(solution)/shard_map/ppermute | solution.py:473
  65.6 10.5 %collective-permute-start.5 = (f32[48,256]{1,0:T(8,128)S(1)}, f32[48,256]{1,0:T(8,128)S(1)}, u32[]{:S(2)}, u32[]{:S(2)}) collective-permute-start(f32[48,256]{1,0:T(8,128)S(1)} %get-tuple-element.25.odd_own), channel_id=1, source_target_pairs={{1,2},{2,1},{5,6},{6,5},{9,10},{10,9},{13,14},{14,13},{17,18},{18,... | collective-permute-start | bytes 147464 | tf_op jit(solution)/shard_map/ppermute | solution.py:473
  76.1 1.9 %copy-start.6 = (s32[1,256,1]{1,2,0:T(1,128)S(1)}, s32[1,256,1]{1,2,0:T(1,128)}, u32[]{:S(2)}) copy-start(s32[1,256,1]{1,2,0:T(1,128)} %param.11) | copy-start | bytes 3076

commit v6 on v5

--- a/solution.py
+++ b/solution.py
@@ -23,6 +23,7 @@
 EY = SB + 128
 
 CHUNKS = 4
+PIECES = 1
 UNROLL = 3
 GROUP = 4
 
@@ -424,12 +425,12 @@
 def shell_kernel(
     routes_ref, temp_ref, even_in, odd_in, flux_hbm, out_ref, flux_ref, sems
 ):
-    some = SPAN // CHUNKS
+    some = SPAN // PIECES
     loads = [
         pltpu.make_async_copy(
             flux_hbm.at[pl.ds(n * some, some)], flux_ref.at[pl.ds(n * some, some)], sems.at[n]
         )
-        for n in range(CHUNKS)
+        for n in range(PIECES)
     ]
     for load in loads:
         load.start()
@@ -449,9 +450,9 @@
     same = jnp.logical_and(target_col == target, lane < sub)
     rank_col = jnp.sum(jnp.where(same, 1.0, 0.0), axis=1, keepdims=True)
     position = (target_col * CAP + rank_col).astype(jnp.int32)
-    slots = SLOTS // CHUNKS
+    slots = SLOTS // PIECES
     total = jnp.zeros((NB, SB), F32)
-    for n in range(CHUNKS):
+    for n in range(PIECES):
         take = jnp.where(iota((NB, slots), 1) + n * slots == position, 1.0, 0.0).astype(BF16)
         loads[n].wait()
         rows = slice(n * some, (n + 1) * some)
@@ -609,7 +610,7 @@
         out_specs=whole(NB, SB),
         scratch_shapes=[
             pltpu.VMEM((SPAN, 2 * CAP, 128), F32),
-            pltpu.SemaphoreType.DMA((CHUNKS,)),
+            pltpu.SemaphoreType.DMA((PIECES,)),
         ],
         compiler_params=params(16),
         name="shell",

time: 81.5 us -> 81.2 us (level)
  no operation moved by 1% of the time
where the time goes in v6:
time: 81.2 us; the launch traced here: 80.2 us
  starting transfers between devices  38.1 us (47%)
  waiting for transfers between devices  22 us (27%)
  Pallas kernels  18.4 us (23%)
  between operations  0.85 us (1%)
    all_to_all x1, waiting for transfers between devices, local(): lax.all_to_all(sent.reshape(SPAN * PER, 1, 128), 'span', split_axis=0, co...  14.1 us
    all_to_all x1, starting transfers between devices, local(): lax.all_to_all(flux.reshape(SPAN, 2 * CAP, 128), 'span', split_axis=0, co...  13.6 us
    all_to_all x1, starting transfers between devices, local(): lax.all_to_all(sent.reshape(SPAN * PER, 1, 128), 'span', split_axis=0, co...  12.8 us
    ppermute x6, starting transfers between devices, swap(): return (lax.ppermute(even, axis, pairs), lax.ppermute(odd, axis, shifted))  11.7 us
    ppermute x6, waiting for transfers between devices, swap(): return (lax.ppermute(even, axis, pairs), lax.ppermute(odd, axis, shifted))  7.92 us
    pallas_call x1, Pallas kernels, local(): pl.pallas_call(sweeps_kernel, out_shape=jax.ShapeDtypeStruct((DZ, CX, SB)...  4.32 us
    pallas_call x1, Pallas kernels, local(): pl.pallas_call(owner_kernel, out_shape=(pltpu.HBM((2 * SLOTS, 128), F32),...  2.62 us
    pallas_call x1, Pallas kernels, local(): pl.pallas_call(edge_rows_kernel, out_shape=(rows, rows), grid=(1,), in_sp...  2.57 us
  transfers between devices with their start and end apart: 8, of which 2 were waited for; matrix products, arithmetic and copies ran while one was open for 0% of the time, Pallas kernels for 14%

profile of v6, /device:TPU:1, one launch (start us, length us, event | category | flops | bytes accessed | tf_op | source)
XLA Modules:
  0.0 80.2 jit_solution(2886362266844918691)
XLA Ops:
  0.6 2.4 %pack.1 = f32[2112,128]{1,0:T(8,128)} custom-call(s32[1,256]{1,0:T(1,128)} %bitcast.18, s32[1,256]{1,0:T(1,128)} %tile_hbm.1, s32[1,256]{1,0:T(1,128)} %closed_hbm.1, f32[256,256]{1,0:T(8,128)} %bitcast.15, f32[256,256]{1,0:T(8,128)} %bitcast.22), custom_call_target="tpu_custom_call" | custom-call | flops 402653184 | bytes 4194304 | tf_op jit(solution)/shard_map/pack/pallas_call | solution.py:495
  3.0 12.8 %all-to-all-start = ((f32[2112,1,128]{2,1,0:T(1,128)}), f32[2112,1,128]{2,1,0:T(1,128)}, u32[]{:S(2)}, u32[]{:S(2)}) async-start(f32[2112,1,128]{2,1,0:T(1,128)} %bitcast.20), calls=%async_computation | async-start | bytes 2162688 | tf_op jit(solution)/shard_map/all_to_all | solution.py:514
  15.8 0.0 copy-start
  15.9 0.0 copy-start.2
  15.9 0.0 copy-start.3
  15.9 2.6 %edge_rows.1 = (f32[144,256]{1,0:T(8,128)}, f32[144,256]{1,0:T(8,128)}) custom-call(f32[48,32,256]{2,1,0:T(8,128)} %die_last.1, f32[48,32,256]{2,1,0:T(8,128)} %die_last.1, f32[48,32,256]{2,1,0:T(8,128)} %diff_top.1, f32[48,32,256]{2,1,0:T(8,128)} %diff_top.1), custom_call_target="tpu_custom_call" | custom-call | tf_op jit(solution)/shard_map/edge_rows/pallas_call | solution.py:482
  18.4 0.9 %collective-permute-start = (f32[144,256]{1,0:T(8,128)}, f32[144,256]{1,0:T(8,128)S(1)}, u32[]{:S(2)}, u32[]{:S(2)}) collective-permute-start(f32[144,256]{1,0:T(8,128)} %get-tuple-element.16), channel_id=1, source_target_pairs={{0,4},{4,0},{8,12},{12,8},{16,20},{20,16},{24,28},{28,24},{32,36},... | collective-permute-start | bytes 442376 | tf_op jit(solution)/shard_map/ppermute | solution.py:474
  19.4 0.7 collective-permute-start.1
  20.1 7.9 %collective-permute-done.even_in = f32[144,256]{1,0:T(8,128)S(1)} collective-permute-done((f32[144,256]{1,0:T(8,128)}, f32[144,256]{1,0:T(8,128)S(1)}, u32[]{:S(2)}, u32[]{:S(2)}) %collective-permute-start) | collective-permute-done | bytes 147488 | tf_op jit(solution)/shard_map/ppermute | solution.py:474
  28.0 0.0 collective-permute-done.1.odd_in
  28.0 0.0 copy-done
  28.0 0.0 copy-done.2
  28.0 0.0 copy-done.3
  28.0 2.4 %edge_columns.1 = (f32[48,256]{1,0:T(8,128)}, f32[48,256]{1,0:T(8,128)}, f32[384,256]{1,0:T(8,128)}, f32[384,256]{1,0:T(8,128)}, f32[32,256]{1,0:T(8,128)}) custom-call(f32[1536,256]{1,0:T(8,128)S(1)} %bitcast.13, f32[1536,256]{1,0:T(8,128)S(1)} %bitcast.11, f32[144,256]{1,0:T(8,128)S(1)} %collective-permute-done.even_in, ...), custom_call_target="tpu_custom_call" | custom-call | tf_op jit(solution)/shard_map/edge_columns/pallas_call | solution.py:519
  30.4 0.0 copy-start.7
  30.4 0.0 copy-start.8
  30.4 14.1 %all-to-all-done = f32[2112,1,128]{2,1,0:T(1,128)} async-done(((f32[2112,1,128]{2,1,0:T(1,128)}), f32[2112,1,128]{2,1,0:T(1,128)}, u32[]{:S(2)}, u32[]{:S(2)}) %all-to-all-start) | async-done | bytes 1081376 | tf_op jit(solution)/shard_map/all_to_all | solution.py:514
  44.5 2.6 %owner.1 = (f32[1024,128]{1,0:T(8,128)}, f32[32,256]{1,0:T(8,128)}, f32[8,256]{1,0:T(8,128)}, f32[8,256]{1,0:T(8,128)}) custom-call(f32[2112,128]{1,0:T(8,128)} %bitcast.5.got_hbm, f32[32,256]{1,0:T(8,128)} %get-tuple-element.18.face_hbm), custom_call_target="tpu_custom_call" | custom-call | tf_op jit(solution)/shard_map/owner/pallas_call | solution.py:530
  47.1 0.4 collective-permute-start.2
  47.6 0.6 collective-permute-start.3
  48.2 13.6 %all-to-all-start.1 = ((f32[64,16,128]{2,1,0:T(8,128)}), f32[64,16,128]{2,1,0:T(8,128)}, u32[]{:S(2)}, u32[]{:S(2)}) async-start(f32[64,16,128]{2,1,0:T(8,128)} %bitcast.21), calls=%async_computation.1 | async-start | bytes 1048576 | tf_op jit(solution)/shard_map/all_to_all | solution.py:554
  61.9 0.0 collective-permute-done.2.even_in
  61.9 0.0 collective-permute-done.3.odd_in
  61.9 0.0 copy-done.7
  61.9 0.0 copy-done.8
  61.9 0.0 copy-start.9
  61.9 0.7 copy-done.9
  62.7 0.0 copy-start.1
  62.7 0.0 copy-start.4
  62.7 0.0 copy-start.5
  62.7 0.1 heat_edges.1
  62.8 2.9 %collective-permute-start.4 = (f32[48,256]{1,0:T(8,128)S(1)}, f32[48,256]{1,0:T(8,128)S(1)}, u32[]{:S(2)}, u32[]{:S(2)}) collective-permute-start(f32[48,256]{1,0:T(8,128)S(1)} %get-tuple-element.24.even_own), channel_id=1, source_target_pairs={{0,1},{1,0},{2,3},{3,2},{4,5},{5,4},{6,7},{7,6},{8,9},{9,8},{10,11... | collective-permute-start | bytes 147464 | tf_op jit(solution)/shard_map/ppermute | solution.py:474
  65.6 6.2 %collective-permute-start.5 = (f32[48,256]{1,0:T(8,128)S(1)}, f32[48,256]{1,0:T(8,128)S(1)}, u32[]{:S(2)}, u32[]{:S(2)}) collective-permute-start(f32[48,256]{1,0:T(8,128)S(1)} %get-tuple-element.25.odd_own), channel_id=1, source_target_pairs={{1,2},{2,1},{5,6},{6,5},{9,10},{10,9},{13,14},{14,13},{17,18},{18,... | collective-permute-start | bytes 147464 | tf_op jit(solution)/shard_map/ppermute | solution.py:474
  71.8 0.0 copy-done.1
  71.8 0.0 copy-done.4
  71.8 0.0 copy-done.5
  71.8 4.3 %sweeps.1.base_ref = f32[48,32,256]{2,1,0:T(8,128)S(1)} custom-call(f32[1536,256]{1,0:T(8,128)S(1)} %bitcast.14, f32[1536,256]{1,0:T(8,128)S(1)} %bitcast.12, f32[384,256]{1,0:T(8,128)S(1)} %copy-done.5, f32[384,256]{1,0:T(8,128)S(1)} %copy-done.4, f32[40,256]{1,0:T(8,128)S(1)} %get-tuple-element.29.after_ref.heat_ref), custom_call_target="tpu_custom_call" | custom-call | tf_op jit(solution)/shard_map/sweeps/pallas_call | solution.py:568
  76.1 0.0 copy-start.6
  76.2 0.0 collective-permute-done.4.even_in
  76.2 0.0 collective-permute-done.5.odd_in
  76.2 1.8 %finish.1 = f32[48,32,256]{2,1,0:T(8,128)} custom-call(f32[48,32,256]{2,1,0:T(8,128)S(1)} %sweeps.1.base_ref, f32[48,32,256]{2,1,0:T(8,128)S(1)} %copy-done.1, f32[384,256]{1,0:T(8,128)S(1)} %copy-done.4, f32[40,256]{1,0:T(8,128)S(1)} %get-tuple-element.29.after_ref.heat_ref, f32[48,256]{1,0:T(8,128)S(1)} %get-tuple-element.24.even_own, ...), custom_call_target="tpu_custom_call" | custom-call | tf_op jit(solution)/shard_map/finish/pallas_call | solution.py:587
  78.0 0.0 all-to-all-done.1.flux_hbm
  78.0 0.0 copy-done.6
  78.0 2.2 %shell.1 = f32[256,256]{1,0:T(8,128)} custom-call(s32[1,256]{1,0:T(1,128)S(1)} %bitcast.19, f32[256,256]{1,0:T(8,128)S(1)} %bitcast.17, f32[48,256]{1,0:T(8,128)S(1)} %collective-permute-done.4.even_in, f32[48,256]{1,0:T(8,128)S(1)} %collective-permute-done.5.odd_in, f32[64,16,128]{2,1,0:T(8,128)} %all-to-all-done.1.flux_hbm), custom_call_target="tpu_custom_call" | custom-call | tf_op jit(solution)/shard_map/shell/pallas_call | solution.py:605
Async XLA Ops:
  3.0 41.5 %all-to-all-start = ((f32[2112,1,128]{2,1,0:T(1,128)}), f32[2112,1,128]{2,1,0:T(1,128)}, u32[]{:S(2)}, u32[]{:S(2)}) async-start(f32[2112,1,128]{2,1,0:T(1,128)} %bitcast.20), calls=%async_computation | async-start | bytes 2162688 | tf_op jit(solution)/shard_map/all_to_all | solution.py:514
  15.8 12.1 %copy-start = (f32[48,32,256]{2,1,0:T(8,128)S(1)}, f32[48,32,256]{2,1,0:T(8,128)}, u32[]{:S(2)}) copy-start(f32[48,32,256]{2,1,0:T(8,128)} %diff_top.1) | copy-start | bytes 4718596
  15.9 12.1 %copy-start.2 = (f32[48,32,256]{2,1,0:T(8,128)S(1)}, f32[48,32,256]{2,1,0:T(8,128)}, u32[]{:S(2)}) copy-start(f32[48,32,256]{2,1,0:T(8,128)} %die_last.1) | copy-start | bytes 4718596
  15.9 12.1 %copy-start.3 = (f32[1,256,256]{2,1,0:T(8,128)S(1)}, f32[1,256,256]{2,1,0:T(8,128)}, u32[]{:S(2)}) copy-start(f32[1,256,256]{2,1,0:T(8,128)} %param.7) | copy-start | bytes 786436
  18.4 9.5 %collective-permute-start = (f32[144,256]{1,0:T(8,128)}, f32[144,256]{1,0:T(8,128)S(1)}, u32[]{:S(2)}, u32[]{:S(2)}) collective-permute-start(f32[144,256]{1,0:T(8,128)} %get-tuple-element.16), channel_id=1, source_target_pairs={{0,4},{4,0},{8,12},{12,8},{16,20},{20,16},{24,28},{28,24},{32,36},... | collective-permute-start | bytes 442376 | tf_op jit(solution)/shard_map/ppermute | solution.py:474
  19.4 8.6 %collective-permute-start.1 = (f32[144,256]{1,0:T(8,128)}, f32[144,256]{1,0:T(8,128)S(1)}, u32[]{:S(2)}, u32[]{:S(2)}) collective-permute-start(f32[144,256]{1,0:T(8,128)} %get-tuple-element.17), channel_id=1, source_target_pairs={{4,8},{8,4},{12,16},{16,12},{20,24},{24,20},{28,32},{32,28},{36,40... | collective-permute-start | bytes 442376 | tf_op jit(solution)/shard_map/ppermute | solution.py:474
  30.4 31.5 %copy-start.7 = (f32[48,256]{1,0:T(8,128)S(1)}, f32[48,256]{1,0:T(8,128)}, u32[]{:S(2)}) copy-start(f32[48,256]{1,0:T(8,128)} %get-tuple-element.22.even_packed) | copy-start | bytes 147460
  30.4 31.5 %copy-start.8 = (f32[48,256]{1,0:T(8,128)S(1)}, f32[48,256]{1,0:T(8,128)}, u32[]{:S(2)}) copy-start(f32[48,256]{1,0:T(8,128)} %get-tuple-element.23.odd_packed) | copy-start | bytes 147460
  47.1 14.7 %collective-permute-start.2 = (f32[8,256]{1,0:T(8,128)}, f32[8,256]{1,0:T(8,128)S(1)}, u32[]{:S(2)}, u32[]{:S(2)}) collective-permute-start(f32[8,256]{1,0:T(8,128)} %get-tuple-element.20), channel_id=1, source_target_pairs={{0,4},{4,0},{8,12},{12,8},{16,20},{20,16},{24,28},{28,24},{32,36},... | collective-permute-start | bytes 24584 | tf_op jit(solution)/shard_map/ppermute | solution.py:474
  47.6 14.3 %collective-permute-start.3 = (f32[8,256]{1,0:T(8,128)}, f32[8,256]{1,0:T(8,128)S(1)}, u32[]{:S(2)}, u32[]{:S(2)}) collective-permute-start(f32[8,256]{1,0:T(8,128)} %get-tuple-element.21), channel_id=1, source_target_pairs={{4,8},{8,4},{12,16},{16,12},{20,24},{24,20},{28,32},{32,28},{36,40... | collective-permute-start | bytes 24584 | tf_op jit(solution)/shard_map/ppermute | solution.py:474
  48.2 29.8 %all-to-all-start.1 = ((f32[64,16,128]{2,1,0:T(8,128)}), f32[64,16,128]{2,1,0:T(8,128)}, u32[]{:S(2)}, u32[]{:S(2)}) async-start(f32[64,16,128]{2,1,0:T(8,128)} %bitcast.21), calls=%async_computation.1 | async-start | bytes 1048576 | tf_op jit(solution)/shard_map/all_to_all | solution.py:554
  61.9 0.8 copy-start.9
  62.7 9.1 %copy-start.1 = (f32[48,32,256]{2,1,0:T(8,128)S(1)}, f32[48,32,256]{2,1,0:T(8,128)}, u32[]{:S(2)}) copy-start(f32[48,32,256]{2,1,0:T(8,128)} %diff_top.1) | copy-start | bytes 4718596
  62.7 9.1 %copy-start.4 = (f32[384,256]{1,0:T(8,128)S(1)}, f32[384,256]{1,0:T(8,128)}, u32[]{:S(2)}) copy-start(f32[384,256]{1,0:T(8,128)} %get-tuple-element.28.diff_rim) | copy-start | bytes 1179652
  62.7 9.1 %copy-start.5 = (f32[384,256]{1,0:T(8,128)S(1)}, f32[384,256]{1,0:T(8,128)}, u32[]{:S(2)}) copy-start(f32[384,256]{1,0:T(8,128)} %get-tuple-element.27.die_rim) | copy-start | bytes 1179652
  62.8 13.4 %collective-permute-start.4 = (f32[48,256]{1,0:T(8,128)S(1)}, f32[48,256]{1,0:T(8,128)S(1)}, u32[]{:S(2)}, u32[]{:S(2)}) collective-permute-start(f32[48,256]{1,0:T(8,128)S(1)} %get-tuple-element.24.even_own), channel_id=1, source_target_pairs={{0,1},{1,0},{2,3},{3,2},{4,5},{5,4},{6,7},{7,6},{8,9},{9,8},{10,11... | collective-permute-start | bytes 147464 | tf_op jit(solution)/shard_map/ppermute | solution.py:474
  65.6 10.5 %collective-permute-start.5 = (f32[48,256]{1,0:T(8,128)S(1)}, f32[48,256]{1,0:T(8,128)S(1)}, u32[]{:S(2)}, u32[]{:S(2)}) collective-permute-start(f32[48,256]{1,0:T(8,128)S(1)} %get-tuple-element.25.odd_own), channel_id=1, source_target_pairs={{1,2},{2,1},{5,6},{6,5},{9,10},{10,9},{13,14},{14,13},{17,18},{18,... | collective-permute-start | bytes 147464 | tf_op jit(solution)/shard_map/ppermute | solution.py:474
  76.1 1.9 %copy-start.6 = (s32[1,256,1]{1,2,0:T(1,128)S(1)}, s32[1,256,1]{1,2,0:T(1,128)}, u32[]{:S(2)}) copy-start(s32[1,256,1]{1,2,0:T(1,128)} %param.11) | copy-start | bytes 3076

commit v7 on v6

--- a/solution.py
+++ b/solution.py
@@ -345,14 +345,14 @@
     got_hbm, face_hbm, flux_hbm, heat_hbm, even_hbm, odd_hbm,
     got_ref, face_ref, flux_ref, heat_ref, even_ref, odd_ref, sems, out_sems,
 ):
-    rows = SPAN * PER // CHUNKS
+    rows = SPAN * PER // PIECES
     loads = [
         pltpu.make_async_copy(
             got_hbm.at[pl.ds(n * rows, rows)], got_ref.at[pl.ds(n * rows, rows)], sems.at[n]
         )
-        for n in range(CHUNKS)
+        for n in range(PIECES)
     ]
-    loads.append(pltpu.make_async_copy(face_hbm, face_ref, sems.at[CHUNKS]))
+    loads.append(pltpu.make_async_copy(face_hbm, face_ref, sems.at[PIECES]))
     for load in loads:
         load.start()
     lane = iota((SPAN, 128), 1).astype(F32)
@@ -545,7 +545,7 @@
             pltpu.VMEM((CX, SB), F32),
             pltpu.VMEM((8, SB), F32),
             pltpu.VMEM((8, SB), F32),
-            pltpu.SemaphoreType.DMA((CHUNKS + 1,)),
+            pltpu.SemaphoreType.DMA((PIECES + 1,)),
             pltpu.SemaphoreType.DMA((4,)),
         ],
         compiler_params=params(60),

time: 81.2 us -> 81.2 us (level)
  no operation moved by 1% of the time
where the time goes in v7:
time: 81.2 us; the launch traced here: 80.2 us
  starting transfers between devices  38.1 us (47%)
  waiting for transfers between devices  22 us (27%)
  Pallas kernels  18.4 us (23%)
  between operations  0.85 us (1%)
    all_to_all x1, waiting for transfers between devices, local(): lax.all_to_all(sent.reshape(SPAN * PER, 1, 128), 'span', split_axis=0, co...  14.1 us
    all_to_all x1, starting transfers between devices, local(): lax.all_to_all(flux.reshape(SPAN, 2 * CAP, 128), 'span', split_axis=0, co...  13.6 us
    all_to_all x1, starting transfers between devices, local(): lax.all_to_all(sent.reshape(SPAN * PER, 1, 128), 'span', split_axis=0, co...  12.8 us
    ppermute x6, starting transfers between devices, swap(): return (lax.ppermute(even, axis, pairs), lax.ppermute(odd, axis, shifted))  11.7 us
    ppermute x6, waiting for transfers between devices, swap(): return (lax.ppermute(even, axis, pairs), lax.ppermute(odd, axis, shifted))  7.92 us
    pallas_call x1, Pallas kernels, local(): pl.pallas_call(sweeps_kernel, out_shape=jax.ShapeDtypeStruct((DZ, CX, SB)...  4.32 us
    pallas_call x1, Pallas kernels, local(): pl.pallas_call(owner_kernel, out_shape=(pltpu.HBM((2 * SLOTS, 128), F32),...  2.64 us
    pallas_call x1, Pallas kernels, local(): pl.pallas_call(edge_rows_kernel, out_shape=(rows, rows), grid=(1,), in_sp...  2.57 us
  transfers between devices with their start and end apart: 8, of which 2 were waited for; matrix products, arithmetic and copies ran while one was open for 0% of the time, Pallas kernels for 14%

profile of v7, /device:TPU:1, one launch (start us, length us, event | category | flops | bytes accessed | tf_op | source)
XLA Modules:
  0.0 80.2 jit_solution(17142134380214732753)
XLA Ops:
  0.6 2.4 %pack.1 = f32[2112,128]{1,0:T(8,128)} custom-call(s32[1,256]{1,0:T(1,128)} %bitcast.18, s32[1,256]{1,0:T(1,128)} %tile_hbm.1, s32[1,256]{1,0:T(1,128)} %closed_hbm.1, f32[256,256]{1,0:T(8,128)} %bitcast.15, f32[256,256]{1,0:T(8,128)} %bitcast.22), custom_call_target="tpu_custom_call" | custom-call | flops 402653184 | bytes 4194304 | tf_op jit(solution)/shard_map/pack/pallas_call | solution.py:495
  3.0 12.8 %all-to-all-start = ((f32[2112,1,128]{2,1,0:T(1,128)}), f32[2112,1,128]{2,1,0:T(1,128)}, u32[]{:S(2)}, u32[]{:S(2)}) async-start(f32[2112,1,128]{2,1,0:T(1,128)} %bitcast.20), calls=%async_computation | async-start | bytes 2162688 | tf_op jit(solution)/shard_map/all_to_all | solution.py:514
  15.8 0.0 copy-start
  15.9 0.0 copy-start.2
  15.9 0.0 copy-start.3
  15.9 2.6 %edge_rows.1 = (f32[144,256]{1,0:T(8,128)}, f32[144,256]{1,0:T(8,128)}) custom-call(f32[48,32,256]{2,1,0:T(8,128)} %die_last.1, f32[48,32,256]{2,1,0:T(8,128)} %die_last.1, f32[48,32,256]{2,1,0:T(8,128)} %diff_top.1, f32[48,32,256]{2,1,0:T(8,128)} %diff_top.1), custom_call_target="tpu_custom_call" | custom-call | tf_op jit(solution)/shard_map/edge_rows/pallas_call | solution.py:482
  18.4 0.9 %collective-permute-start = (f32[144,256]{1,0:T(8,128)}, f32[144,256]{1,0:T(8,128)S(1)}, u32[]{:S(2)}, u32[]{:S(2)}) collective-permute-start(f32[144,256]{1,0:T(8,128)} %get-tuple-element.16), channel_id=1, source_target_pairs={{0,4},{4,0},{8,12},{12,8},{16,20},{20,16},{24,28},{28,24},{32,36},... | collective-permute-start | bytes 442376 | tf_op jit(solution)/shard_map/ppermute | solution.py:474
  19.4 0.7 collective-permute-start.1
  20.1 7.9 %collective-permute-done.even_in = f32[144,256]{1,0:T(8,128)S(1)} collective-permute-done((f32[144,256]{1,0:T(8,128)}, f32[144,256]{1,0:T(8,128)S(1)}, u32[]{:S(2)}, u32[]{:S(2)}) %collective-permute-start) | collective-permute-done | bytes 147488 | tf_op jit(solution)/shard_map/ppermute | solution.py:474
  28.0 0.0 collective-permute-done.1.odd_in
  28.0 0.0 copy-done
  28.0 0.0 copy-done.2
  28.0 0.0 copy-done.3
  28.0 2.4 %edge_columns.1 = (f32[48,256]{1,0:T(8,128)}, f32[48,256]{1,0:T(8,128)}, f32[384,256]{1,0:T(8,128)}, f32[384,256]{1,0:T(8,128)}, f32[32,256]{1,0:T(8,128)}) custom-call(f32[1536,256]{1,0:T(8,128)S(1)} %bitcast.13, f32[1536,256]{1,0:T(8,128)S(1)} %bitcast.11, f32[144,256]{1,0:T(8,128)S(1)} %collective-permute-done.even_in, ...), custom_call_target="tpu_custom_call" | custom-call | tf_op jit(solution)/shard_map/edge_columns/pallas_call | solution.py:519
  30.4 0.0 copy-start.7
  30.4 0.0 copy-start.8
  30.4 14.1 %all-to-all-done = f32[2112,1,128]{2,1,0:T(1,128)} async-done(((f32[2112,1,128]{2,1,0:T(1,128)}), f32[2112,1,128]{2,1,0:T(1,128)}, u32[]{:S(2)}, u32[]{:S(2)}) %all-to-all-start) | async-done | bytes 1081376 | tf_op jit(solution)/shard_map/all_to_all | solution.py:514
  44.5 2.6 %owner.1 = (f32[1024,128]{1,0:T(8,128)}, f32[32,256]{1,0:T(8,128)}, f32[8,256]{1,0:T(8,128)}, f32[8,256]{1,0:T(8,128)}) custom-call(f32[2112,128]{1,0:T(8,128)} %bitcast.5.got_hbm, f32[32,256]{1,0:T(8,128)} %get-tuple-element.18.face_hbm), custom_call_target="tpu_custom_call" | custom-call | tf_op jit(solution)/shard_map/owner/pallas_call | solution.py:530
  47.1 0.4 collective-permute-start.2
  47.6 0.6 collective-permute-start.3
  48.2 13.6 %all-to-all-start.1 = ((f32[64,16,128]{2,1,0:T(8,128)}), f32[64,16,128]{2,1,0:T(8,128)}, u32[]{:S(2)}, u32[]{:S(2)}) async-start(f32[64,16,128]{2,1,0:T(8,128)} %bitcast.21), calls=%async_computation.1 | async-start | bytes 1048576 | tf_op jit(solution)/shard_map/all_to_all | solution.py:554
  61.9 0.0 collective-permute-done.2.even_in
  61.9 0.0 collective-permute-done.3.odd_in
  61.9 0.0 copy-done.7
  61.9 0.0 copy-done.8
  61.9 0.0 copy-start.9
  61.9 0.7 copy-done.9
  62.7 0.0 copy-start.1
  62.7 0.0 copy-start.4
  62.7 0.0 copy-start.5
  62.7 0.1 heat_edges.1
  62.8 2.9 %collective-permute-start.4 = (f32[48,256]{1,0:T(8,128)S(1)}, f32[48,256]{1,0:T(8,128)S(1)}, u32[]{:S(2)}, u32[]{:S(2)}) collective-permute-start(f32[48,256]{1,0:T(8,128)S(1)} %get-tuple-element.24.even_own), channel_id=1, source_target_pairs={{0,1},{1,0},{2,3},{3,2},{4,5},{5,4},{6,7},{7,6},{8,9},{9,8},{10,11... | collective-permute-start | bytes 147464 | tf_op jit(solution)/shard_map/ppermute | solution.py:474
  65.6 6.2 %collective-permute-start.5 = (f32[48,256]{1,0:T(8,128)S(1)}, f32[48,256]{1,0:T(8,128)S(1)}, u32[]{:S(2)}, u32[]{:S(2)}) collective-permute-start(f32[48,256]{1,0:T(8,128)S(1)} %get-tuple-element.25.odd_own), channel_id=1, source_target_pairs={{1,2},{2,1},{5,6},{6,5},{9,10},{10,9},{13,14},{14,13},{17,18},{18,... | collective-permute-start | bytes 147464 | tf_op jit(solution)/shard_map/ppermute | solution.py:474
  71.8 0.0 copy-done.1
  71.8 0.0 copy-done.4
  71.8 0.0 copy-done.5
  71.8 4.3 %sweeps.1.base_ref = f32[48,32,256]{2,1,0:T(8,128)S(1)} custom-call(f32[1536,256]{1,0:T(8,128)S(1)} %bitcast.14, f32[1536,256]{1,0:T(8,128)S(1)} %bitcast.12, f32[384,256]{1,0:T(8,128)S(1)} %copy-done.5, f32[384,256]{1,0:T(8,128)S(1)} %copy-done.4, f32[40,256]{1,0:T(8,128)S(1)} %get-tuple-element.29.after_ref.heat_ref), custom_call_target="tpu_custom_call" | custom-call | tf_op jit(solution)/shard_map/sweeps/pallas_call | solution.py:568
  76.2 0.0 copy-start.6
  76.2 0.0 collective-permute-done.4.even_in
  76.2 0.0 collective-permute-done.5.odd_in
  76.2 1.8 %finish.1 = f32[48,32,256]{2,1,0:T(8,128)} custom-call(f32[48,32,256]{2,1,0:T(8,128)S(1)} %sweeps.1.base_ref, f32[48,32,256]{2,1,0:T(8,128)S(1)} %copy-done.1, f32[384,256]{1,0:T(8,128)S(1)} %copy-done.4, f32[40,256]{1,0:T(8,128)S(1)} %get-tuple-element.29.after_ref.heat_ref, f32[48,256]{1,0:T(8,128)S(1)} %get-tuple-element.24.even_own, ...), custom_call_target="tpu_custom_call" | custom-call | tf_op jit(solution)/shard_map/finish/pallas_call | solution.py:587
  78.0 0.0 all-to-all-done.1.flux_hbm
  78.0 0.0 copy-done.6
  78.0 2.2 %shell.1 = f32[256,256]{1,0:T(8,128)} custom-call(s32[1,256]{1,0:T(1,128)S(1)} %bitcast.19, f32[256,256]{1,0:T(8,128)S(1)} %bitcast.17, f32[48,256]{1,0:T(8,128)S(1)} %collective-permute-done.4.even_in, f32[48,256]{1,0:T(8,128)S(1)} %collective-permute-done.5.odd_in, f32[64,16,128]{2,1,0:T(8,128)} %all-to-all-done.1.flux_hbm), custom_call_target="tpu_custom_call" | custom-call | tf_op jit(solution)/shard_map/shell/pallas_call | solution.py:605
Async XLA Ops:
  3.0 41.5 %all-to-all-start = ((f32[2112,1,128]{2,1,0:T(1,128)}), f32[2112,1,128]{2,1,0:T(1,128)}, u32[]{:S(2)}, u32[]{:S(2)}) async-start(f32[2112,1,128]{2,1,0:T(1,128)} %bitcast.20), calls=%async_computation | async-start | bytes 2162688 | tf_op jit(solution)/shard_map/all_to_all | solution.py:514
  15.8 12.1 %copy-start = (f32[48,32,256]{2,1,0:T(8,128)S(1)}, f32[48,32,256]{2,1,0:T(8,128)}, u32[]{:S(2)}) copy-start(f32[48,32,256]{2,1,0:T(8,128)} %diff_top.1) | copy-start | bytes 4718596
  15.9 12.1 %copy-start.2 = (f32[48,32,256]{2,1,0:T(8,128)S(1)}, f32[48,32,256]{2,1,0:T(8,128)}, u32[]{:S(2)}) copy-start(f32[48,32,256]{2,1,0:T(8,128)} %die_last.1) | copy-start | bytes 4718596
  15.9 12.1 %copy-start.3 = (f32[1,256,256]{2,1,0:T(8,128)S(1)}, f32[1,256,256]{2,1,0:T(8,128)}, u32[]{:S(2)}) copy-start(f32[1,256,256]{2,1,0:T(8,128)} %param.7) | copy-start | bytes 786436
  18.4 9.5 %collective-permute-start = (f32[144,256]{1,0:T(8,128)}, f32[144,256]{1,0:T(8,128)S(1)}, u32[]{:S(2)}, u32[]{:S(2)}) collective-permute-start(f32[144,256]{1,0:T(8,128)} %get-tuple-element.16), channel_id=1, source_target_pairs={{0,4},{4,0},{8,12},{12,8},{16,20},{20,16},{24,28},{28,24},{32,36},... | collective-permute-start | bytes 442376 | tf_op jit(solution)/shard_map/ppermute | solution.py:474
  19.4 8.6 %collective-permute-start.1 = (f32[144,256]{1,0:T(8,128)}, f32[144,256]{1,0:T(8,128)S(1)}, u32[]{:S(2)}, u32[]{:S(2)}) collective-permute-start(f32[144,256]{1,0:T(8,128)} %get-tuple-element.17), channel_id=1, source_target_pairs={{4,8},{8,4},{12,16},{16,12},{20,24},{24,20},{28,32},{32,28},{36,40... | collective-permute-start | bytes 442376 | tf_op jit(solution)/shard_map/ppermute | solution.py:474
  30.4 31.5 %copy-start.7 = (f32[48,256]{1,0:T(8,128)S(1)}, f32[48,256]{1,0:T(8,128)}, u32[]{:S(2)}) copy-start(f32[48,256]{1,0:T(8,128)} %get-tuple-element.22.even_packed) | copy-start | bytes 147460
  30.4 31.5 %copy-start.8 = (f32[48,256]{1,0:T(8,128)S(1)}, f32[48,256]{1,0:T(8,128)}, u32[]{:S(2)}) copy-start(f32[48,256]{1,0:T(8,128)} %get-tuple-element.23.odd_packed) | copy-start | bytes 147460
  47.1 14.7 %collective-permute-start.2 = (f32[8,256]{1,0:T(8,128)}, f32[8,256]{1,0:T(8,128)S(1)}, u32[]{:S(2)}, u32[]{:S(2)}) collective-permute-start(f32[8,256]{1,0:T(8,128)} %get-tuple-element.20), channel_id=1, source_target_pairs={{0,4},{4,0},{8,12},{12,8},{16,20},{20,16},{24,28},{28,24},{32,36},... | collective-permute-start | bytes 24584 | tf_op jit(solution)/shard_map/ppermute | solution.py:474
  47.6 14.3 %collective-permute-start.3 = (f32[8,256]{1,0:T(8,128)}, f32[8,256]{1,0:T(8,128)S(1)}, u32[]{:S(2)}, u32[]{:S(2)}) collective-permute-start(f32[8,256]{1,0:T(8,128)} %get-tuple-element.21), channel_id=1, source_target_pairs={{4,8},{8,4},{12,16},{16,12},{20,24},{24,20},{28,32},{32,28},{36,40... | collective-permute-start | bytes 24584 | tf_op jit(solution)/shard_map/ppermute | solution.py:474
  48.2 29.8 %all-to-all-start.1 = ((f32[64,16,128]{2,1,0:T(8,128)}), f32[64,16,128]{2,1,0:T(8,128)}, u32[]{:S(2)}, u32[]{:S(2)}) async-start(f32[64,16,128]{2,1,0:T(8,128)} %bitcast.21), calls=%async_computation.1 | async-start | bytes 1048576 | tf_op jit(solution)/shard_map/all_to_all | solution.py:554
  61.9 0.8 copy-start.9
  62.7 9.1 %copy-start.1 = (f32[48,32,256]{2,1,0:T(8,128)S(1)}, f32[48,32,256]{2,1,0:T(8,128)}, u32[]{:S(2)}) copy-start(f32[48,32,256]{2,1,0:T(8,128)} %diff_top.1) | copy-start | bytes 4718596
  62.7 9.1 %copy-start.4 = (f32[384,256]{1,0:T(8,128)S(1)}, f32[384,256]{1,0:T(8,128)}, u32[]{:S(2)}) copy-start(f32[384,256]{1,0:T(8,128)} %get-tuple-element.28.diff_rim) | copy-start | bytes 1179652
  62.7 9.1 %copy-start.5 = (f32[384,256]{1,0:T(8,128)S(1)}, f32[384,256]{1,0:T(8,128)}, u32[]{:S(2)}) copy-start(f32[384,256]{1,0:T(8,128)} %get-tuple-element.27.die_rim) | copy-start | bytes 1179652
  62.8 13.4 %collective-permute-start.4 = (f32[48,256]{1,0:T(8,128)S(1)}, f32[48,256]{1,0:T(8,128)S(1)}, u32[]{:S(2)}, u32[]{:S(2)}) collective-permute-start(f32[48,256]{1,0:T(8,128)S(1)} %get-tuple-element.24.even_own), channel_id=1, source_target_pairs={{0,1},{1,0},{2,3},{3,2},{4,5},{5,4},{6,7},{7,6},{8,9},{9,8},{10,11... | collective-permute-start | bytes 147464 | tf_op jit(solution)/shard_map/ppermute | solution.py:474
  65.6 10.5 %collective-permute-start.5 = (f32[48,256]{1,0:T(8,128)S(1)}, f32[48,256]{1,0:T(8,128)S(1)}, u32[]{:S(2)}, u32[]{:S(2)}) collective-permute-start(f32[48,256]{1,0:T(8,128)S(1)} %get-tuple-element.25.odd_own), channel_id=1, source_target_pairs={{1,2},{2,1},{5,6},{6,5},{9,10},{10,9},{13,14},{14,13},{17,18},{18,... | collective-permute-start | bytes 147464 | tf_op jit(solution)/shard_map/ppermute | solution.py:474
  76.2 1.9 %copy-start.6 = (s32[1,256,1]{1,2,0:T(1,128)S(1)}, s32[1,256,1]{1,2,0:T(1,128)}, u32[]{:S(2)}) copy-start(s32[1,256,1]{1,2,0:T(1,128)} %param.11) | copy-start | bytes 3076
